TPU v7x, 32 devices: a whole 2x2x4 slice. The times are simulated.
32 devices in a mesh: fsdp: 2 (over x), ctx: 4 (over z), tp: 4 (over y, core).
Axes of the slice: x: 2, y: 2, z: 4, core: 2. Of those that a mesh axis runs over, the one named last changes fastest.
Arguments:
- block_input: bfloat16 [4096, 6, 768], P(('ctx', 'tp'), 'fsdp'), may hold values from -6 to 6
- ln1_gain: bfloat16 [768], replicated, may hold values from 0.5 to 1.5
- ln1_bias: bfloat16 [768], replicated, may hold values from -1.5 to 1.5
- w_qkv: bfloat16 [3, 768, 768], P(None, 'fsdp', 'tp'), may hold values from -0.21875 to 0.21875
- qkv_bias: bfloat16 [2, 768], replicated, may hold values from -1.5 to 1.5
- rel_h: bfloat16 [27, 64], replicated, may hold values from -0.75 to 0.75
- rel_w: bfloat16 [27, 64], replicated, may hold values from -0.75 to 0.75
- w_proj: bfloat16 [768, 768], P('tp', 'fsdp'), may hold values from -1.25 to 1.25
- proj_bias: bfloat16 [768], replicated, may hold values from -1.5 to 1.5
- ln2_gain: bfloat16 [768], replicated, may hold values from 0.5 to 1.5
- ln2_bias: bfloat16 [768], replicated, may hold values from -1.5 to 1.5
- w_up: bfloat16 [768, 3072], P('fsdp', 'tp'), may hold values from -0.21875 to 0.21875
- up_bias: bfloat16 [3072], replicated, may hold values from -1.5 to 1.5
- w_down: bfloat16 [3072, 768], P('tp', 'fsdp'), may hold values from -0.109375 to 0.109375
- down_bias: bfloat16 [768], replicated, may hold values from -1.5 to 1.5
- cotangent: bfloat16 [4096, 6, 768], P(('ctx', 'tp'), 'fsdp'), may hold values from -6 to 6
Outputs:
- block_out: bfloat16 [4096, 6, 768], P(('ctx', 'tp'), 'fsdp')
- grad_input: bfloat16 [4096, 6, 768], P(('ctx', 'tp'), 'fsdp')
- grad_ln1_gain: float32 [768], replicated
- grad_ln1_bias: float32 [768], replicated
- grad_w_qkv: float32 [3, 768, 768], P(None, 'fsdp', 'tp')
- grad_qkv_bias: float32 [2, 768], replicated
- grad_rel_h: float32 [27, 64], replicated
- grad_rel_w: float32 [27, 64], replicated
- grad_w_proj: float32 [768, 768], P('tp', 'fsdp')
- grad_proj_bias: float32 [768], replicated
- grad_ln2_gain: float32 [768], replicated
- grad_ln2_bias: float32 [768], replicated
- grad_w_up: float32 [768, 3072], P('fsdp', 'tp')
- grad_up_bias: float32 [3072], replicated
- grad_w_down: float32 [3072, 768], P('tp', 'fsdp')
- grad_down_bias: float32 [768], replicated
All inputs are finite; a program needn't handle non-finite values.
Results may differ from a plain program's by a relative error of at most 0.019.
Values may be sent and summed in bfloat16 or wider, within the bound.
A program may use at most 448 MiB of HBM per device.

v0:
```python
from functools import partial

import jax
import jax.numpy as jnp
from jax import lax
from jax.sharding import PartitionSpec as P

HEAD_DIM = 64
WIN = 14
SIDE = 64
WMAX = 9
PADDED = 70
NWIN = 25


EPSILON = 1e-06
HIGH = lax.Precision.HIGHEST


def layer_norm(rows, gain, shift):
    row_mean = jnp.mean(rows, axis=-1, keepdims=True)
    centered = rows - row_mean
    row_var = jnp.mean(centered * centered, axis=-1, keepdims=True)
    return centered * lax.rsqrt(row_var + EPSILON) * gain + shift


def outside_mask():
    position = jnp.arange(PADDED)
    return (position[:, None] >= SIDE) | (position[None, :] >= SIDE)


def to_windows(cells, fill):
    trail_dims = cells.shape[1:]
    cell_grid = cells.reshape((SIDE, SIDE) + trail_dims)
    pad_extra = PADDED - SIDE
    cell_grid = jnp.pad(cell_grid, ((0, pad_extra), (0, pad_extra)) + ((0, 0),) * len(trail_dims))
    pad_here = outside_mask().reshape((PADDED, PADDED) + (1,) * len(trail_dims))
    cell_grid = jnp.where(pad_here, fill, cell_grid)
    per_side = PADDED // WIN
    cell_grid = cell_grid.reshape((per_side, WIN, per_side, WIN) + trail_dims)
    cell_grid = jnp.swapaxes(cell_grid, 1, 2)
    return cell_grid.reshape((per_side * per_side, WIN * WIN) + trail_dims)


def from_windows(windows):
    trail_dims = windows.shape[2:]
    per_side = PADDED // WIN
    cell_grid = windows.reshape((per_side, per_side, WIN, WIN) + trail_dims)
    cell_grid = jnp.swapaxes(cell_grid, 1, 2)
    return cell_grid.reshape((PADDED, PADDED) + trail_dims)


def crop_cells(cell_grid):
    return cell_grid[:SIDE, :SIDE].reshape((SIDE * SIDE,) + cell_grid.shape[2:])


def window_scores(queries, keys_win, table_h, table_w):
    direct = jnp.einsum(
        "sabihe,scdihe->sihabcd", queries, keys_win, preferred_element_type=jnp.float32
    ) * HEAD_DIM ** (-0.5)
    along_h = jnp.einsum("sabihe,ace->sihabc", queries, table_h, preferred_element_type=jnp.float32)
    along_w = jnp.einsum("sabihe,bde->sihabd", queries, table_w, preferred_element_type=jnp.float32)
    total_scores = direct + along_h[..., None] + along_w[:, :, :, :, :, None, :]
    return total_scores.reshape(direct.shape[:3] + (WIN * WIN, WIN * WIN))


def local(
    block_input,
    ln1_gain,
    ln1_bias,
    w_qkv,
    qkv_bias,
    rel_h,
    rel_w,
    w_proj,
    proj_bias,
    ln2_gain,
    ln2_bias,
    w_up,
    up_bias,
    w_down,
    down_bias,
    cotangent,
):
    local_rows, images_here, width = block_input.shape
    head_cols = w_qkv.shape[2]
    heads_here = head_cols // HEAD_DIM
    units_here = w_up.shape[1]
    tp_place = lax.axis_index("tp")
    ctx_place = lax.axis_index("ctx")
    ctx_count = lax.axis_size("ctx")
    score_scale = HEAD_DIM ** (-0.5)

    def rows_forward(row_block):
        return lax.all_gather(row_block, "tp", axis=0, tiled=True)

    def rows_backward(row_block):
        return lax.all_gather(row_block, "tp", axis=0, tiled=True)

    def sums_forward(term_fn):
        return lax.psum_scatter(
            term_fn(jnp.int32(0), local_rows * lax.axis_size("tp")).astype(jnp.bfloat16),
            "tp",
            scatter_dimension=0,
            tiled=True,
        ).astype(jnp.float32)

    def sums_backward(term_fn):
        return lax.psum_scatter(
            term_fn(jnp.int32(0), local_rows * lax.axis_size("tp")).astype(jnp.bfloat16),
            "tp",
            scatter_dimension=0,
            tiled=True,
        ).astype(jnp.float32)

    wqkv_all, wproj_all, wup_all, wdown_all = (
        lax.all_gather(w_qkv, "fsdp", axis=1, tiled=True),
        lax.all_gather(w_proj, "fsdp", axis=1, tiled=True),
        lax.all_gather(w_up, "fsdp", axis=0, tiled=True),
        lax.all_gather(w_down, "fsdp", axis=1, tiled=True),
    )
    gain_one = ln1_gain.astype(jnp.float32)
    shift_one = ln1_bias.astype(jnp.float32)
    gain_two = ln2_gain.astype(jnp.float32)
    shift_two = ln2_bias.astype(jnp.float32)
    bias_here = lax.dynamic_slice_in_dim(qkv_bias, tp_place * head_cols, head_cols, 1).astype(
        jnp.float32
    )
    bias_three = jnp.stack([bias_here[0], jnp.zeros_like(bias_here[0]), bias_here[1]])
    up_here = lax.dynamic_slice_in_dim(up_bias, tp_place * units_here, units_here, 0).astype(
        jnp.float32
    )
    x_float = block_input.astype(jnp.float32)
    normed_one = layer_norm(x_float, gain_one, shift_one).astype(jnp.bfloat16)
    rows_one = rows_forward(normed_one)
    qkv_rows = (
        jnp.einsum("rid,tdc->ritc", rows_one, wqkv_all, preferred_element_type=jnp.float32)
        + bias_three
    ).astype(jnp.bfloat16)
    qkv_image = lax.all_gather(qkv_rows, "ctx", axis=0, tiled=True)
    qkv_windows = to_windows(qkv_image, bias_three.astype(jnp.bfloat16))
    window_place = jnp.arange(NWIN)
    window_table = jnp.where(window_place < WMAX, 0, 1 + (window_place - WMAX) % (ctx_count - 1))
    is_owned = window_table == ctx_place
    slot_rank = jnp.cumsum(is_owned.astype(jnp.int32)) - 1
    slot_pick = is_owned[None, :] & (slot_rank[None, :] == jnp.arange(WMAX)[:, None])
    slot_window = jnp.sum(slot_pick.astype(jnp.int32) * jnp.arange(NWIN)[None, :], axis=1)
    slot_live = jnp.sum(slot_pick.astype(jnp.int32), axis=1).astype(jnp.bfloat16)
    pick_low = slot_pick.astype(jnp.bfloat16)
    slot_qkv = jnp.take(qkv_windows, slot_window, axis=0)
    shape_grid = (WMAX, WIN, WIN, images_here, heads_here, HEAD_DIM)
    shape_flat = (WMAX, WIN * WIN, images_here, heads_here, HEAD_DIM)
    queries = slot_qkv[:, :, :, 0].reshape(shape_grid)
    keys_win = slot_qkv[:, :, :, 1].reshape(shape_grid)
    values_win = slot_qkv[:, :, :, 2].reshape(shape_flat)
    offsets = jnp.arange(WIN)[:, None] - jnp.arange(WIN)[None, :] + WIN - 1
    one_hot = (offsets[:, :, None] == jnp.arange(2 * WIN - 1)[None, None, :]).astype(jnp.bfloat16)
    table_h = jnp.einsum("ack,ke->ace", one_hot, rel_h, preferred_element_type=jnp.float32).astype(
        jnp.bfloat16
    )
    table_w = jnp.einsum("ack,ke->ace", one_hot, rel_w, preferred_element_type=jnp.float32).astype(
        jnp.bfloat16
    )
    scores = window_scores(queries, keys_win, table_h, table_w)
    row_top = jnp.max(scores, axis=-1, keepdims=True)
    log_total = row_top + jnp.log(jnp.sum(jnp.exp(scores - row_top), axis=-1, keepdims=True))
    probs_low = jnp.exp(scores - log_total).astype(jnp.bfloat16)
    attended = jnp.einsum(
        "sihqk,skihe->sqihe", probs_low, values_win, preferred_element_type=jnp.float32
    ).astype(jnp.bfloat16)
    attended = attended.reshape(WMAX, WIN * WIN, images_here, head_cols)
    placed = jnp.einsum(
        "sw,sqic->wqic", pick_low, attended, preferred_element_type=jnp.float32
    ).astype(jnp.bfloat16)
    attn_image = crop_cells(from_windows(placed))
    attn_rows = (
        lax.psum_scatter(attn_image, "ctx", scatter_dimension=0, tiled=True)
        .astype(jnp.float32)
        .astype(jnp.bfloat16)
    )

    def proj_term(first_row, row_count):
        return jnp.einsum("ric,cd->rid", attn_rows, wproj_all, preferred_element_type=jnp.float32)

    middle = x_float + sums_forward(proj_term) + proj_bias.astype(jnp.float32)
    normed_two = layer_norm(middle, gain_two, shift_two).astype(jnp.bfloat16)
    rows_two = rows_forward(normed_two)
    gate_in = (
        jnp.einsum("rid,df->rif", rows_two, wup_all, preferred_element_type=jnp.float32) + up_here
    )
    hidden = jax.nn.gelu(gate_in, approximate=False).astype(jnp.bfloat16)

    def down_term(first_row, row_count):
        return jnp.einsum("rif,fd->rid", hidden, wdown_all, preferred_element_type=jnp.float32)

    block_out = (middle + sums_forward(down_term) + down_bias.astype(jnp.float32)).astype(
        jnp.bfloat16
    )
    cot_float = cotangent.astype(jnp.float32)
    grad_down_bias = jnp.sum(cot_float, axis=(0, 1))
    cot_rows = rows_backward(cotangent)
    grad_w_down = jnp.einsum("rif,rid->fd", hidden, cot_rows, preferred_element_type=jnp.float32)
    grad_hidden = jnp.einsum("rid,fd->rif", cot_rows, wdown_all, preferred_element_type=jnp.float32)
    gelu_value, gelu_back = jax.vjp(partial(jax.nn.gelu, approximate=False), gate_in)
    grad_gate = gelu_back(grad_hidden)[0].astype(jnp.bfloat16)
    grad_w_up = jnp.einsum("rid,rif->df", rows_two, grad_gate, preferred_element_type=jnp.float32)
    grad_up_here = jnp.sum(grad_gate, axis=(0, 1), dtype=jnp.float32)

    def up_back_term(first_row, row_count):
        return jnp.einsum("rif,df->rid", grad_gate, wup_all, preferred_element_type=jnp.float32)

    grad_normed_two = sums_backward(up_back_term)
    norm_value, norm_two_back = jax.vjp(layer_norm, middle, gain_two, shift_two)
    grad_mid_norm, grad_gain_two, grad_shift_two = norm_two_back(grad_normed_two)
    grad_middle = grad_mid_norm + cot_float
    grad_branch = grad_middle.astype(jnp.bfloat16)
    grad_proj_bias = jnp.sum(grad_branch, axis=(0, 1), dtype=jnp.float32)
    branch_rows = rows_backward(grad_branch)
    grad_w_proj = jnp.einsum(
        "ric,rid->cd", attn_rows, branch_rows, preferred_element_type=jnp.float32
    )
    grad_att_rows = jnp.einsum(
        "rid,cd->ric", branch_rows, wproj_all, preferred_element_type=jnp.float32
    ).astype(jnp.bfloat16)
    grad_att_image = lax.all_gather(grad_att_rows, "ctx", axis=0, tiled=True)
    grad_att = jnp.take(
        to_windows(grad_att_image, jnp.zeros((), jnp.bfloat16)), slot_window, axis=0
    )
    grad_att = (grad_att * slot_live[:, None, None, None]).reshape(shape_flat)
    scores_again = window_scores(queries, keys_win, table_h, table_w)
    probs = jnp.exp(scores_again - log_total)
    probs_again = probs.astype(jnp.bfloat16)
    grad_values = jnp.einsum(
        "sihqk,sqihe->skihe", probs_again, grad_att, preferred_element_type=jnp.float32
    )
    grad_probs = jnp.einsum(
        "sqihe,skihe->sihqk", grad_att, values_win, preferred_element_type=jnp.float32
    )
    grad_scores = probs * (grad_probs - jnp.sum(probs * grad_probs, axis=-1, keepdims=True))
    grad_scores = grad_scores.astype(jnp.bfloat16).reshape(
        (WMAX, images_here, heads_here, WIN, WIN, WIN, WIN)
    )
    grad_query = score_scale * jnp.einsum(
        "sihabcd,scdihe->sabihe", grad_scores, keys_win, preferred_element_type=jnp.float32
    )
    grad_key = score_scale * jnp.einsum(
        "sihabcd,sabihe->scdihe", grad_scores, queries, preferred_element_type=jnp.float32
    )
    along_rows = jnp.sum(grad_scores, axis=6, dtype=jnp.float32)
    along_cols = jnp.sum(grad_scores, axis=5, dtype=jnp.float32)
    grad_query = grad_query + jnp.einsum(
        "sihabc,ace->sabihe", along_rows, table_h.astype(jnp.float32), precision=HIGH
    )
    grad_query = grad_query + jnp.einsum(
        "sihabd,bde->sabihe", along_cols, table_w.astype(jnp.float32), precision=HIGH
    )
    query_float = queries.astype(jnp.float32)
    hot_float = one_hot.astype(jnp.float32)
    grad_table_h = jnp.einsum("sihabc,sabihe->ace", along_rows, query_float, precision=HIGH)
    grad_table_w = jnp.einsum("sihabd,sabihe->bde", along_cols, query_float, precision=HIGH)
    grad_rel_h = jnp.einsum("ack,ace->ke", hot_float, grad_table_h, precision=HIGH)
    grad_rel_w = jnp.einsum("ack,ace->ke", hot_float, grad_table_w, precision=HIGH)
    slot_shape = (WMAX, WIN * WIN, images_here, head_cols)
    stacked = jnp.stack(
        [
            grad_query.reshape(slot_shape),
            grad_key.reshape(slot_shape),
            grad_values.reshape(slot_shape),
        ],
        axis=3,
    ).astype(jnp.bfloat16)
    placed_grad = jnp.einsum(
        "sw,skitc->wkitc", pick_low, stacked, preferred_element_type=jnp.float32
    )
    grad_grid = from_windows(placed_grad)
    pad_values = jnp.sum(
        jnp.where(outside_mask()[:, :, None, None], grad_grid[:, :, :, 2], 0.0), axis=(0, 1, 2)
    )
    grad_qkv_rows = lax.psum_scatter(
        crop_cells(grad_grid).astype(jnp.bfloat16), "ctx", scatter_dimension=0, tiled=True
    )
    grad_w_qkv = jnp.einsum(
        "rid,ritc->tdc", rows_one, grad_qkv_rows, preferred_element_type=jnp.float32
    )
    column_sums = jnp.sum(grad_qkv_rows, axis=(0, 1), dtype=jnp.float32)
    bias_grad_here = jnp.stack([column_sums[0], column_sums[2] + pad_values])
    grad_qkv_bias = lax.dynamic_update_slice_in_dim(
        jnp.zeros((2, width), jnp.float32), bias_grad_here, tp_place * head_cols, 1
    )
    grad_up_bias = lax.dynamic_update_slice_in_dim(
        jnp.zeros((up_bias.shape[0],), jnp.float32), grad_up_here, tp_place * units_here, 0
    )

    def qkv_back_term(first_row, row_count):
        return jnp.einsum(
            "ritc,tdc->rid", grad_qkv_rows, wqkv_all, preferred_element_type=jnp.float32
        )

    grad_normed_one = sums_backward(qkv_back_term)
    first_value, norm_one_back = jax.vjp(layer_norm, x_float, gain_one, shift_one)
    grad_x_norm, grad_gain_one, grad_shift_one = norm_one_back(grad_normed_one)
    grad_input = (grad_x_norm + grad_middle).astype(jnp.bfloat16)
    few_sums = lax.psum(
        (
            grad_gain_one,
            grad_shift_one,
            grad_qkv_bias,
            grad_rel_h,
            grad_rel_w,
            grad_proj_bias,
            grad_gain_two,
            grad_shift_two,
            grad_up_bias,
            grad_down_bias,
        ),
        ("fsdp", "ctx", "tp"),
    )
    summed_here = (
        lax.psum(grad_w_qkv.astype(jnp.bfloat16), "ctx").astype(jnp.float32),
        lax.psum(grad_w_proj.astype(jnp.bfloat16), "ctx").astype(jnp.float32),
        lax.psum(grad_w_up.astype(jnp.bfloat16), "ctx").astype(jnp.float32),
        lax.psum(grad_w_down.astype(jnp.bfloat16), "ctx").astype(jnp.float32),
    )
    weight_sums = (
        lax.psum_scatter(
            summed_here[0].astype(jnp.bfloat16), "fsdp", scatter_dimension=1, tiled=True
        ).astype(jnp.float32),
        lax.psum_scatter(
            summed_here[1].astype(jnp.bfloat16), "fsdp", scatter_dimension=1, tiled=True
        ).astype(jnp.float32),
        lax.psum_scatter(
            summed_here[2].astype(jnp.bfloat16), "fsdp", scatter_dimension=0, tiled=True
        ).astype(jnp.float32),
        lax.psum_scatter(
            summed_here[3].astype(jnp.bfloat16), "fsdp", scatter_dimension=1, tiled=True
        ).astype(jnp.float32),
    )
    return (
        block_out,
        grad_input,
        few_sums[0],
        few_sums[1],
        weight_sums[0],
        few_sums[2],
        few_sums[3],
        few_sums[4],
        weight_sums[1],
        few_sums[5],
        few_sums[6],
        few_sums[7],
        weight_sums[2],
        few_sums[8],
        weight_sums[3],
        few_sums[9],
    )


def solution(mesh):
    return jax.shard_map(
        local,
        mesh=mesh,
        in_specs=(
            P(("ctx", "tp"), "fsdp", None),
            P(),
            P(),
            P(None, "fsdp", "tp"),
            P(),
            P(),
            P(),
            P("tp", "fsdp"),
            P(),
            P(),
            P(),
            P("fsdp", "tp"),
            P(),
            P("tp", "fsdp"),
            P(),
            P(("ctx", "tp"), "fsdp", None),
        ),
        out_specs=(
            P(("ctx", "tp"), "fsdp", None),
            P(("ctx", "tp"), "fsdp", None),
            P(),
            P(),
            P(None, "fsdp", "tp"),
            P(),
            P(),
            P(),
            P("tp", "fsdp"),
            P(),
            P(),
            P(),
            P("fsdp", "tp"),
            P(),
            P("tp", "fsdp"),
            P(),
        ),
        check_vma=False,
    )
```

profile of v0, /device:TPU:14, one launch (start us, length us, event | category | flops | bytes accessed | tf_op | source)
XLA Modules:
  0.0 2565.8 jit_solution(2144947894630229785)
XLA Ops:
  17.1 12.6 all_gather.31
  29.7 24.3 all-gather.9.cloned.1.call-done
  62.9 240.2 %all-gather.11.cloned.1.call-done = bf16[4096,3,3,192]{0,3,2,1:T(8,128)(2,1)} async-done(((bf16[1024,3,3,192]{0,3,2,1:T(8,128)(2,1)}), bf16[4096,3,3,192]{0,3,2,1:T(8,128)(2,1)}) %all-gather.11.cloned.1.call-update) | async-done | bytes 14155792 | tf_op jit(solution)/shard_map/all_gather | solution.py:140
  303.0 21.3 copy.93
  324.4 15.7 pad_select_fusion
  340.1 35.3 %reshape.410 = bf16[5,14,5,14,3,3,192]{6,3,2,1,0,5,4:T(8,128)(2,1)} reshape(bf16[70,70,3,3,192]{4,1,0,3,2:T(8,128)(2,1)} %pad_select_fusion) | data formatting | bytes 33868800 | tf_op jit(solution)/shard_map/reshape | solution.py:40
  375.4 21.2 copy.95
  396.5 36.2 %reshape.356 = bf16[25,196,3,3,192]{4,1,3,2,0:T(8,128)(2,1)} reshape(bf16[5,5,14,14,3,3,192]{6,3,2,5,4,1,0:T(8,128)(2,1)} %copy.95) | data formatting | bytes 33868800 | tf_op jit(solution)/shard_map/reshape | solution.py:42
  432.7 31.8 %copy.96 = bf16[25,196,3,3,192]{1,4,3,2,0:T(8,128)(2,1)} copy(bf16[25,196,3,3,192]{4,1,3,2,0:T(8,128)(2,1)} %reshape.356) | data formatting | bytes 33868800 | tf_op jit(solution)/shard_map/reshape | solution.py:42
  464.5 12.4 gather_fusion
  493.9 16.9 fusion.54
  510.8 13.0 copy.104
  523.8 16.9 fusion.51
  550.2 55.6 %fusion.159 = (f32[9,3,3,14,14]{4,3,2,1,0:T(8,128)S(1)}, f32[9,3,3,14,14,14,14]{4,6,5,3,2,1,0:T(8,128)}) fusion(f32[9,3,3,14,14,14]{4,5,3,2,1,0:T(8,128)} %copy.104, bf16[9,14,14,3,3,64,1]{5,4,2,1,3,0,6:T(4,128)(2,1)} %bitcast.221, bf16[9,14,14,3,3,64,1]{5,4,2,1,3,0,6:T(4,128)(2,1)} %bitcast.216, f32[9,3,3,14,14,14]{4,5,2,1,0,3:T(8,128)} %fusion.51), kind=kOutput, calls=%fused_computation.225 | convolution fusion | flops 410727936 | bytes 18352656 | tf_op jit(solution)/shard_map/sabihe,scdihe->sihabcd/dot_general | solution.py:58
  605.8 101.6 %copy.176 = f32[9,3,3,14,14,14,14]{4,3,6,5,2,1,0:T(8,128)} copy(f32[9,3,3,14,14,14,14]{4,6,5,3,2,1,0:T(8,128)} %get-tuple-element.59) | data formatting | bytes 24893568 | tf_op jit(solution)/shard_map/reshape | solution.py:64
  707.4 39.7 %exponential_reduce_fusion = f32[9,3,3,14,14]{4,3,2,1,0:T(8,128)S(1)} fusion(f32[9,3,3,14,14,14,14]{4,6,5,3,2,1,0:T(8,128)} %get-tuple-element.59, f32[9,3,3,14,14]{4,3,2,1,0:T(8,128)S(1)} %get-tuple-element.58), kind=kLoop, calls=%fused_computation.5 | loop fusion | flops 6207516 | bytes 12573792 | tf_op jit(solution)/shard_map/reduce_sum | solution.py:166
  747.6 74.5 %reshape.411 = f32[9,3,3,196,196]{3,4,2,1,0:T(8,128)} reshape(f32[9,3,3,14,14,14,14]{4,3,6,5,2,1,0:T(8,128)} %copy.176) | data formatting | bytes 24893568 | tf_op jit(solution)/shard_map/reshape | solution.py:64
  822.2 8.7 fusion.81
  836.6 15.6 copy.109
  852.1 12.7 reshape.359
  872.2 13.0 reshape.360
  899.0 104.8 %reduce-scatter.17.cloned.1.call-done = bf16[1024,3,192]{2,0,1:T(8,128)(2,1)} async-done(((bf16[4096,3,192]{2,0,1:T(8,128)(2,1)}), bf16[1024,3,192]{2,0,1:T(8,128)(2,1)}) %reduce-scatter.17.cloned.1.call-update) | async-done | bytes 1179664 | tf_op jit(solution)/shard_map/reduce_scatter | solution.py:177
  1009.4 46.9 %reduce-scatter.19.cloned.1.call-done = bf16[256,3,768]{2,0,1:T(8,128)(2,1)} async-done(((bf16[1024,3,768]{2,0,1:T(8,128)(2,1)}), bf16[256,3,768]{2,0,1:T(8,128)(2,1)}) %reduce-scatter.19.cloned.1.call-update) | async-done | bytes 1179664 | tf_op jit(solution)/shard_map/reduce_scatter | solution.py:101
  1064.0 35.3 %all-gather.13.cloned.1.call-done = bf16[1024,3,768]{2,0,1:T(8,128)(2,1)} async-done(((bf16[256,3,768]{2,0,1:T(8,128)(2,1)}), bf16[1024,3,768]{2,0,1:T(8,128)(2,1)}) %all-gather.13.cloned.1.call-update) | async-done | bytes 4718608 | tf_op jit(solution)/shard_map/all_gather | solution.py:95
  1099.2 9.4 fusion.76
  1112.3 22.9 multiply_convert_fusion.1
  1135.1 27.2 %all-gather.19.cloned.1.call-done = bf16[1024,3,768]{2,0,1:T(8,128)(2,1)} async-done(((bf16[256,3,768]{2,0,1:T(8,128)(2,1)}), bf16[1024,3,768]{2,0,1:T(8,128)(2,1)}) %all-gather.19.cloned.1.call-update) | async-done | bytes 4718608 | tf_op jit(solution)/shard_map/all_gather | solution.py:98
  1162.4 12.2 convert_reduce_fusion.2
  1182.3 47.8 %reduce-scatter.23.cloned.1.call-done = bf16[256,3,768]{2,0,1:T(8,128)(2,1)} async-done(((bf16[1024,3,768]{2,0,1:T(8,128)(2,1)}), bf16[256,3,768]{2,0,1:T(8,128)(2,1)}) %reduce-scatter.23.cloned.1.call-update) | async-done | bytes 1179664 | tf_op jit(solution)/shard_map/reduce_scatter | solution.py:109
  1240.2 37.4 %all-gather.21.cloned.1.call-done = bf16[1024,3,768]{2,0,1:T(8,128)(2,1)} async-done(((bf16[256,3,768]{2,0,1:T(8,128)(2,1)}), bf16[1024,3,768]{2,0,1:T(8,128)(2,1)}) %all-gather.21.cloned.1.call-update) | async-done | bytes 4718608 | tf_op jit(solution)/shard_map/all_gather | solution.py:98
  1282.8 87.9 %all-gather.23.cloned.1.call-done = bf16[4096,3,192]{0,2,1:T(8,128)(2,1)} async-done(((bf16[1024,3,192]{0,2,1:T(8,128)(2,1)}), bf16[4096,3,192]{0,2,1:T(8,128)(2,1)}) %all-gather.23.cloned.1.call-update) | async-done | bytes 4718608 | tf_op jit(solution)/shard_map/all_gather | solution.py:225
  1370.7 7.9 copy.113
  1385.8 12.7 reshape.412
  1398.5 7.9 copy.115
  1406.4 13.0 reshape.364
  1419.4 11.6 copy.116
  1435.0 21.9 multiply_convert_fusion
  1456.9 77.4 %reshape.365 = bf16[9,3,3,14,14,14,14]{4,3,6,5,2,1,0:T(8,128)(2,1)} reshape(bf16[9,3,3,196,196]{3,4,2,1,0:T(8,128)(2,1)} %multiply_convert_fusion) | data formatting | bytes 12446784 | tf_op jit(solution)/shard_map/reshape | solution.py:240
  1534.3 54.1 %convert_reduce_fusion.1 = (f32[9,3,3,14,14,14]{4,3,5,2,1,0:T(8,128)}, f32[9,3,3,14,14,14]{4,3,5,2,1,0:T(8,128)}) fusion(bf16[9,3,3,14,14,14,14]{4,3,6,5,2,1,0:T(8,128)(2,1)} %reshape.365), kind=kLoop, calls=%fused_computation.4 | loop fusion | flops 8890560 | bytes 8001504 | tf_op jit(solution)/shard_map/reduce_sum | solution.py:249
  1588.3 36.6 %fusion.3 = f32[9,3,3,64,14,14,1]{3,5,6,4,2,1,0:T(8,128)} fusion(bf16[9,3,3,14,14,14,14]{4,3,6,5,2,1,0:T(8,128)(2,1)} %reshape.365, bf16[9,14,14,3,3,64,1]{5,4,2,1,3,0,6:T(4,128)(2,1)} %bitcast.222), kind=kOutput, calls=%fused_computation.9 | convolution fusion | flops 398297088 | bytes 12319776 | tf_op jit(solution)/shard_map/sihabcd,scdihe->sabihe/dot_general | solution.py:243
  1624.9 40.2 %fusion.35 = bf16[9,14,14,3,3,64]{5,2,1,4,3,0:T(8,128)(2,1)} fusion(bf16[9,3,3,14,14,14,14]{4,3,6,5,2,1,0:T(8,128)(2,1)} %reshape.365, bf16[9,14,14,3,3,64,1]{5,4,2,1,3,0,6:T(4,128)(2,1)} %bitcast.217), kind=kOutput, calls=%fused_computation.71 | convolution fusion | flops 400329216 | bytes 10287648 | tf_op jit(solution)/shard_map/sihabcd,sabihe->scdihe/dot_general | solution.py:246
  1665.1 10.2 fusion.84
  1675.2 12.7 copy.120
  1695.3 16.9 fusion.26
  1731.7 8.9 copy.125
  1757.4 23.3 fusion.8
  1780.7 64.2 %copy.130 = f32[25,196,3,3,192]{4,1,3,2,0:T(8,128)} copy(f32[25,196,3,3,192]{1,0,4,3,2:T(8,128)} %fusion.8) | data formatting | bytes 67737600 | tf_op jit(solution)/shard_map/sw,skitc->wkitc/dot_general | solution.py:272
  1844.9 49.4 %reshape.366 = f32[5,5,14,14,3,3,192]{6,3,2,5,4,1,0:T(8,128)} reshape(f32[25,196,3,3,192]{4,1,3,2,0:T(8,128)} %copy.130) | data formatting | bytes 67737600 | tf_op jit(solution)/shard_map/reshape | solution.py:48
  1894.3 35.0 %copy.131 = f32[5,14,5,14,3,3,192]{6,3,2,5,4,1,0:T(8,128)} copy(f32[5,14,5,14,3,3,192]{6,3,1,5,4,2,0:T(8,128)} %bitcast.215) | data formatting | bytes 67737600 | tf_op jit(solution)/shard_map/transpose | solution.py:49
  1929.3 50.2 %reshape.367 = f32[70,70,3,3,192]{4,1,3,2,0:T(8,128)} reshape(f32[5,14,5,14,3,3,192]{6,3,2,5,4,1,0:T(8,128)} %copy.131) | data formatting | bytes 67737600 | tf_op jit(solution)/shard_map/reshape | solution.py:50
  1979.6 13.6 slice.57
  2013.8 299.8 %reduce-scatter.25.cloned.1.call-done = bf16[1024,3,3,192]{3,0,2,1:T(8,128)(2,1)} async-done(((bf16[4096,3,3,192]{3,0,2,1:T(8,128)(2,1)}), bf16[1024,3,3,192]{3,0,2,1:T(8,128)(2,1)}) %reduce-scatter.25.cloned.1.call-update) | async-done | bytes 3538960 | tf_op jit(solution)/shard_map/reduce_scatter | solution.py:279
  2323.8 9.1 bitcast_convert_fusion.2
  2341.7 13.9 reduce-scatter.33.cloned.1.call-done
  2357.2 20.9 reduce-scatter.31.cloned.1.call-done
  2381.3 21.2 reduce-scatter.29.cloned.1.call-done
  2402.6 7.9 bitcast_convert_fusion
  2411.8 8.1 convolution_convert_fusion.2
  2421.4 14.5 copy.164
  2436.0 14.5 fusion.104
  2451.4 16.0 fusion.107
  2468.3 8.4 fusion.7
  2497.6 11.0 reduce-scatter.21.cloned.1.call-done
  2514.5 44.1 %all-reduce.2 = (f32[768]{0:T(1024)}, f32[768]{0:T(1024)}, f32[2,768]{1,0:T(2,128)}, f32[27,64]{1,0:T(8,128)}, f32[27,64]{1,0:T(8,128)}, /*index=5*/f32[768]{0:T...) all-reduce(f32[768]{0:T(1024)} %get-tuple-element.22, ...), channel_id=1, replica_groups=mesh['fsdp'=2,'ctx'=4,'tp'=4] {'fsdp','ctx','tp'}, use_global_device_ids=true, to_apply=%region_23.24 | all-reduce | flops 12672 | bytes 101376 | tf_op jit(solution)/shard_map/psum | solution.py:303
  (277 shorter events, 241.7 us)
Async XLA Ops:
  8.0 54.2 %copy-start = (bf16[27,64]{1,0:T(8,128)(2,1)S(1)}, bf16[27,64]{1,0:T(8,128)(2,1)}, u32[]{:S(2)}) copy-start(bf16[27,64]{1,0:T(8,128)(2,1)} %param.22) | copy-start | bytes 10372
  8.0 9.0 copy-start.17
  8.0 46.0 %all-gather.9.cloned.1.call-start = ((), (), s32[]{:S(2)}) async-start(), calls=%async_computation.10 | async-start | bytes 5898240 | tf_op jit(solution)/shard_map/all_gather | solution.py:95
  16.2 286.8 %all-gather.11.cloned.1.call-start = ((), (), s32[]{:S(2)}) async-start(), calls=%async_computation.11 | async-start | bytes 17694720 | tf_op jit(solution)/shard_map/all_gather | solution.py:140
  29.6 31.1 %copy-start.15 = (bf16[3,768,192]{1,2,0:T(8,128)(2,1)}, bf16[3,768,192]{1,2,0:T(8,128)(2,1)S(1)}, u32[]{:S(2)}) copy-start(bf16[3,768,192]{1,2,0:T(8,128)(2,1)S(1)} %all_gather.31) | copy-start | bytes 2654212
  29.7 32.9 %copy-start.64 = (bf16[27,64]{1,0:T(8,128)(2,1)S(1)}, bf16[27,64]{1,0:T(8,128)(2,1)}, u32[]{:S(2)}) copy-start(bf16[27,64]{1,0:T(8,128)(2,1)} %param.21) | copy-start | bytes 10372
  60.8 943.0 %reduce-scatter.17.cloned.1.call-start = ((), (), s32[]{:S(2)}) async-start(), calls=%async_computation.12 | async-start | bytes 7864320 | tf_op jit(solution)/shard_map/reduce_scatter | solution.py:177
  62.2 402.4 %copy-start.50 = (s32[1024]{0:T(1024)}, s32[1024]{0:T(1024)S(1)}, u32[]{:S(2)}) copy-start(s32[1024]{0:T(1024)S(1)} %pad_clamp_fusion) | copy-start | bytes 12292
  62.2 262.2 %copy-start.37 = (s32[14,14]{1,0:T(8,128)}, s32[14,14]{1,0:T(8,128)S(1)}, u32[]{:S(2)}) copy-start(s32[14,14]{1,0:T(8,128)S(1)} %subtract_add_fusion) | copy-start | bytes 2356
  62.4 431.5 %copy-start.20 = (bf16[14,14,64,1,1,1]{2,1,5,4,3,0:T(8,128)(2,1)}, bf16[14,14,64,1,1,1]{2,1,5,4,3,0:T(8,128)(2,1)S(1)}, u32[]{:S(2)}) copy-start(bf16[14,14,64,1,1,1]{2,1,5,4,3,0:T(8,128)(2,1)S(1)} %fusion.112) | copy-start | bytes 75268
  62.5 414.5 %copy-start.55 = (pred[9]{0:T(512)(128)(4,1)}, pred[9]{0:T(512)(128)(4,1)S(1)}, u32[]{:S(2)}) copy-start(pred[9]{0:T(512)(128)(4,1)S(1)} %compare_and_fusion) | copy-start | bytes 31
  62.6 261.7 %copy-start.28 = (pred[70,70]{1,0:T(8,128)(4,1)}, pred[70,70]{1,0:T(8,128)(4,1)S(1)}, u32[]{:S(2)}) copy-start(pred[70,70]{1,0:T(8,128)(4,1)S(1)} %broadcast_or_fusion) | copy-start | bytes 14704
  62.8 461.0 %copy-start.22 = (bf16[14,14,64]{2,1,0:T(8,128)(2,1)}, bf16[14,14,64]{2,1,0:T(8,128)(2,1)S(1)}, u32[]{:S(2)}) copy-start(bf16[14,14,64]{2,1,0:T(8,128)(2,1)S(1)} %convolution_convert_fusion.6) | copy-start | bytes 75268
  747.6 74.5 %copy-start.13 = (f32[9,3,3,196]{3,2,1,0:T(4,128)}, f32[9,3,3,196]{3,2,1,0:T(4,128)S(1)}, u32[]{:S(2)}) copy-start(f32[9,3,3,196]{3,2,1,0:T(4,128)S(1)} %add.290) | copy-start | bytes 190516
  747.6 74.5 %copy-start.10 = (bf16[9,196,3,1,192]{1,4,3,2,0:T(8,128)(2,1)S(1)}, bf16[9,196,3,1,192]{1,4,3,2,0:T(8,128)(2,1)}, u32[]{:S(2)}) copy-start(bf16[9,196,3,1,192]{1,4,3,2,0:T(8,128)(2,1)} %get-tuple-element.50) | copy-start | bytes 6096388
  822.1 8.7 copy-start.48
  822.1 8.7 copy-start.52
  891.8 164.5 %reduce-scatter.19.cloned.1.call-start = ((), (), s32[]{:S(2)}) async-start(), calls=%async_computation.13 | async-start | bytes 5898240 | tf_op jit(solution)/shard_map/reduce_scatter | solution.py:101
  899.0 104.8 %copy-start.12 = (bf16[192,768]{1,0:T(8,128)(2,1)}, bf16[192,768]{1,0:T(8,128)(2,1)S(1)}, u32[]{:S(2)}) copy-start(bf16[192,768]{1,0:T(8,128)(2,1)S(1)} %all_gather.33) | copy-start | bytes 884740
  1008.7 47.6 %copy-start.2 = (bf16[256,3,768]{2,0,1:T(8,128)(2,1)S(1)}, bf16[256,3,768]{2,0,1:T(8,128)(2,1)}, u32[]{:S(2)}) copy-start(bf16[256,3,768]{2,0,1:T(8,128)(2,1)} %param.16) | copy-start | bytes 3538948
  1008.7 55.3 %all-gather.15.cloned.1.call-start = ((), (), s32[]{:S(2)}) async-start(), calls=%async_computation.15 | async-start | bytes 1769472 | tf_op jit(solution)/shard_map/all_gather | solution.py:119
  1009.3 89.9 %all-gather.13.cloned.1.call-start = ((), (), s32[]{:S(2)}) async-start(), calls=%async_computation.14 | async-start | bytes 5898240 | tf_op jit(solution)/shard_map/all_gather | solution.py:95
  1009.4 228.0 %copy-start.18 = (f32[768]{0:T(1024)}, f32[768]{0:T(1024)S(1)}, u32[]{:S(2)}) copy-start(f32[768]{0:T(1024)S(1)} %convert_element_type.210) | copy-start | bytes 9220
  1009.4 228.0 %copy-start.33 = (f32[768]{0:T(1024)}, f32[768]{0:T(1024)S(1)}, u32[]{:S(2)}) copy-start(f32[768]{0:T(1024)S(1)} %convert_element_type.211) | copy-start | bytes 9220
  1058.1 179.2 %copy-start.24 = (f32[256,3]{0,1:T(4,128)}, f32[256,3]{0,1:T(4,128)S(1)}, u32[]{:S(2)}) copy-start(f32[256,3]{0,1:T(4,128)S(1)} %broadcast_multiply_fusion) | copy-start | bytes 9220
  1060.1 48.6 %copy-start.45 = (f32[256,3]{0,1:T(4,128)}, f32[256,3]{0,1:T(4,128)S(1)}, u32[]{:S(2)}) copy-start(f32[256,3]{0,1:T(4,128)S(1)} %multiply_reduce_fusion.1) | copy-start | bytes 9220
  1060.1 177.3 %copy-start.36 = (f32[256,3]{0,1:T(4,128)}, f32[256,3]{0,1:T(4,128)S(1)}, u32[]{:S(2)}) copy-start(f32[256,3]{0,1:T(4,128)S(1)} %fusion.143) | copy-start | bytes 9220
  1061.8 73.3 %all-gather.17.cloned.1.call-start = ((), (), s32[]{:S(2)}) async-start(), calls=%async_computation.16 | async-start | bytes 1769472 | tf_op jit(solution)/shard_map/all_gather | solution.py:120
  1062.4 100.0 %all-gather.19.cloned.1.call-start = ((), (), s32[]{:S(2)}) async-start(), calls=%async_computation.18 | async-start | bytes 5898240 | tf_op jit(solution)/shard_map/all_gather | solution.py:98
  1063.1 167.0 %reduce-scatter.23.cloned.1.call-start = ((), (), s32[]{:S(2)}) async-start(), calls=%async_computation.19 | async-start | bytes 5898240 | tf_op jit(solution)/shard_map/reduce_scatter | solution.py:109
  1162.4 14.4 copy-start.63
  1182.3 55.1 %copy-start.9 = (bf16[256,3,768]{2,0,1:T(8,128)(2,1)S(1)}, bf16[256,3,768]{2,0,1:T(8,128)(2,1)}, u32[]{:S(2)}) copy-start(bf16[256,3,768]{2,0,1:T(8,128)(2,1)} %param.31) | copy-start | bytes 3538948
  1182.3 95.3 %all-gather.21.cloned.1.call-start = ((), (), s32[]{:S(2)}) async-start(), calls=%async_computation.20 | async-start | bytes 5898240 | tf_op jit(solution)/shard_map/all_gather | solution.py:98
  1230.1 7.3 copy-start.6
  1233.8 6.3 copy-start.40
  1240.2 42.6 %copy-start.61 = (s32[9]{0:T(128)S(1)}, s32[9]{0:T(128)}, u32[]{:S(2)}) copy-start(s32[9]{0:T(128)} %get-tuple-element.28) | copy-start | bytes 112
  1240.2 130.5 %all-gather.23.cloned.1.call-start = ((), (), s32[]{:S(2)}) async-start(), calls=%async_computation.21 | async-start | bytes 5898240 | tf_op jit(solution)/shard_map/all_gather | solution.py:225
  1282.7 1030.9 %reduce-scatter.25.cloned.1.call-start = ((), (), s32[]{:S(2)}) async-start(), calls=%async_computation.22 | async-start | bytes 23592960 | tf_op jit(solution)/shard_map/reduce_scatter | solution.py:279
  1282.8 95.8 %copy-start.29 = (pred[70,70]{1,0:T(8,128)(4,1)S(1)}, pred[70,70]{1,0:T(8,128)(4,1)}, u32[]{:S(2)}) copy-start(pred[70,70]{1,0:T(8,128)(4,1)} %copy-done.28) | copy-start | bytes 14704
  1675.2 12.7 copy-start.21
  1688.0 7.3 copy-start.23
  1999.8 339.7 %reduce-scatter.35.cloned.1.call-start = ((), (), s32[]{:S(2)}) async-start(), calls=%async_computation.27 | async-start | bytes 1769472
  1999.9 9.3 copy-start.8
  2009.1 346.4 %reduce-scatter.33.cloned.1.call-start = ((), (), s32[]{:S(2)}) async-start(), calls=%async_computation.26 | async-start | bytes 589824
  2013.6 364.5 %reduce-scatter.31.cloned.1.call-start = ((), (), s32[]{:S(2)}) async-start(), calls=%async_computation.25 | async-start | bytes 1474560
  2323.7 78.8 %reduce-scatter.29.cloned.1.call-start = ((), (), s32[]{:S(2)}) async-start(), calls=%async_computation.24 | async-start | bytes 1769472 | tf_op jit(solution)/shard_map/reduce_scatter | solution.py:331
  2332.8 69.8 %copy-start.16 = (bf16[3,768,192]{1,2,0:T(8,128)(2,1)S(1)}, bf16[3,768,192]{1,2,0:T(8,128)(2,1)}, u32[]{:S(2)}) copy-start(bf16[3,768,192]{1,2,0:T(8,128)(2,1)} %copy-done.15) | copy-start | bytes 2654212
  2332.9 150.2 %all-reduce.6.cloned.1.call-start = ((), (), s32[]{:S(2)}) async-start(), calls=%async_computation.28 | async-start | bytes 3538944 | tf_op jit(solution)/shard_map/psum | solution.py:319
  2402.6 87.7 %reduce-scatter.27.cloned.1.call-start = ((), (), s32[]{:S(2)}) async-start(), calls=%async_computation.23 | async-start | bytes 5898240 | tf_op jit(solution)/shard_map/reduce_scatter | solution.py:109
  2410.6 98.0 %reduce-scatter.21.cloned.1.call-start = ((), (), s32[]{:S(2)}) async-start(), calls=%async_computation.17 | async-start | bytes 5898240 | tf_op jit(solution)/shard_map/reduce_scatter | solution.py:101
  2421.4 14.5 copy-start.41
  2436.0 14.5 copy-start.38
  2451.4 16.9 copy-start.30
  2451.4 25.3 slice-start
  2468.3 8.4 slice-start.1
  2476.7 13.5 copy-start.3
  2476.7 13.5 copy-start.27
  2476.8 13.5 copy-start.35
  2483.0 6.5 copy-start.32
  2483.0 25.6 copy-start.5
  2483.0 25.6 copy-start.7
  2483.0 25.6 copy-start.19
  2483.1 25.6 copy-start.25
  2497.0 61.5 %copy-start.1 = (bf16[27,64]{1,0:T(8,128)(2,1)S(1)}, bf16[27,64]{1,0:T(8,128)(2,1)}, u32[]{:S(2)}) copy-start(bf16[27,64]{1,0:T(8,128)(2,1)} %param.22) | copy-start | bytes 10372
  (23 other events, 49.8 us)
Sparse Core Ops, SparseCore 0:
  16.3 37.6 all-gather.8
  60.9 242.0 all-gather.10
  891.9 111.7 reduce-scatter.16
  1008.8 47.4 reduce-scatter.18
  1282.8 87.7 all-gather.22
  2000.0 313.6 reduce-scatter.24
  2316.5 22.9 reduce-scatter.34
  2342.4 13.1 reduce-scatter.32
  2358.5 19.5 reduce-scatter.30
  2380.8 21.7 reduce-scatter.28
  2406.5 76.4 all-reduce.5
Sparse Core Ops, SparseCore 1:
  1010.7 22.2 all-gather.14
  1061.9 37.3 all-gather.12
  1100.7 22.6 all-gather.16
  1125.1 37.3 all-gather.18
  1182.4 47.7 reduce-scatter.22
  1240.3 37.3 all-gather.20
  2410.6 47.7 reduce-scatter.26
  2460.8 47.7 reduce-scatter.20
where the time goes:
time: 2580 us; the launch traced here: 2570 us
  waiting for transfers between devices  1030 us (40%)
  local copies, waits for them, and re-layouts  874 us (34%)
  matrix products  380 us (15%)
  other arithmetic  200 us (8%)
  blocking collectives  62.9 us (2%)
    reduce_scatter x1, waiting for transfers between devices, local(): lax.psum_scatter(crop_cells(grad_grid).astype(jnp.bfloat16), 'ctx', scatt...  300 us
    all_gather x1, waiting for transfers between devices, local(): qkv_image = lax.all_gather(qkv_rows, 'ctx', axis=0, tiled=True)  240 us
    reshape x2, local copies, waits for them, and re-layouts, window_scores(): return total_scores.reshape(direct.shape[:3] + (WIN * WIN, WIN * WIN))  176 us
    reduce_scatter x1, waiting for transfers between devices, local(): lax.psum_scatter(attn_image, 'ctx', scatter_dimension=0, tiled=True)  105 us
    reshape x4, local copies, waits for them, and re-layouts, to_windows(): return cell_grid.reshape((per_side * per_side, WIN * WIN) + trail_dims)  92.6 us
    all_gather x1, waiting for transfers between devices, local(): grad_att_image = lax.all_gather(grad_att_rows, 'ctx', axis=0, tiled=True)  87.9 us
    reshape x1, local copies, waits for them, and re-layouts, local(): grad_scores.astype(jnp.bfloat16)  77.4 us
    all_gather x2, waiting for transfers between devices, rows_backward(): return lax.all_gather(row_block, 'tp', axis=0, tiled=True)  64.6 us
  transfers between devices with their start and end apart: 19, of which 16 were waited for; matrix products, arithmetic and copies ran while one was open for 7% of the time, Pallas kernels for 0%

commit v1 on v0

v1 whole, which is shorter than its diff:
```python
import functools
import math

import jax
import jax.numpy as jnp
from jax import lax
from jax.experimental import pallas as pl
from jax.experimental.pallas import tpu as pltpu
from jax.sharding import PartitionSpec as P

HEAD_DIM = 64
HEADS = 12
WIN = 14
SIDE = 64
BANDS = 4
PAIRS = 7
D = 768
EPSILON = 1e-06
MESH = pl.DeviceIdType.MESH
BF = jnp.bfloat16
F32 = jnp.float32

FULL = 224
PART = 128
NFULL = 3
NPART = 2
PBASE = NFULL * FULL
ROWS = PBASE + NPART * PART
PIECE = 144
GROUPS = 3
SEG = 32
MASKED = -1e9
VMEM_LIMIT = 60 * 2**20


def coords():
    return lax.axis_index("fsdp"), lax.axis_index("ctx"), lax.axis_index("tp")


def part_kind(ctx, tp, k, images):
    return (3 - ctx) * 8 + tp * 2 + k


def pack_matrix():
    row = lax.broadcasted_iota(jnp.int32, (PIECE, 128), 0)
    col = lax.broadcasted_iota(jnp.int32, (PIECE, 128), 1)
    wide = row < 128
    c = jnp.where(wide, row // 32, 4)
    u = jnp.where(wide, (row % 32) // 16, (row - 128) // 8)
    b = jnp.where(wide, row % 16, (row - 128) % 8)
    source = u * SIDE + c * WIN + b
    return ((source == col) & (b < WIN)).astype(BF)


def piece_places(ctx, tp, images):
    dev = ctx * 4 + tp
    out = []
    for i in range(images):
        for u in range(2):
            m = dev * 2 + u
            band = m // PAIRS
            p = m % PAIRS
            low = band == BANDS
            for c in range(5):
                q_low = i * 5 + c
                if c < 4:
                    f = i * 4 + c
                    d_ctx = jnp.where(low, 3 - q_low // 8, band)
                    d_tp = jnp.where(low, (q_low % 8) // 2, f // 3)
                    slot = jnp.where(low, NFULL + q_low % 2, f % 3)
                    d_row = jnp.where(low, PBASE + (q_low % 2) * PART, (f % 3) * FULL) + p * 32
                    out.append((i, u, c, d_ctx, d_tp, d_row, slot, p))
                else:
                    q = jnp.where(low, q_low, 15 + (3 - band) * 3 + i)
                    d_ctx = 3 - q // 8
                    d_tp = (q % 8) // 2
                    d_row = PBASE + (q % 2) * PART + p * 16
                    out.append((i, u, c, d_ctx, d_tp, d_row, NFULL + q % 2, p))
    return out


def window_places(ctx, tp):
    out = []
    for k in range(NFULL):
        f = tp * 3 + k
        for p in range(PAIRS):
            m = ctx * PAIRS + p
            dev = m // 2
            out.append((k, p, 32, None, f // 4, m % 2, f % 4, dev // 4, dev % 4, k * FULL + p * 32))
    for k in range(NPART):
        q = (3 - ctx) * 8 + tp * 2 + k
        bottom = q < 15
        corner = bottom & (q % 5 == 4)
        right = (q >= 15) & (q < 27)
        qr = jnp.where(right, q - 15, 0)
        band = jnp.where(bottom, BANDS, 3 - qr // 3)
        image = jnp.where(bottom, q // 5, qr % 3)
        base = PBASE + k * PART
        for p in range(PAIRS):
            m = band * PAIRS + p
            dev = jnp.minimum(m // 2, 15)
            place = (image, m % 2, dev // 4, dev % 4)
            if p < 4:
                wide = bottom & jnp.logical_not(corner)
                out.append((NFULL + k, p, 32, wide, image, m % 2, q % 5, dev // 4, dev % 4, base + p * 32))
            narrow = (corner | right) if p < 4 else right
            out.append((NFULL + k, p, 16, narrow, image, m % 2, 4, dev // 4, dev % 4, base + p * 16))
    return out


def group_barrier(extra=()):
    f, c, t = coords()
    sem = pltpu.get_barrier_semaphore()
    count = 0
    for dc in range(4):
        for dt in range(4):
            if dc == 0 and dt == 0:
                continue
            pl.semaphore_signal(sem, inc=1, device_id=(f, (c + dc) % 4, (t + dt) % 4), device_id_type=MESH)
            count += 1
    for dest in extra:
        pl.semaphore_signal(sem, inc=1, device_id=dest, device_id_type=MESH)
        count += 1
    pl.semaphore_wait(sem, count)


def send_or_copy(src, dst, dest, me, send_sem, recv_sem):
    (d_ctx, d_tp), (f, ctx, tp) = dest, me
    here = (d_ctx == ctx) & (d_tp == tp)

    @pl.when(here)
    def _():
        pltpu.make_async_copy(src, dst, recv_sem).start()

    @pl.when(jnp.logical_not(here))
    def _():
        pltpu.make_async_remote_copy(
            src_ref=src, dst_ref=dst, send_sem=send_sem, recv_sem=recv_sem,
            device_id=(f, d_ctx, d_tp), device_id_type=MESH,
        ).start()


def wait_sent(src, dest, me, send_sem):
    (d_ctx, d_tp), (f, ctx, tp) = dest, me
    away = jnp.logical_not((d_ctx == ctx) & (d_tp == tp))

    @pl.when(away)
    def _():
        pltpu.make_async_copy(src, src, send_sem).wait()


def start_pieces(stage, out, a, images, me, ss, rs):
    _, ctx, tp = me
    for n, (i, u, c, d_ctx, d_tp, d_row, slot, p) in enumerate(piece_places(ctx, tp, images)):
        rows = 32 if c < 4 else 16
        src = stage.at[a, i, u, pl.ds(c * 32, rows)]
        dst = out.at[pl.ds(pl.multiple_of(d_row, 16), rows)]
        send_or_copy(src, dst, (d_ctx, d_tp), me, ss.at[a, n], rs.at[a, slot, p])


def finish_piece_sends(stage, a, images, me, ss):
    _, ctx, tp = me
    for n, (i, u, c, d_ctx, d_tp, d_row, slot, p) in enumerate(piece_places(ctx, tp, images)):
        rows = 32 if c < 4 else 16
        wait_sent(stage.at[a, i, u, pl.ds(c * 32, rows)], (d_ctx, d_tp), me, ss.at[a, n])


def wait_pieces(out, a, me, rs):
    _, ctx, tp = me
    for slot, p, rows, exists, *_rest, row in window_places(ctx, tp):
        dst = out.at[pl.ds(row, rows)]
        wait = pltpu.make_async_copy(dst, dst, rs.at[a, slot, p]).wait
        if exists is None:
            wait()
        else:
            pl.when(exists)(wait)


def block(ref, w, t, f, part=None):
    rows, cols = ((192, 384), (192, 384), (384, 768), (768, 384))[w]
    row_at, col_at = (f, t) if w == 2 else (t, f)
    start, size = row_at * rows, rows
    if part is not None:
        size = rows // 2
        start = start + part * size
    row_slice = pl.ds(pl.multiple_of(start, 16), size)
    col_slice = pl.ds(pl.multiple_of(col_at * cols, 128), cols)
    if w == 0:
        return ref.at[:, row_slice, col_slice]
    return ref.at[row_slice, col_slice]


def shard_half(ref, w, part):
    size = (96, 96, 192, 384)[w]
    if w == 0:
        return ref.at[:, pl.ds(part * size, size)]
    return ref.at[pl.ds(part * size, size)]


def remote(src, dst, dest, send_sem, recv_sem):
    return pltpu.make_async_remote_copy(
        src_ref=src, dst_ref=dst, send_sem=send_sem, recv_sem=recv_sem, device_id=dest, device_id_type=MESH
    )


class Gather:
    def __init__(self, shards, wholes, me, ss, rs, ls):
        self.shards, self.wholes = shards, wholes
        self.ss, self.rs, self.ls = ss, rs, ls
        f, c, t = me
        y = (t + 2) % 4
        s = t + 1 - 2 * (t % 2)
        self.me = me
        self.other_f, self.other_y, self.other_s = 1 - f, y, s
        self.to_x, self.to_y, self.to_s = (1 - f, c, t), (f, c, y), (f, c, s)

    def copy(self, w, k):
        f, _, t = self.me
        g, y = self.other_f, self.other_y
        whole = self.wholes[w]
        own = self.shards[w]
        if k < 3:
            src, dst = own, block(whole, w, t, f)
            dest = (self.to_x, self.to_y, self.to_s)[k]
        elif k == 3:
            src = dst = block(whole, w, t, g, 0)
            dest = self.to_y
        elif k == 4:
            src = dst = block(whole, w, y, f, 1)
            dest = self.to_x
        elif k == 5:
            src = dst = block(whole, w, t, g)
            dest = self.to_s
        elif k == 6:
            src = dst = block(whole, w, y, f)
            dest = self.to_s
        else:
            src = dst = block(whole, w, y, g, k - 7)
            dest = self.to_s
        return remote(src, dst, dest, self.ss.at[w, k], self.rs.at[w, k])

    def landed(self, w, k):
        f, _, t = self.me
        g, y, s = self.other_f, self.other_y, self.other_s
        sy = (s + 2) % 4
        whole = self.wholes[w]
        place = (
            (t, g, None), (y, f, None), (s, f, None),
            (y, g, 0), (y, g, 1),
            (s, g, None), (sy, f, None), (sy, g, 0), (sy, g, 1),
        )[k]
        return block(whole, w, *place)

    def wait_recv(self, w, k):
        dst = self.landed(w, k)
        pltpu.make_async_copy(dst, dst, self.rs.at[w, k]).wait()

    def wait_send(self, w, k):
        src = self.landed(w, k)
        pltpu.make_async_copy(src, src, self.ss.at[w, k]).wait()

    def start_own(self, w):
        f, _, t = self.me
        for k in range(3):
            self.copy(w, k).start()
        pltpu.make_async_copy(self.shards[w], block(self.wholes[w], w, t, f), self.ls.at[w]).start()

    def forward_first(self, w):
        self.wait_recv(w, 0)
        self.copy(w, 3).start()
        self.copy(w, 5).start()
        self.wait_recv(w, 1)
        self.copy(w, 4).start()
        self.copy(w, 6).start()

    def forward_second(self, w):
        self.wait_recv(w, 3)
        self.copy(w, 7).start()
        self.wait_recv(w, 4)
        self.copy(w, 8).start()

    def finish(self, w):
        f, _, t = self.me
        for k in (2, 5, 6, 7, 8):
            self.wait_recv(w, k)
        for k in range(9):
            self.wait_send(w, k)
        pltpu.make_async_copy(self.shards[w], block(self.wholes[w], w, t, f), self.ls.at[w]).wait()


def gather_kernel(images, with_weights, *refs):
    if with_weights:
        x_ref, c_ref, wq, wp, wu, wd, xw, cw, gq, gp, gu, gd, stage, ss, rs, gss, grs, gls = refs
    else:
        x_ref, c_ref, xw, cw, stage, ss, rs = refs
    me = coords()
    f, ctx, tp = me
    extra = ((1 - f, ctx, tp),) if with_weights else ()
    group_barrier(extra)
    pack = pack_matrix()
    if with_weights:
        gather = Gather((wq, wp, wu, wd), (gq, gp, gu, gd), me, gss, grs, gls)
    for a, (src, out) in enumerate(((x_ref, xw), (c_ref, cw))):
        for i in range(images):
            for u in range(2):
                stage[a, i, u] = jnp.dot(
                    pack, src[i, pl.ds(u * 128, 128)], preferred_element_type=F32
                ).astype(BF)
        start_pieces(stage, out, a, images, me, ss, rs)
        if with_weights and a == 0:
            for w in range(4):
                gather.start_own(w)
    if with_weights:
        for w in range(4):
            gather.forward_first(w)
        for w in range(4):
            gather.forward_second(w)
    for a, out in enumerate((xw, cw)):
        wait_pieces(out, a, me, rs)
        finish_piece_sends(stage, a, images, me, ss)
    if with_weights:
        for w in range(4):
            gather.finish(w)


def gather_in(x3, c3, shards):
    images = x3.shape[0]
    any_spec = pl.BlockSpec(memory_space=pl.ANY)
    vmem = pl.BlockSpec(memory_space=pltpu.VMEM)
    with_weights = shards is not None
    token_shape = jax.ShapeDtypeStruct((ROWS, D), BF)
    out_shape = [token_shape, token_shape]
    scratch = [
        pltpu.VMEM((2, images, 2, PIECE, D), BF),
        pltpu.SemaphoreType.DMA((2, images * 10)),
        pltpu.SemaphoreType.DMA((2, NFULL + NPART, PAIRS)),
    ]
    args = [x3, c3]
    if with_weights:
        args += list(shards)
        out_shape += [
            jax.ShapeDtypeStruct(s, BF) for s in ((3, D, D), (D, D), (D, 4 * D), (4 * D, D))
        ]
        scratch += [pltpu.SemaphoreType.DMA((4, 9)), pltpu.SemaphoreType.DMA((4, 9)), pltpu.SemaphoreType.DMA((4,))]
    return pl.pallas_call(
        functools.partial(gather_kernel, images, with_weights),
        out_shape=out_shape,
        in_specs=[vmem, vmem] + [any_spec] * (len(args) - 2),
        out_specs=[any_spec] * len(out_shape),
        scratch_shapes=scratch,
        compiler_params=pltpu.CompilerParams(
            collective_id=0, has_side_effects=True, vmem_limit_bytes=VMEM_LIMIT
        ),
        name="tokens_and_weights_in",
    )(*args)


STEP_ROWS = (576, 192, 768, 768)


def add_rows(dst, src, rows, cols):
    size = 96 if rows % 96 == 0 else 64

    @pl.loop(0, rows // size)
    def _(n):
        here = pl.ds(pl.multiple_of(n * size, 16), size)
        dst[here] = (dst[here].astype(F32) + src[here].astype(F32)).astype(BF)


def add_view(dst, src, w):
    if w == 0:
        for k in range(3):
            view = dst.at[k]
            add_rows(view, src.at[k], view.shape[0], view.shape[1])
    else:
        add_rows(dst, src, dst.shape[0], dst.shape[1])


def copy_f32(dst, src, w):
    if w == 0:
        for k in range(3):
            copy_f32(dst.at[k], src.at[k], 1)
        return
    rows = dst.shape[0]
    size = 96 if rows % 96 == 0 else 64

    @pl.loop(0, rows // size)
    def _(n):
        here = pl.ds(pl.multiple_of(n * size, 16), size)
        dst[here] = src[here].astype(F32)


HALF_SHAPES = ((3, 96, 384), (96, 384), (192, 768), (384, 384))
SHARD_SHAPES = ((3, 192, 384), (192, 384), (384, 768), (768, 384))


def reduce_kernel(images, with_weights, *refs):
    if with_weights:
        (y_ref, g_ref, gq, gp, gu, gd, few_ref, y_out, g_out, oq, op, ou, od, few_out,
         stage, ss, rs, r1q, r1p, r1u, r1d, raq, rap, rau, rad, rzq, rzp, rzu, rzd,
         few_in, s1, v1, s2, v2, s3, v3, fs, fr) = refs
    else:
        y_ref, g_ref, y_out, g_out, stage, ss, rs = refs
    me = coords()
    f, ctx, tp = me
    group_barrier(((1 - f, ctx, tp),) if with_weights else ())

    places = window_places(ctx, tp)
    pairs = ((y_ref, y_out), (g_ref, g_out))
    for a, (src_ref, _) in enumerate(pairs):
        for n, (slot, p, rows, exists, image, u, c, d_ctx, d_tp, row) in enumerate(places):
            def go(a=a, n=n, rows=rows, image=image, u=u, c=c, d_ctx=d_ctx, d_tp=d_tp, row=row, src_ref=src_ref):
                src = src_ref.at[pl.ds(row, rows)]
                dst = stage.at[a, image, u, pl.ds(pl.multiple_of(c * 32, 16), rows)]
                send_or_copy(src, dst, (d_ctx, d_tp), me, ss.at[a, n], rs.at[a, image, u, c])
            if exists is None:
                go()
            else:
                pl.when(exists)(go)

    if with_weights:
        grads = (gq, gp, gu, gd)
        outs = (oq, op, ou, od)
        r1, ra, rz = (r1q, r1p, r1u, r1d), (raq, rap, rau, rad), (rzq, rzp, rzu, rzd)
        g, y, s = 1 - f, (tp + 2) % 4, tp + 1 - 2 * (tp % 2)
        sy = (s + 2) % 4
        to_x, to_y, to_s = (g, ctx, tp), (f, ctx, y), (f, ctx, s)
        order = (3, 2, 1, 0)
        waits = []

        def send(src, dst, dest, send_sem, recv_sem):
            cp = remote(src, dst, dest, send_sem, recv_sem)
            cp.start()
            waits.append(cp)
            return cp

        few_out[...] = few_ref[...]
        few_steps = (to_s, to_x, to_y, (f, ctx + 1 - 2 * (ctx % 2), tp), (f, (ctx + 2) % 4, tp))

        def few_start(n):
            few_in[5 + n] = few_out[...]
            return send(few_in.at[5 + n], few_in.at[n], few_steps[n], fs.at[n], fr.at[n])

        def few_finish(cp, n):
            cp.wait_recv()
            few_out[...] = few_out[...] + few_in[n]

        first = {}
        for w in order:
            for n, t_there in enumerate((s, sy)):
                for h in range(2):
                    first[w, n, h] = send(
                        block(grads[w], w, t_there, h), r1[w].at[n, h], to_s, s1.at[w, n, h], v1.at[w, n, h]
                    )
        few = few_start(0)

        phase1 = {}
        for w in order:
            for n, t_here in enumerate((tp, y)):
                for h in range(2):
                    first[w, n, h].wait_recv()
                    add_view(block(grads[w], w, t_here, h), r1[w].at[n, h], w)
            phase1[w] = (
                send(block(grads[w], w, tp, g, 0), ra[w].at[0], to_x, s2.at[w, 0], v2.at[w, 0]),
                send(block(grads[w], w, y, g, 0), ra[w].at[1], to_x, s2.at[w, 1], v2.at[w, 1]),
                send(block(grads[w], w, y, f, 1), ra[w].at[2], to_y, s2.at[w, 2], v2.at[w, 2]),
                send(block(grads[w], w, y, g, 1), ra[w].at[3], to_y, s2.at[w, 3], v2.at[w, 3]),
            )
        few_finish(few, 0)
        few = few_start(1)
        phase2 = {}
        for w in order:
            views = (
                block(grads[w], w, tp, f, 0), block(grads[w], w, y, f, 0),
                block(grads[w], w, tp, f, 1), block(grads[w], w, tp, g, 1),
            )
            for k in range(4):
                phase1[w][k].wait_recv()
                add_view(views[k], ra[w].at[k], w)
            phase2[w] = (
                send(block(grads[w], w, y, f, 0), ra[w].at[4], to_y, s2.at[w, 4], v2.at[w, 4]),
                send(block(grads[w], w, tp, g, 1), ra[w].at[5], to_x, s2.at[w, 5], v2.at[w, 5]),
            )
        few_finish(few, 1)
        few = few_start(2)

        outer = (ctx == 0) | (ctx == 3)
        inner = jnp.logical_not(outer)
        mid_peer = (f, 3 - ctx, tp)
        in_peer = (f, jnp.where(ctx == 0, 1, 2), tp)
        out_peer = (f, jnp.where(ctx == 1, 0, 3), tp)
        for w in order:
            for k in range(2):
                phase2[w][k].wait_recv()
                add_view(block(grads[w], w, tp, f, k), ra[w].at[4 + k], w)
            mine = block(grads[w], w, tp, f)

            @pl.when(outer)
            def _(w=w, mine=mine):
                remote(mine, rz[w].at[0], in_peer, s3.at[w, 0], v3.at[w, 0]).start()
        for w in order:
            mine = block(grads[w], w, tp, f)

            @pl.when(inner)
            def _(w=w, mine=mine):
                pltpu.make_async_copy(rz[w].at[0], rz[w].at[0], v3.at[w, 0]).wait()
                add_view(mine, rz[w].at[0], w)
                remote(mine, rz[w].at[1], mid_peer, s3.at[w, 0], v3.at[w, 1]).start()
        for w in order:
            mine = block(grads[w], w, tp, f)

            @pl.when(inner)
            def _(w=w, mine=mine):
                pltpu.make_async_copy(rz[w].at[1], rz[w].at[1], v3.at[w, 1]).wait()
                add_view(rz[w].at[1], mine, w)
                remote(rz[w].at[1], rz[w].at[2], out_peer, s3.at[w, 1], v3.at[w, 2]).start()
                copy_f32(outs[w], rz[w].at[1], w)
        few_finish(few, 2)
        few = few_start(3)
        for w in order:
            @pl.when(outer)
            def _(w=w):
                pltpu.make_async_copy(rz[w].at[2], rz[w].at[2], v3.at[w, 2]).wait()
                copy_f32(outs[w], rz[w].at[2], w)
        few_finish(few, 3)
        few = few_start(4)
        few_finish(few, 4)

        for cp in waits:
            cp.wait_send()
        for w in order:
            one = rz[w].at[0]
            pltpu.make_async_copy(one, one, s3.at[w, 0]).wait()

            @pl.when(inner)
            def _(one=one, w=w):
                pltpu.make_async_copy(one, one, s3.at[w, 1]).wait()

    unpack = pack_matrix()
    for a, (src_ref, out_ref) in enumerate(pairs):
        for i in range(images):
            for u in range(2):
                for c in range(5):
                    rows = 32 if c < 4 else 16
                    dst = stage.at[a, i, u, pl.ds(c * 32, rows)]
                    pltpu.make_async_copy(dst, dst, rs.at[a, i, u, c]).wait()
                out_ref[i, pl.ds(u * 128, 128)] = lax.dot_general(
                    unpack, stage[a, i, u], (((0,), (0,)), ((), ())), preferred_element_type=F32
                ).astype(BF)
        for n, (slot, p, rows, exists, image, u, c, d_ctx, d_tp, row) in enumerate(places):
            def done(a=a, n=n, rows=rows, d_ctx=d_ctx, d_tp=d_tp, row=row, src_ref=src_ref):
                wait_sent(src_ref.at[pl.ds(row, rows)], (d_ctx, d_tp), me, ss.at[a, n])
            if exists is None:
                done()
            else:
                pl.when(exists)(done)


def send_back(y, g, images, grads=None, few=None):
    vmem = pl.BlockSpec(memory_space=pltpu.VMEM)
    with_weights = grads is not None
    n_places = NFULL * PAIRS + NPART * (4 + PAIRS)
    token = jax.ShapeDtypeStruct((images, 256, D), BF)
    out_shape = [token, token]
    args = [y, g]
    dma = pltpu.SemaphoreType.DMA
    scratch = [
        pltpu.VMEM((2, images, 2, PIECE, D), BF),
        dma((2, n_places)),
        dma((2, images, 2, 5)),
    ]
    if with_weights:
        args += list(grads) + [few]
        out_shape += [jax.ShapeDtypeStruct(s, F32) for s in SHARD_SHAPES]
        out_shape += [jax.ShapeDtypeStruct(few.shape, F32)]
        scratch += [pltpu.VMEM((2, 2) + s, BF) for s in SHARD_SHAPES]
        scratch += [pltpu.VMEM((6,) + s, BF) for s in HALF_SHAPES]
        scratch += [pltpu.VMEM((3,) + s, BF) for s in SHARD_SHAPES]
        scratch += [pltpu.VMEM((10,) + few.shape, F32)]
        scratch += [dma((4, 2, 2)), dma((4, 2, 2)), dma((4, 6)), dma((4, 6)), dma((4, 2)), dma((4, 3)), dma((5,)), dma((5,))]
    return pl.pallas_call(
        functools.partial(reduce_kernel, images, with_weights),
        out_shape=out_shape,
        in_specs=[vmem] * len(args),
        out_specs=[vmem] * len(out_shape),
        scratch_shapes=scratch,
        compiler_params=pltpu.CompilerParams(
            collective_id=1, has_side_effects=True, vmem_limit_bytes=VMEM_LIMIT
        ),
        name="tokens_and_gradients_out",
    )(*args)


def barrel(x, shift, left):
    lanes = x.shape[-1]
    for bit in (1, 2, 4, 8):
        moved = pltpu.roll(x, lanes - bit if left else bit, 1)
        x = jnp.where((shift // bit) % 2 == 1, moved, x)
    return x


def row_places(rows, narrow):
    r = lax.broadcasted_iota(jnp.int32, (rows, 128), 0)
    if narrow is None:
        return r // 16, r % 16
    is_narrow = narrow > 0
    return jnp.where(is_narrow, r // 8, r // 16), jnp.where(is_narrow, r % 8, r % 16)


def half_mask(hh):
    lane = lax.broadcasted_iota(jnp.int32, (1, 128), 1)
    return ((lane // 64) == hh).astype(BF)


def nt(a, b):
    return lax.dot_general(a, b, (((1,), (1,)), ((), ())), preferred_element_type=F32)


def tn(a, b):
    return lax.dot_general(a, b, (((0,), (0,)), ((), ())), preferred_element_type=F32)


def key_rows(ref, base, rows, col, fill):
    part = ref[pl.ds(base, rows), pl.ds(col, 128)]
    if rows == FULL:
        return part
    return jnp.concatenate([part, jnp.broadcast_to(fill, (FULL - rows, 128)).astype(BF)], axis=0)


def attention_slot(qkv, rel_cols, bias_v, e_at, o_ref, p_ref, p_at, base, rows, narrow, x_scr):
    a_row, b_row = row_places(rows, narrow)
    q_all = qkv[pl.ds(base, rows), pl.ds(0, D)]
    lane = lax.broadcasted_iota(jnp.int32, (rows, 128), 1) % SEG
    for axis, pos in ((0, a_row), (1, b_row)):
        raw = jnp.dot(q_all, rel_cols[:, pl.ds(axis * 384, 384)], preferred_element_type=F32)
        for g in range(GROUPS):
            v = barrel(raw[:, g * 128:(g + 1) * 128], jnp.maximum(13 - pos, 0), True)
            hi = v.astype(BF).astype(F32)
            lo = pltpu.roll(v - hi, 16, 1)
            mix = jnp.where(lane < WIN, hi, jnp.where(lane >= 16, lo, 0.0))
            if axis == 0:
                mix = jnp.where(lane == 15, 1.0, mix)
            x_scr[pl.ds(0, rows), pl.ds(g * 256 + axis * 128, 128)] = mix.astype(BF)
    for hp in range(6):
        q = q_all[:, hp * 128:(hp + 1) * 128]
        k = key_rows(qkv, base, rows, D + hp * 128, jnp.zeros((1, 128), BF))
        v = key_rows(qkv, base, rows, 2 * D + hp * 128, bias_v[:, pl.ds(hp * 128, 128)])
        out = jnp.zeros((rows, 128), F32)
        for hh in range(2):
            h = hp * 2 + hh
            x = x_scr[pl.ds(0, rows), pl.ds((h // 4) * 256, 256)]
            s = nt(q, k * (half_mask(hh) * 0.125)) + nt(x, e_at[h % 4])
            p = jnp.exp(s - jnp.max(s, axis=-1, keepdims=True))
            p = (p * (1.0 / jnp.sum(p, axis=-1, keepdims=True))).astype(BF)
            p_ref[p_at * HEADS + h] = p
            out = out + jnp.dot(p, v * half_mask(hh), preferred_element_type=F32)
        o_ref[pl.ds(base, rows), pl.ds(hp * 128, 128)] = out.astype(BF)


def narrow_flag(k):
    _, ctx, tp = coords()
    q = (3 - ctx) * 8 + tp * 2 + k
    is_narrow = ((q < 15) & (q % 5 == 4)) | ((q >= 15) & (q < 27))
    return jnp.where(is_narrow, 1, 0)


def attention_kernel(qkv, rel_cols, bias_v, e_ref, o_ref, pf_ref, pp_ref, x_scr):
    @pl.loop(0, NFULL)
    def _(n):
        attention_slot(qkv, rel_cols, bias_v, e_ref.at[0], o_ref, pf_ref, n,
                       pl.multiple_of(n * FULL, 16), FULL, None, x_scr)

    @pl.loop(0, NPART)
    def _(n):
        attention_slot(qkv, rel_cols, bias_v, e_ref.at[1 + n], o_ref, pp_ref, n,
                       pl.multiple_of(PBASE + n * PART, 16), PART, narrow_flag(n), x_scr)


def attention(qkv, rel_cols, bias_v, e):
    vmem = pl.BlockSpec(memory_space=pltpu.VMEM)
    return pl.pallas_call(
        attention_kernel,
        out_shape=[
            jax.ShapeDtypeStruct((ROWS, D), BF),
            jax.ShapeDtypeStruct((NFULL * HEADS, FULL, FULL), BF),
            jax.ShapeDtypeStruct((NPART * HEADS, PART, FULL), BF),
        ],
        in_specs=[vmem] * 4,
        out_specs=[vmem] * 3,
        scratch_shapes=[pltpu.VMEM((FULL, GROUPS * 256), BF)],
        compiler_params=pltpu.CompilerParams(vmem_limit_bytes=VMEM_LIMIT),
        name="attention_forward",
    )(qkv, rel_cols, bias_v, e)


def attention_back_slot(qkv, do_ref, rel_cols, bias_v, e_at, p_ref, p_at, dqkv, d_scr, acc_scr, pad_acc,
                        rel_acc, base, rows, narrow):
    a_row, b_row = row_places(rows, narrow)
    for g in range(GROUPS):
        dx = jnp.zeros((rows, 256), F32)
        for hp in (2 * g, 2 * g + 1):
            q = qkv[pl.ds(base, rows), pl.ds(hp * 128, 128)]
            k = key_rows(qkv, base, rows, D + hp * 128, jnp.zeros((1, 128), BF))
            v = key_rows(qkv, base, rows, 2 * D + hp * 128, bias_v[:, pl.ds(hp * 128, 128)])
            do = do_ref[pl.ds(base, rows), pl.ds(hp * 128, 128)]
            dq = jnp.zeros((rows, 128), F32)
            dk = jnp.zeros((FULL, 128), F32)
            dv = jnp.zeros((FULL, 128), F32)
            for hh in range(2):
                h = hp * 2 + hh
                mask = half_mask(hh)
                do_m = do * mask
                dp = nt(do_m, v)
                p_low = p_ref[p_at * HEADS + h]
                t = p_low.astype(F32)
                tp = t * dp
                ds = (tp - t * jnp.sum(tp, axis=-1, keepdims=True)).astype(BF)
                dq = dq + jnp.dot(ds, k * (mask * 0.125), preferred_element_type=F32)
                dx = dx + jnp.dot(ds, e_at[h % 4], preferred_element_type=F32)
                dk = dk + tn(ds, q * (mask * 0.125))
                dv = dv + tn(p_low, do_m)
            acc_scr[pl.ds(0, rows), pl.ds(hp * 128, 128)] = dq
            dqkv[pl.ds(base, rows), pl.ds(D + hp * 128, 128)] = dk[:rows].astype(BF)
            dqkv[pl.ds(base, rows), pl.ds(2 * D + hp * 128, 128)] = dv[:rows].astype(BF)
            if rows < FULL:
                pad_acc[:, pl.ds(hp * 128, 128)] += jnp.sum(dv[rows:], axis=0, keepdims=True)
        lane = lax.broadcasted_iota(jnp.int32, (rows, 128), 1) % SEG
        for axis, pos in ((0, a_row), (1, b_row)):
            v = jnp.where(lane < WIN, dx[:, axis * 128:(axis + 1) * 128], 0.0)
            v = barrel(v, jnp.maximum(13 - pos, 0), False)
            d_scr[pl.ds(0, rows), pl.ds(axis * 384 + g * 128, 128)] = v.astype(BF)
    d = d_scr[pl.ds(0, rows), :]
    q_all = qkv[pl.ds(base, rows), pl.ds(0, D)]
    dq = acc_scr[pl.ds(0, rows), :] + nt(d, rel_cols[...])
    dqkv[pl.ds(base, rows), pl.ds(0, D)] = dq.astype(BF)
    rel_acc[...] += tn(d, q_all)


def attention_back_kernel(qkv, do_ref, rel_cols, bias_v, e_ref, pf_ref, pp_ref, dqkv, pad_ref, rel_ref,
                          d_scr, acc_scr, rel_acc):
    pad_ref[...] = jnp.zeros_like(pad_ref)
    rel_acc[...] = jnp.zeros_like(rel_acc)

    @pl.loop(0, NFULL)
    def _(n):
        attention_back_slot(qkv, do_ref, rel_cols, bias_v, e_ref.at[0], pf_ref, n, dqkv, d_scr, acc_scr, pad_ref,
                            rel_acc, pl.multiple_of(n * FULL, 16), FULL, None)

    @pl.loop(0, NPART)
    def _(n):
        attention_back_slot(qkv, do_ref, rel_cols, bias_v, e_ref.at[1 + n], pp_ref, n, dqkv, d_scr, acc_scr, pad_ref,
                            rel_acc, pl.multiple_of(PBASE + n * PART, 16), PART, narrow_flag(n))

    lane = lax.broadcasted_iota(jnp.int32, (SEG, D), 1) // HEAD_DIM
    for axis in range(2):
        total = jnp.zeros((SEG, D), F32)
        for h in range(HEADS):
            total = total + jnp.where(lane == h, rel_acc[pl.ds(axis * 384 + h * SEG, SEG), :], 0.0)
        rel_ref[axis] = total


def attention_back(qkv, do, rel_cols, bias_v, e, pf, pp):
    vmem = pl.BlockSpec(memory_space=pltpu.VMEM)
    return pl.pallas_call(
        attention_back_kernel,
        out_shape=[
            jax.ShapeDtypeStruct((ROWS, 3 * D), BF),
            jax.ShapeDtypeStruct((1, D), F32),
            jax.ShapeDtypeStruct((2, SEG, D), F32),
        ],
        in_specs=[vmem] * 7,
        out_specs=[vmem] * 3,
        scratch_shapes=[
            pltpu.VMEM((FULL, D), BF),
            pltpu.VMEM((FULL, D), F32),
            pltpu.VMEM((D, D), F32),
        ],
        compiler_params=pltpu.CompilerParams(vmem_limit_bytes=VMEM_LIMIT),
        name="attention_backward",
    )(qkv, do, rel_cols, bias_v, e, pf, pp)


def slot_tables():
    _, ctx, tp = coords()
    r = jnp.arange(FULL)
    full_real = (r % 16) < WIN
    real = [full_real] * NFULL
    keys = [(r // 16, r % 16, full_real)]
    for k in range(NPART):
        q = (3 - ctx) * 8 + tp * 2 + k
        bottom = q < 15
        corner = bottom & (q % 5 == 4)
        right = (q >= 15) & (q < 27)
        rp = r[:PART]
        real.append(
            jnp.where(corner, rp < 64, jnp.where(right, rp < 112, bottom & (rp % 16 < WIN)))
        )
        a_right = jnp.where(r < 112, r // 8, (r - 112) // 8)
        b_right = jnp.where(r < 112, r % 8, 8 + (r - 112) % 8)
        a_corner = jnp.where(r < 64, r // 8, jnp.where(r < 128, (r - 64) // 8, 8 + (r - 128) // 16))
        b_corner = jnp.where(r < 64, r % 8, jnp.where(r < 128, 8 + (r - 64) % 8, (r - 128) % 16))
        a = jnp.where(corner, a_corner, jnp.where(right, a_right, r // 16))
        b = jnp.where(corner, b_corner, jnp.where(right, b_right, r % 16))
        keys.append((a, b, b < WIN))
    a = jnp.stack([x[0] for x in keys])[:, None, :, None]
    b = jnp.stack([x[1] for x in keys])[:, None, :, None]
    ok = jnp.stack([x[2] for x in keys])[:, None, :, None]
    col = jnp.arange(256)[None, None, None, :]
    head = jnp.arange(4)[None, :, None, None]
    mine = ((col % 128) // SEG) == head
    j = col % 16
    pos = jnp.where(col < 128, a, b)
    one = (mine & ok & (j == pos) & (j < WIN)).astype(F32)
    out = (mine & jnp.logical_not(ok) & (col < 128) & (col % SEG == 15)).astype(F32) * MASKED
    return jnp.concatenate(real)[:, None], (one + out).astype(BF)


def relative_columns(rel_h, rel_w):
    parts = []
    eye = jnp.eye(HEADS, dtype=BF)
    for rel in (rel_h, rel_w):
        rev = jnp.pad(rel[::-1], ((0, SEG - rel.shape[0]), (0, 0))).T
        wide = eye[:, None, :, None] * rev[None, :, None, :]
        parts.append(wide.reshape(D, HEADS * SEG))
    return jnp.concatenate(parts, axis=1)


def norm_stats(v):
    mean = jnp.mean(v, axis=-1, keepdims=True)
    centered = v - mean
    r = lax.rsqrt(jnp.mean(centered * centered, axis=-1, keepdims=True) + EPSILON)
    return centered * r, r


def norm_back(n, xhat, r, gain):
    m = n * gain
    return r * (m - jnp.mean(m, -1, keepdims=True) - xhat * jnp.mean(m * xhat, -1, keepdims=True))


def gelu_both(u):
    x = jnp.abs(u) * math.sqrt(0.5)
    t = 1.0 / (1.0 + 0.3275911 * x)
    e = jnp.exp(-0.5 * u * u)
    poly = t * (0.254829592 + t * (-0.284496736 + t * (1.421413741 + t * (-1.453152027 + t * 1.061405429))))
    tail = 0.5 * poly * e
    phi = jnp.where(u >= 0, 1.0 - tail, tail)
    return u * phi, phi + u * e * (1.0 / math.sqrt(2 * math.pi))


def mm(a, b, dims="mk,kn->mn"):
    return jnp.einsum(dims, a, b, preferred_element_type=F32)


def whole_weights(shards):
    wq, wp, wu, wd = shards
    wq = lax.all_gather(lax.all_gather(wq, "fsdp", axis=2, tiled=True), "tp", axis=1, tiled=True)
    wp = lax.all_gather(lax.all_gather(wp, "fsdp", axis=1, tiled=True), "tp", axis=0, tiled=True)
    wu = lax.all_gather(lax.all_gather(wu, "fsdp", axis=0, tiled=True), "tp", axis=1, tiled=True)
    wd = lax.all_gather(lax.all_gather(wd, "fsdp", axis=1, tiled=True), "tp", axis=0, tiled=True)
    return wq, wp, wu, wd


def summed_weights(grads):
    dims = ((1, 2), (0, 1), (1, 0), (0, 1))
    out = []
    for grad, (t_dim, f_dim) in zip(grads, dims):
        part = lax.psum_scatter(grad, "tp", scatter_dimension=t_dim, tiled=True)
        part = lax.psum_scatter(part, "fsdp", scatter_dimension=f_dim, tiled=True)
        out.append(lax.psum(part, "ctx").astype(F32))
    return out


def local(direct, block_input, ln1_gain, ln1_bias, w_qkv, qkv_bias, rel_h, rel_w, w_proj, proj_bias,
          ln2_gain, ln2_bias, w_up, up_bias, w_down, down_bias, cotangent):
    images = block_input.shape[1]
    x3 = jnp.transpose(block_input, (1, 0, 2))
    c3 = jnp.transpose(cotangent, (1, 0, 2))
    shards = (jnp.transpose(w_qkv, (0, 2, 1)), w_proj, w_up, w_down)
    if direct:
        xw, cw, wq, wp, wu, wd = gather_in(x3, c3, shards)
    else:
        xw, cw = gather_in(x3, c3, None)
        wq, wp, wu, wd = whole_weights(shards)
    wq = wq.reshape(3 * D, D)
    real, e = slot_tables()
    rel_cols = relative_columns(rel_h, rel_w)
    g1, b1, g2, b2 = (v.astype(F32) for v in (ln1_gain, ln1_bias, ln2_gain, ln2_bias))
    x = jnp.where(real, xw, 0).astype(F32)
    cot_low = jnp.where(real, cw, 0)
    cot = cot_low.astype(F32)
    bias_three = jnp.concatenate([qkv_bias[0], jnp.zeros_like(qkv_bias[0]), qkv_bias[1]]).astype(F32)

    xhat1, r1 = norm_stats(x)
    n1 = jnp.where(real, xhat1 * g1 + b1, 0.0).astype(BF)
    qkv = (mm(n1, wq, "mk,nk->mn") + bias_three).astype(BF)
    attended, pf, pp = attention(qkv, rel_cols, qkv_bias[1:2], e)
    middle = x + mm(attended, wp) + proj_bias.astype(F32)
    xhat2, r2 = norm_stats(middle)
    n2 = (xhat2 * g2 + b2).astype(BF)
    gate_in = mm(n2, wu) + up_bias.astype(F32)
    hidden, slope = gelu_both(gate_in)
    hidden = hidden.astype(BF)
    out = (middle + mm(hidden, wd) + down_bias.astype(F32)).astype(BF)

    d_down_bias = jnp.sum(cot, axis=0)
    d_wd = mm(hidden, cot_low, "km,kn->mn").astype(BF)
    d_gate = (mm(cot_low, wd, "mk,nk->mn") * slope).astype(BF)
    d_wu = mm(n2, d_gate, "km,kn->mn").astype(BF)
    d_up_bias = jnp.sum(d_gate, axis=0, dtype=F32)
    d_n2 = mm(d_gate, wu, "mk,nk->mn")
    d_g2 = jnp.sum(d_n2 * xhat2, axis=0)
    d_b2 = jnp.sum(d_n2, axis=0)
    d_middle = cot + norm_back(d_n2, xhat2, r2, g2)
    branch = d_middle.astype(BF)
    d_proj_bias = jnp.sum(branch, axis=0, dtype=F32)
    d_wp = mm(attended, branch, "km,kn->mn").astype(BF)
    d_att = mm(branch, wp, "mk,nk->mn").astype(BF)
    dqkv, d_pad, d_rel = attention_back(qkv, d_att, rel_cols, qkv_bias[1:2], e, pf, pp)
    d_wq = mm(dqkv, n1, "km,kn->mn").astype(BF).reshape(3, D, D)
    sums = jnp.sum(dqkv, axis=0, dtype=F32)
    d_n1 = mm(dqkv, wq)
    d_g1 = jnp.sum(jnp.where(real, d_n1 * xhat1, 0.0), axis=0)
    d_b1 = jnp.sum(jnp.where(real, d_n1, 0.0), axis=0)
    d_x = (d_middle + norm_back(d_n1, xhat1, r1, g1)).astype(BF)
    d_rel = d_rel.reshape(2, SEG, HEADS, HEAD_DIM).sum(axis=2)[:, :27][:, ::-1]

    few = (d_g1, d_b1, sums[:D], sums[2 * D:] + d_pad[0], d_rel.reshape(-1), d_proj_bias, d_g2, d_b2, d_up_bias, d_down_bias)
    sizes = [v.shape[0] for v in few]
    flat = jnp.concatenate(few)
    pad = -flat.shape[0] % 1024
    flat = jnp.pad(flat, (0, pad)).reshape(-1, 128)
    grads = (d_wq, d_wp, d_wu, d_wd)
    if direct:
        out3, dx3, oq, op, ou, od, flat = send_back(out, d_x, images, grads, flat)
    else:
        out3, dx3 = send_back(out, d_x, images)
        oq, op, ou, od = summed_weights(grads)
        flat = lax.psum(flat, ("fsdp", "ctx", "tp"))
    flat = flat.reshape(-1)
    parts, at = [], 0
    for size in sizes:
        parts.append(flat[at:at + size])
        at += size
    s_g1, s_b1, s_q, s_v, s_rel, s_proj, s_g2, s_b2, s_up, s_down = parts
    s_rel = s_rel.reshape(2, 27, HEAD_DIM)
    return (
        jnp.transpose(out3, (1, 0, 2)), jnp.transpose(dx3, (1, 0, 2)), s_g1, s_b1,
        jnp.transpose(oq, (0, 2, 1)), jnp.stack([s_q, s_v]), s_rel[0], s_rel[1],
        op, s_proj, s_g2, s_b2, ou, s_up, od, s_down,
    )


def solution(mesh):
    direct = mesh.shape["fsdp"] == 2
    rows = P(("ctx", "tp"), "fsdp", None)
    w_specs = (P(None, "fsdp", "tp"), P("tp", "fsdp"), P("fsdp", "tp"), P("tp", "fsdp"))
    return jax.shard_map(
        functools.partial(local, direct),
        mesh=mesh,
        in_specs=(rows, P(), P(), w_specs[0], P(), P(), P(), w_specs[1], P(), P(), P(), w_specs[2], P(), w_specs[3], P(), rows),
        out_specs=(rows, rows, P(), P(), w_specs[0], P(), P(), P(), w_specs[1], P(), P(), P(), w_specs[2], P(), w_specs[3], P()),
        check_vma=False,
    )
```

time: 2580 us -> 477 us (0.18)
  waiting for transfers between devices: 1030 us -> 0 us
  local copies, waits for them, and re-layouts: 874 us -> 22.3 us
  Pallas kernels: 0 us -> 338 us
  matrix products: 380 us -> 92.6 us
  other arithmetic: 200 us -> 18.7 us
  blocking collectives: 62.9 us -> 0 us
    reduce_scatter x7 -> x0, waiting for transfers between devices: 531 us -> none  [the longest x1 300 us: local(): lax.psum_scatter(crop_cells(grad_grid).astype(jnp.bfloat16), 'ctx', scatt...]
    reshape x13 -> x4, local copies, waits for them, and re-layouts: 520 us -> 1.82 us  [the longest x1 1.05 us: local(): d_rel = d_rel.reshape(2, SEG, HEADS, HEAD_DIM).sum(axis=2)[:, :27][:, ::-1]]
    all_gather x8 -> x0, waiting for transfers between devices: 452 us -> none  [the longest x1 240 us: local(): qkv_image = lax.all_gather(qkv_rows, 'ctx', axis=0, tiled=True)]
    pallas_call x0 -> x4, Pallas kernels: none -> 338 us  [the longest x1 179 us: send_back(): pl.pallas_call(functools.partial(reduce_kernel, images, with_weights), ou...]
    dot_general x29 -> x12, matrix products: 358 us -> 92.6 us  [mm(): return jnp.einsum(dims, a, b, preferred_element_type=F32)]
    reduce_sum x14 -> x6, other arithmetic: 126 us -> 9.59 us  [the longest x1 2.85 us: local(): sums = jnp.sum(dqkv, axis=0, dtype=F32)]
    transpose x5 -> x1, local copies, waits for them, and re-layouts: 84.4 us -> 0.01 us  [relative_columns(): rev = jnp.pad(rel[::-1], ((0, SEG - rel.shape[0]), (0, 0))).T]
    dot_general x1 -> x0, local copies, waits for them, and re-layouts: 64.2 us -> none  [local(): jnp.einsum('sw,skitc->wkitc', pick_low, stacked, preferred_element_type=j...]
  transfers between devices with their start and end apart: 19 -> 0, of which waited for: 16 -> 0; matrix products, arithmetic and copies ran while one was open for 7% -> 0% of each run, Pallas kernels for 0% -> 0%
where the time goes in v1:
time: 477 us; the launch traced here: 473 us
  Pallas kernels  338 us (71%)
  matrix products  92.6 us (19%)
  local copies, waits for them, and re-layouts  22.3 us (5%)
  other arithmetic  18.7 us (4%)
    pallas_call x1, Pallas kernels, send_back(): pl.pallas_call(functools.partial(reduce_kernel, images, with_weights), ou...  179 us
    pallas_call x1, Pallas kernels, gather_in(): pl.pallas_call(functools.partial(gather_kernel, images, with_weights), ou...  102 us
    dot_general x12, matrix products, mm(): return jnp.einsum(dims, a, b, preferred_element_type=F32)  92.6 us
    pallas_call x1, Pallas kernels, attention_back(): pl.pallas_call(attention_back_kernel, out_shape=[jax.ShapeDtypeStruct((RO...  29.3 us
    pallas_call x1, Pallas kernels, attention(): pl.pallas_call(attention_kernel, out_shape=[jax.ShapeDtypeStruct((ROWS, D...  28 us

profile of v1, /device:TPU:14, one launch (start us, length us, event | category | flops | bytes accessed | tf_op | source)
XLA Modules:
  0.0 473.1 jit_solution(13916786029700234901)
XLA Ops:
  0.7 0.1 concatenate.24
  0.8 101.7 %tokens_and_weights_in.1 = (bf16[928,768]{1,0:T(8,128)(2,1)}, bf16[928,768]{1,0:T(8,128)(2,1)}, bf16[3,768,768]{2,1,0:T(8,128)(2,1)}, bf16[768,768]{1,0:T(8,128)...) custom-call(bf16[3,256,768]{2,1,0:T(8,128)(2,1)} %bitcast.68, bf16[3,256,768]{2,1,0:T(8,128)(2,1)} %bitcast.69, ...), custom_call_target="tpu_custom_call" | custom-call | tf_op jit(solution)/shard_map/tokens_and_weights_in/pallas_call | solution.py:345
  102.6 0.0 copy-start.12
  102.6 0.0 copy-start.17
  102.6 0.0 copy-start.18
  102.6 1.9 convert_reduce_fusion.2
  104.6 2.8 convert_reduce_fusion.3
  107.4 0.6 slice_reduce_fusion
  108.0 0.0 copy-start.13
  108.0 0.0 copy-start.14
  108.0 7.9 %add_convert_fusion.qkv = bf16[928,2304]{1,0:T(8,128)(2,1)} fusion(bf16[2304,768]{1,0:T(8,128)(2,1)} %bitcast.81, f32[2304]{0:T(1024)S(1)} %maximum_convert_fusion, f32[768]{0:T(1024)S(1)} %convert_element_type.108, f32[768]{0:T(1024)S(1)} %convert_element_type.107, f32[928]{0:T(1024)S(1)} %add_rsqrt_fusion.1, f32[928]{0:T(1024)S(1)} %broadcast_multiply_fusion.7, ...), kind=kOutput, calls=%fused_computation.12 | convolution fusion | flops 3294117888 | bytes 9264288 | tf_op jit(solution)/shard_map/mk,nk->mn/dot_general | solution.py:851
  116.1 0.2 select_compare_fusion
  116.4 2.1 add_convert_fusion.3.e_ref
  118.6 1.4 broadcast_multiply_fusion.1
  120.1 2.9 mul.207
  122.9 2.1 copy.34
  125.0 1.6 mul.210
  126.6 1.4 copy.35
  128.0 2.2 pad_maximum_fusion.rel_cols
  130.2 28.0 %attention_forward.1 = (bf16[928,768]{1,0:T(8,128)(2,1)}, bf16[36,224,224]{2,1,0:T(8,128)(2,1)}, bf16[24,128,224]{2,1,0:T(8,128)(2,1)}) custom-call(bf16[928,2304]{1,0:T(8,128)(2,1)} %add_convert_fusion.qkv, bf16[768,768]{1,0:T(8,128)(2,1)} %pad_maximum_fusion.rel_cols, bf16[1,768]{1,0:T(2,128)(2,1)} %get-tuple-element.82.bias_v, ...), custom_call_target="tpu_custom_call" | custom-call | tf_op jit(solution)/shard_map/attention_forward/pallas_call | solution.py:681
  158.2 0.0 slice-start.5
  158.2 3.0 fusion.45
  161.2 0.0 copy-start.20
  161.2 0.0 copy-start.15
  161.2 0.0 copy-start.21
  161.3 0.0 slice-start
  161.3 0.5 multiply_reduce_fusion.2
  161.7 0.2 copy-done.20
  161.9 0.0 copy-done.15
  162.0 0.0 copy-done.21
  162.0 0.0 slice-start.1
  162.1 15.5 %multiply_convert_fusion = (bf16[928,3072]{1,0:T(8,128)(2,1)}, f32[928,3072]{1,0:T(8,128)}) fusion(f32[3072]{0:T(1024)S(1)} %convert_element_type.119, bf16[768,3072]{1,0:T(8,128)(2,1)S(1)} %bitcast.80, f32[928,768]{1,0:T(8,128)S(1)} %get-tuple-element.86, f32[768]{0:T(1024)S(1)} %convert_element_type.117, f32[768]{0:T(1024)S(1)} %convert_element_type.116, ...), kind=kOutput, calls=%fused_computation.10 | convolution fusion | flops 4447985664 | bytes 24700160 | tf_op jit(solution)/shard_map/mk,kn->mn/dot_general | solution.py:851
  177.6 15.5 %convert_reduce_fusion = (f32[3072]{0:T(1024)S(1)}, bf16[928,3072]{1,0:T(8,128)(2,1)S(1)}) fusion(f32[928,3072]{1,0:T(8,128)} %get-tuple-element.88, f32[3072]{0:T(1024)S(1)} %convert_element_type.119, bf16[3072,768]{1,0:T(8,128)(2,1)S(1)} %bitcast.76, bf16[928,768]{1,0:T(8,128)(2,1)S(1)} %copy-done.5, pred[928]{0:T(1024)(128)(4,1)S(1)} %concatenate.24), kind=kOutput, calls=%fused_computation.9 | convolution fusion | flops 4459385856 | bytes 23274400 | tf_op jit(solution)/shard_map/mk,nk->mn/dot_general | solution.py:851
  193.1 5.2 %multiply_reduce_fusion = (f32[768]{0:T(1024)S(1)}, f32[928]{0:T(1024)S(1)}, f32[928]{0:T(1024)S(1)}, f32[768]{0:T(1024)S(1)}, f32[928,768]{1,0:T(8,128)S(1)}) fusion(f32[928,768]{1,0:T(8,128)S(1)} %get-tuple-element.86, f32[928]{0:T(1024)S(1)} %add_rsqrt_fusion, f32[928]{0:T(1024)S(1)} %broadcast_multiply_fusion.6, f32[768]{0:T(1024)S(1)} %convert_element_type.116, ...), kind=kOutput, calls=%fused_computation.39 | convolution fusion | flops 4385263616 | bytes 16145920 | tf_op jit(solution)/shard_map/mk,nk->mn/dot_general | solution.py:851
  198.3 1.5 convert_reduce_fusion.4
  199.8 2.4 convolution_convert_fusion.3.do_ref
  202.3 29.3 %attention_backward.1 = (bf16[928,2304]{1,0:T(8,128)(2,1)}, f32[1,768]{1,0:T(1,128)}, f32[2,32,768]{2,1,0:T(8,128)}) custom-call(bf16[928,2304]{1,0:T(8,128)(2,1)} %add_convert_fusion.qkv, bf16[928,768]{1,0:T(8,128)(2,1)} %convolution_convert_fusion.3.do_ref, bf16[768,768]{1,0:T(8,128)(2,1)} %pad_maximum_fusion.rel_cols, ...), custom_call_target="tpu_custom_call" | custom-call | tf_op jit(solution)/shard_map/attention_backward/pallas_call | solution.py:764
  231.6 9.0 %fusion.22 = (f32[768]{0:T(1024)S(1)}, f32[928]{0:T(1024)S(1)}, f32[928]{0:T(1024)S(1)}, f32[768]{0:T(1024)S(1)}, f32[928,768]{1,0:T(8,128)}) fusion(f32[928]{0:T(1024)S(1)} %add_rsqrt_fusion.1, f32[928]{0:T(1024)S(1)} %broadcast_multiply_fusion.7, pred[928]{0:T(1024)(128)(4,1)S(1)} %concatenate.24, bf16[928,768]{1,0:T(8,128)(2,1)S(1)} %copy-done, ...), kind=kOutput, calls=%fused_computation.36 | convolution fusion | flops 3293401600 | bytes 12116384 | tf_op jit(solution)/shard_map/mk,kn->mn/dot_general | solution.py:851
  240.6 2.9 convert_reduce_fusion.1
  243.5 1.0 reshape.684
  244.6 0.1 reduce_sum.164
  244.7 0.1 reshape.685
  244.9 0.6 pad_bitcast_fusion.refs_6_
  245.5 10.4 %convolution_convert_fusion.1.refs_4_ = bf16[768,3072]{1,0:T(8,128)(2,1)} fusion(bf16[928,3072]{1,0:T(8,128)(2,1)} %copy-done.26, f32[928,768]{1,0:T(8,128)} %copy-done.1, f32[768]{0:T(1024)S(1)} %convert_element_type.117, f32[768]{0:T(1024)S(1)} %convert_element_type.116, f32[928]{0:T(1024)S(1)} %add_rsqrt_fusion, f32[928]{0:T(1024)S(1)} %broadcast_multiply_fusion.6), kind=kOutput, calls=%fused_computation.14 | convolution fusion | flops 4384776192 | bytes 13284608 | tf_op jit(solution)/shard_map/km,kn->mn/dot_general | solution.py:851
  255.9 0.0 slice-start.6
  255.9 2.5 convolution_convert_fusion.4.refs_3_
  258.4 8.5 %convolution_convert_fusion.2 = bf16[2304,768]{1,0:T(8,128)(2,1)} fusion(bf16[928,2304]{1,0:T(8,128)(2,1)} %get-tuple-element.44, f32[768]{0:T(1024)S(1)} %convert_element_type.108, f32[768]{0:T(1024)S(1)} %convert_element_type.107, f32[928]{0:T(1024)S(1)} %add_rsqrt_fusion.1, f32[928]{0:T(1024)S(1)} %broadcast_multiply_fusion.7, ...), kind=kOutput, calls=%fused_computation.15 | convolution fusion | flops 3291611136 | bytes 9255072 | tf_op jit(solution)/shard_map/km,kn->mn/dot_general | solution.py:851
  266.9 0.0 slice-start.2
  266.9 2.2 fusion.20.refs_1_
  269.2 7.1 %convolution_convert_fusion.refs_5_ = bf16[3072,768]{1,0:T(8,128)(2,1)} fusion(bf16[928,3072]{1,0:T(8,128)(2,1)S(1)} %bitcast.84, bf16[928,768]{1,0:T(8,128)(2,1)S(1)} %copy-done.5, pred[928]{0:T(1024)(128)(4,1)S(1)} %concatenate.24), kind=kOutput, calls=%fused_computation.13 | convolution fusion | flops 4381925376 | bytes 11846560 | tf_op jit(solution)/shard_map/km,kn->mn/dot_general | solution.py:851
  276.3 5.7 %add_convert_fusion.1.refs_0_ = bf16[928,768]{1,0:T(8,128)(2,1)} fusion(f32[928,768]{1,0:T(8,128)S(1)} %copy-done.2, bf16[928,3072]{1,0:T(8,128)(2,1)S(1)} %bitcast.84, bf16[3072,768]{1,0:T(8,128)(2,1)S(1)} %bitcast.78, f32[768]{0:T(1024)S(1)} %convert_element_type.121), kind=kOutput, calls=%fused_computation.43 | convolution fusion | flops 4380991488 | bytes 14699520 | tf_op jit(solution)/shard_map/mk,kn->mn/dot_general | solution.py:851
  282.0 178.8 %tokens_and_gradients_out.1 = (bf16[3,256,768]{2,1,0:T(8,128)(2,1)}, bf16[3,256,768]{2,1,0:T(8,128)(2,1)}, f32[3,192,384]{2,1,0:T(8,128)}, f32[192,384]{1,0:T(8,...) custom-call(bf16[928,768]{1,0:T(8,128)(2,1)} %add_convert_fusion.1.refs_0_, ...), custom_call_target="tpu_custom_call" | custom-call | tf_op jit(solution)/shard_map/tokens_and_gradients_out/pallas_call | solution.py:581
  460.8 1.5 slice_bitcast_fusion.3
  462.4 0.6 pad_maximum_fusion.1
  463.0 0.7 slice.103
  463.7 0.1 reshape.687
  463.8 0.6 slice_bitcast_fusion
  464.4 1.3 slice_bitcast_fusion.2
  465.7 2.4 copy.58
  468.1 1.0 copy.59
  469.1 0.9 copy.60
  470.0 0.7 copy.61
  470.8 1.0 copy.62
  471.8 1.0 copy.63
  (111 shorter events, 0.5 us)
Async XLA Ops:
  102.6 4.8 %copy-start.12 = (bf16[2,768]{1,0:T(2,128)(2,1)S(1)}, bf16[2,768]{1,0:T(2,128)(2,1)}, u32[]{:S(2)}) copy-start(bf16[2,768]{1,0:T(2,128)(2,1)} %param.20) | copy-start | bytes 9220
  102.6 5.4 %copy-start.17 = (bf16[768]{0:T(1024)(128)(2,1)S(1)}, bf16[768]{0:T(1024)(128)(2,1)}, u32[]{:S(2)}) copy-start(bf16[768]{0:T(1024)(128)(2,1)} %param.17) | copy-start | bytes 4612
  102.6 5.4 %copy-start.18 = (bf16[768]{0:T(1024)(128)(2,1)S(1)}, bf16[768]{0:T(1024)(128)(2,1)}, u32[]{:S(2)}) copy-start(bf16[768]{0:T(1024)(128)(2,1)} %param.18) | copy-start | bytes 4612
  102.6 5.4 %copy-start = (bf16[928,768]{1,0:T(8,128)(2,1)S(1)}, bf16[928,768]{1,0:T(8,128)(2,1)}, u32[]{:S(2)}) copy-start(bf16[928,768]{1,0:T(8,128)(2,1)} %get-tuple-element.35) | copy-start | bytes 4276228
  108.0 10.5 %copy-start.13 = (bf16[27,64]{1,0:T(8,128)(2,1)S(1)}, bf16[27,64]{1,0:T(8,128)(2,1)}, u32[]{:S(2)}) copy-start(bf16[27,64]{1,0:T(8,128)(2,1)} %param.22) | copy-start | bytes 10372
  108.0 10.5 %copy-start.14 = (bf16[27,64]{1,0:T(8,128)(2,1)S(1)}, bf16[27,64]{1,0:T(8,128)(2,1)}, u32[]{:S(2)}) copy-start(bf16[27,64]{1,0:T(8,128)(2,1)} %param.21) | copy-start | bytes 10372
  130.2 28.0 %copy-start.19 = (bf16[768]{0:T(1024)(128)(2,1)S(1)}, bf16[768]{0:T(1024)(128)(2,1)}, u32[]{:S(2)}) copy-start(bf16[768]{0:T(1024)(128)(2,1)} %param.24) | copy-start | bytes 4612
  130.2 28.0 %copy-start.24 = (bf16[768,768]{1,0:T(8,128)(2,1)S(1)}, bf16[768,768]{1,0:T(8,128)(2,1)}, u32[]{:S(2)}) copy-start(bf16[768,768]{1,0:T(8,128)(2,1)} %get-tuple-element.38) | copy-start | bytes 3538948
  158.2 3.9 slice-start.4
  158.2 3.8 slice-start.5
  161.2 37.1 %copy-start.1 = (f32[928,768]{1,0:T(8,128)}, f32[928,768]{1,0:T(8,128)S(1)}, u32[]{:S(2)}) copy-start(f32[928,768]{1,0:T(8,128)S(1)} %get-tuple-element.86) | copy-start | bytes 8552452
  161.2 0.7 copy-start.20
  161.2 0.7 copy-start.15
  161.2 0.8 copy-start.21
  161.3 16.3 %slice-start = ((s8[4718592]{0:T(1024)(128)(4,1)}), s8[524288]{0:T(1024)(128)(4,1)S(1)}, s32[]{:S(2)}) async-start(s8[4718592]{0:T(1024)(128)(4,1)} %bitcast.75), calls=%async_computation | async-start | bytes 1048576
  162.0 15.5 %copy-start.5 = (bf16[928,768]{1,0:T(8,128)(2,1)S(1)}, bf16[928,768]{1,0:T(8,128)(2,1)}, u32[]{:S(2)}) copy-start(bf16[928,768]{1,0:T(8,128)(2,1)} %get-tuple-element.41) | copy-start | bytes 4276228
  162.0 15.5 %slice-start.1 = ((s8[4718592]{0:T(1024)(128)(4,1)}), s8[4194304]{0:T(1024)(128)(4,1)S(1)}, s32[]{:S(2)}) async-start(s8[4718592]{0:T(1024)(128)(4,1)} %bitcast.75), calls=%async_computation.1 | async-start | bytes 8388608
  193.1 5.2 %copy-start.26 = (bf16[928,3072]{1,0:T(8,128)(2,1)}, bf16[928,3072]{1,0:T(8,128)(2,1)S(1)}, u32[]{:S(2)}) copy-start(bf16[928,3072]{1,0:T(8,128)(2,1)S(1)} %get-tuple-element.92) | copy-start | bytes 17104900
  198.3 1.5 copy-start.25
  199.8 2.5 copy-start.3
  240.6 2.9 copy-start.16
  245.5 10.4 %copy-start.4 = (f32[928,768]{1,0:T(8,128)S(1)}, f32[928,768]{1,0:T(8,128)}, u32[]{:S(2)}) copy-start(f32[928,768]{1,0:T(8,128)} %copy-done.3) | copy-start | bytes 8552452
  245.5 10.4 %copy-start.23 = (bf16[928,768]{1,0:T(8,128)(2,1)S(1)}, bf16[928,768]{1,0:T(8,128)(2,1)}, u32[]{:S(2)}) copy-start(bf16[928,768]{1,0:T(8,128)(2,1)} %get-tuple-element.37) | copy-start | bytes 4276228
  255.9 13.2 %slice-start.6 = ((s8[5701632]{0:T(1024)(128)(4,1)}), s8[4194304]{0:T(1024)(128)(4,1)S(1)}, s32[]{:S(2)}) async-start(s8[5701632]{0:T(1024)(128)(4,1)} %bitcast.83), calls=%async_computation.6 | async-start | bytes 8388608
  258.4 8.5 %copy-start.6 = (f32[928,768]{1,0:T(8,128)S(1)}, f32[928,768]{1,0:T(8,128)}, u32[]{:S(2)}) copy-start(f32[928,768]{1,0:T(8,128)} %get-tuple-element.90) | copy-start | bytes 8552452
  258.4 10.7 %slice-start.7 = ((s8[5701632]{0:T(1024)(128)(4,1)}), s8[1507328]{0:T(1024)(128)(4,1)S(1)}, s32[]{:S(2)}) async-start(s8[5701632]{0:T(1024)(128)(4,1)} %bitcast.83), calls=%async_computation.7 | async-start | bytes 3014656
  266.9 9.3 %slice-start.2 = ((s8[4718592]{0:T(1024)(128)(4,1)}), s8[524288]{0:T(1024)(128)(4,1)S(1)}, s32[]{:S(2)}) async-start(s8[4718592]{0:T(1024)(128)(4,1)} %bitcast.77), calls=%async_computation.2 | async-start | bytes 1048576
  269.2 7.1 %copy-start.22 = (bf16[768]{0:T(1024)(128)(2,1)S(1)}, bf16[768]{0:T(1024)(128)(2,1)}, u32[]{:S(2)}) copy-start(bf16[768]{0:T(1024)(128)(2,1)} %param.30) | copy-start | bytes 4612
  269.2 7.1 %copy-start.2 = (f32[928,768]{1,0:T(8,128)S(1)}, f32[928,768]{1,0:T(8,128)}, u32[]{:S(2)}) copy-start(f32[928,768]{1,0:T(8,128)} %copy-done.1) | copy-start | bytes 8552452
  269.2 7.1 %slice-start.3 = ((s8[4718592]{0:T(1024)(128)(4,1)}), s8[4194304]{0:T(1024)(128)(4,1)S(1)}, s32[]{:S(2)}) async-start(s8[4718592]{0:T(1024)(128)(4,1)} %bitcast.77), calls=%async_computation.3 | async-start | bytes 8388608
  460.8 7.3 %copy-start.9 = (bf16[3,256,768]{2,1,0:T(8,128)(2,1)S(1)}, bf16[3,256,768]{2,1,0:T(8,128)(2,1)}, u32[]{:S(2)}) copy-start(bf16[3,256,768]{2,1,0:T(8,128)(2,1)} %get-tuple-element.48) | copy-start | bytes 3538948
  460.8 8.3 %copy-start.10 = (f32[3,192,384]{2,1,0:T(8,128)S(1)}, f32[3,192,384]{2,1,0:T(8,128)}, u32[]{:S(2)}) copy-start(f32[3,192,384]{2,1,0:T(8,128)} %get-tuple-element.50) | copy-start | bytes 2654212
  465.7 4.3 copy-start.11
  468.1 2.7 copy-start.8
  469.1 2.6 copy-start.7

commit v2 on v1

--- a/solution.py
+++ b/solution.py
@@ -176,7 +176,353 @@
             pl.when(exists)(wait)
 
 
+UNITS = 6
+BLOCKS = ((192, 384), (192, 384), (192, 384), (192, 384), (384, 768), (768, 384))
+OVER_Y = (0, 0, 0, 0, 96, 192)
+
+
 def block(ref, w, t, f, part=None):
+    rows, cols = BLOCKS[w]
+    row_at, col_at = (f, t) if w == 4 else (t, f)
+    start, size = part if part is not None else (0, rows)
+    return ref.at[
+        pl.ds(pl.multiple_of(row_at * rows + start, 16), size),
+        pl.ds(pl.multiple_of(col_at * cols, 128), cols),
+    ]
+
+
+def remote(src, dst, dest, send_sem, recv_sem):
+    return pltpu.make_async_remote_copy(
+        src_ref=src, dst_ref=dst, send_sem=send_sem, recv_sem=recv_sem, device_id=dest, device_id_type=MESH
+    )
+
+
+class Gather:
+    def __init__(self, shards, wholes, me, ss, rs, ls):
+        self.shards, self.wholes = shards, wholes
+        self.ss, self.rs, self.ls = ss, rs, ls
+        f, c, t = me
+        self.me = me
+        self.g, self.y, self.s = 1 - f, (t + 2) % 4, t + 1 - 2 * (t % 2)
+        self.to_x, self.to_y, self.to_s = (self.g, c, t), (f, c, self.y), (f, c, self.s)
+
+    def copies(self, w):
+        a = OVER_Y[w]
+        return [k for k in range(9) if a or k not in (3, 7)]
+
+    def parts(self, w):
+        a, rows = OVER_Y[w], BLOCKS[w][0]
+        return (0, a), (a, rows - a)
+
+    def copy(self, w, k):
+        f, _, t = self.me
+        g, y = self.g, self.y
+        whole = self.wholes[w]
+        first, second = self.parts(w)
+        if k < 3:
+            src, dst = self.shards[w], block(whole, w, t, f)
+            dest = (self.to_x, self.to_y, self.to_s)[k]
+        else:
+            src = dst = block(whole, w, *(
+                (t, g, first), (y, f, second), (t, g), (y, f), (y, g, first), (y, g, second)
+            )[k - 3])
+            dest = (self.to_y, self.to_x, self.to_s, self.to_s, self.to_s, self.to_s)[k - 3]
+        return remote(src, dst, dest, self.ss.at[w, k], self.rs.at[w, k])
+
+    def landed(self, w, k):
+        f, _, t = self.me
+        g, y, s = self.g, self.y, self.s
+        sy = (s + 2) % 4
+        first, second = self.parts(w)
+        place = (
+            (t, g), (y, f), (s, f), (y, g, first), (y, g, second),
+            (s, g), (sy, f), (sy, g, first), (sy, g, second),
+        )[k]
+        return block(self.wholes[w], w, *place)
+
+    def wait_recv(self, w, k):
+        dst = self.landed(w, k)
+        pltpu.make_async_copy(dst, dst, self.rs.at[w, k]).wait()
+
+    def start_own(self, w, ks=(0, 1, 2)):
+        f, _, t = self.me
+        for k in ks:
+            self.copy(w, k).start()
+        if 2 in ks:
+            pltpu.make_async_copy(self.shards[w], block(self.wholes[w], w, t, f), self.ls.at[w]).start()
+
+    def forward_x(self, w):
+        self.wait_recv(w, 0)
+        if OVER_Y[w]:
+            self.copy(w, 3).start()
+        self.copy(w, 5).start()
+
+    def forward_y(self, w):
+        self.wait_recv(w, 1)
+        self.copy(w, 4).start()
+        self.copy(w, 6).start()
+
+    def forward_second(self, w):
+        if OVER_Y[w]:
+            self.wait_recv(w, 3)
+            self.copy(w, 7).start()
+        self.wait_recv(w, 4)
+        self.copy(w, 8).start()
+
+    def arrived(self, w):
+        f, _, t = self.me
+        for k in (2, 5, 6, 7, 8):
+            if k in self.copies(w):
+                self.wait_recv(w, k)
+        pltpu.make_async_copy(self.shards[w], block(self.wholes[w], w, t, f), self.ls.at[w]).wait()
+
+    def sent(self, w):
+        for k in self.copies(w):
+            src = self.landed(w, k)
+            pltpu.make_async_copy(src, src, self.ss.at[w, k]).wait()
+
+
+def part_facts(k):
+    _, ctx, tp = coords()
+    q = (3 - ctx) * 8 + tp * 2 + k
+    bottom = q < 15
+    corner = bottom & (q % 5 == 4)
+    right = (q >= 15) & (q < 27)
+    return bottom, corner, right
+
+
+def row_real(slot, rows):
+    r = lax.broadcasted_iota(jnp.int32, (rows, 1), 0)
+    wide = (r % 16) < WIN
+    if slot < NFULL:
+        return wide
+    bottom, corner, right = part_facts(slot - NFULL)
+    limit = jnp.where(corner, 64, jnp.where(right, 112, jnp.where(bottom, PART, 0)))
+    narrow = jnp.where(corner | right, 1, 0)
+    return (r < limit) & (wide | (narrow > 0))
+
+
+def key_places(kind, shape):
+    r = lax.broadcasted_iota(jnp.int32, shape, 0)
+    a, b = r // 16, r % 16
+    if kind == 0:
+        return a, b
+    _, corner, right = part_facts(kind - 1)
+    corner, right = jnp.where(corner, 1, 0), jnp.where(right, 1, 0)
+    a_right = jnp.where(r < 112, r // 8, (r - 112) // 8)
+    b_right = jnp.where(r < 112, r % 8, 8 + (r - 112) % 8)
+    a_corner = jnp.where(r < 64, r // 8, jnp.where(r < 128, (r - 64) // 8, 8 + (r - 128) // 16))
+    b_corner = jnp.where(r < 64, r % 8, jnp.where(r < 128, 8 + (r - 64) % 8, (r - 128) % 16))
+    a = jnp.where(corner > 0, a_corner, jnp.where(right > 0, a_right, a))
+    b = jnp.where(corner > 0, b_corner, jnp.where(right > 0, b_right, b))
+    return a, b
+
+
+def build_keys(e_ref):
+    shape = (FULL, 128)
+    col = lax.broadcasted_iota(jnp.int32, shape, 1)
+    j = col % 16
+    for kind in range(1 + NPART):
+        a, b = key_places(kind, shape)
+        ok = b < WIN
+        along_a = jnp.where(ok & (j == a) & (j < WIN), 1.0, 0.0)
+        along_a = jnp.where(jnp.logical_not(ok) & (col % SEG == 15), MASKED, along_a)
+        along_b = jnp.where(ok & (j == b) & (j < WIN), 1.0, 0.0)
+        for head in range(4):
+            mine = col // SEG == head
+            e_ref[kind, head, :, pl.ds(0, 128)] = jnp.where(mine, along_a, 0.0).astype(BF)
+            e_ref[kind, head, :, pl.ds(128, 128)] = jnp.where(mine, along_b, 0.0).astype(BF)
+
+
+def build_relative(rel_ref, out_ref):
+    out_ref[...] = jnp.zeros((D, D), BF)
+    i = lax.broadcasted_iota(jnp.int32, (SEG, 128), 0)
+    lane = lax.broadcasted_iota(jnp.int32, (SEG, 128), 1)
+    turn = (lane % SEG == 26 - i).astype(BF)
+    lane64 = lax.broadcasted_iota(jnp.int32, (HEAD_DIM, 128), 1) // SEG
+    for axis in range(2):
+        rev = tn(rel_ref[axis], turn)
+        for h in range(HEADS):
+            out_ref[pl.ds(h * HEAD_DIM, HEAD_DIM), pl.ds(axis * 384 + (h // 4) * 128, 128)] = (
+                jnp.where(lane64 == h % 4, rev, 0.0).astype(BF)
+            )
+
+
+def slots():
+    return [(k, k * FULL, FULL) for k in range(NFULL)] + [
+        (NFULL + k, PBASE + k * PART, PART) for k in range(NPART)
+    ]
+
+
+def forward_kernel(images, direct, *refs):
+    if direct:
+        (x_ref, c_ref, wq_s, wp_s, wu_s, wd_s, vec, rel_ref,
+         x_o, c_o, n1_o, qkv_o, att_o, p_o, wq_o, wp, wu, wd, e_o, rel_o,
+         stage, xw, cw, n1, qkv, att, p_buf, wq, e, rel_cols, x_scr, bias_v, ss, rs, gss, grs, gls, os) = refs
+    else:
+        (x_ref, c_ref, wq_s, vec, rel_ref,
+         x_o, c_o, n1_o, qkv_o, att_o, p_o, e_o, rel_o,
+         stage, xw, cw, n1, qkv, att, p_buf, wq, e, rel_cols, x_scr, bias_v, ss, rs, os) = refs
+    me = coords()
+    f, ctx, tp = me
+    group_barrier(((1 - f, ctx, tp),) if direct else ())
+    pack = pack_matrix()
+
+    def stage_tokens(a, src):
+        for i in range(images):
+            for u in range(2):
+                stage[a, i, u] = jnp.dot(
+                    pack, src[i, pl.ds(u * 128, 128)], preferred_element_type=F32
+                ).astype(BF)
+
+    out_copies = []
+
+    def write(src, dst):
+        cp = pltpu.make_async_copy(src, dst, os.at[len(out_copies)])
+        cp.start()
+        out_copies.append(cp)
+
+    if direct:
+        shards = (wq_s.at[0], wq_s.at[1], wq_s.at[2], wp_s, wu_s, wd_s)
+        gather = Gather(shards, (wq.at[0], wq.at[1], wq.at[2], wp, wu, wd), me, gss, grs, gls)
+        for w in range(3):
+            gather.start_own(w)
+    else:
+        load = pltpu.make_async_copy(wq_s, wq, os.at[15])
+        load.start()
+    stage_tokens(0, x_ref)
+    start_pieces(stage, xw, 0, images, me, ss, rs)
+    build_keys(e)
+    build_relative(rel_ref, rel_cols)
+    write(e, e_o)
+    write(rel_cols, rel_o)
+    stage_tokens(1, c_ref)
+    if direct:
+        for w in range(3):
+            gather.forward_x(w)
+            gather.forward_y(w)
+        gather.start_own(3)
+        gather.start_own(4)
+    wait_pieces(xw, 0, me, rs)
+    for slot, base, rows in slots():
+        here = pl.ds(base, rows)
+        real = row_real(slot, rows)
+        x = jnp.where(real, xw[here].astype(F32), 0.0)
+        xw[here] = x.astype(BF)
+        mean = jnp.mean(x, axis=-1, keepdims=True)
+        centered = x - mean
+        r = lax.rsqrt(jnp.mean(centered * centered, axis=-1, keepdims=True) + EPSILON)
+        n1[here] = jnp.where(
+            real, centered * r * vec[pl.ds(0, 1), pl.ds(0, D)] + vec[pl.ds(1, 1), pl.ds(0, D)], 0.0
+        ).astype(BF)
+    write(xw, x_o)
+    write(n1, n1_o)
+    if direct:
+        for w in range(3):
+            gather.forward_second(w)
+        gather.start_own(5)
+        start_pieces(stage, cw, 1, images, me, ss, rs)
+        for w in range(3):
+            gather.arrived(w)
+        write(wq, wq_o)
+    else:
+        load.wait()
+        start_pieces(stage, cw, 1, images, me, ss, rs)
+
+    @pl.loop(0, 6)
+    def _(n):
+        cols = pl.ds(pl.multiple_of((n % 2) * 384, 128), 384)
+        out = nt(n1[...], wq[n // 2, cols, :])
+        there = pl.ds(pl.multiple_of(n * 384, 128), 384)
+        qkv[:, there] = (out + vec[pl.ds(2, 1), there]).astype(BF)
+
+    write(qkv, qkv_o)
+    bias_v[...] = vec[pl.ds(2, 1), pl.ds(2 * D, D)]
+
+    @pl.loop(0, NFULL)
+    def _(n):
+        attention_slot(qkv, rel_cols, bias_v, e.at[0], att, p_buf, pl.multiple_of(n * FULL, 16), FULL, None, x_scr)
+        if direct:
+            @pl.when(n == 0)
+            def _():
+                gather.forward_x(3)
+                gather.forward_y(3)
+                gather.forward_x(4)
+                gather.forward_y(4)
+
+            @pl.when(n == 1)
+            def _():
+                gather.forward_second(3)
+                gather.forward_x(5)
+                gather.forward_y(5)
+
+            @pl.when(n == 2)
+            def _():
+                gather.forward_second(4)
+
+    @pl.loop(0, NPART)
+    def _(n):
+        attention_slot(qkv, rel_cols, bias_v, e.at[1 + n], att, p_buf,
+                       pl.multiple_of(PBASE + n * PART, 16), PART, narrow_flag(n), x_scr)
+
+    write(att, att_o)
+    write(p_buf, p_o)
+    if direct:
+        gather.forward_second(5)
+    wait_pieces(cw, 1, me, rs)
+    for slot, base, rows in slots():
+        here = pl.ds(base, rows)
+        cw[here] = jnp.where(row_real(slot, rows), cw[here].astype(F32), 0.0).astype(BF)
+    write(cw, c_o)
+    if direct:
+        for w in range(3, UNITS):
+            gather.arrived(w)
+        for w in range(UNITS):
+            gather.sent(w)
+    for a in range(2):
+        finish_piece_sends(stage, a, images, me, ss)
+    for cp in out_copies:
+        cp.wait()
+
+
+def forward(x3, c3, shards, wq_whole, vec, rel):
+    images = x3.shape[0]
+    any_spec = pl.BlockSpec(memory_space=pl.ANY)
+    vmem = pl.BlockSpec(memory_space=pltpu.VMEM)
+    direct = wq_whole is None
+    dma = pltpu.SemaphoreType.DMA
+    shape = jax.ShapeDtypeStruct
+    tokens = shape((ROWS, D), BF)
+    outs = [tokens, tokens, tokens, shape((ROWS, 3 * D), BF), tokens, shape((ROWS, HEADS * 256), BF)]
+    if direct:
+        outs += [shape(s, BF) for s in ((3, D, D), (D, D), (D, 4 * D), (4 * D, D))]
+    outs += [shape((1 + NPART, 4, FULL, 256), BF), shape((D, D), BF)]
+    scratch = [
+        pltpu.VMEM((2, images, 2, PIECE, D), BF),
+        pltpu.VMEM((ROWS, D), BF), pltpu.VMEM((ROWS, D), BF), pltpu.VMEM((ROWS, D), BF),
+        pltpu.VMEM((ROWS, 3 * D), BF), pltpu.VMEM((ROWS, D), BF), pltpu.VMEM((ROWS, HEADS * 256), BF),
+        pltpu.VMEM((3, D, D), BF), pltpu.VMEM((1 + NPART, 4, FULL, 256), BF), pltpu.VMEM((D, D), BF),
+        pltpu.VMEM((FULL, GROUPS * 256), BF), pltpu.VMEM((1, D), F32),
+        dma((2, images * 10)), dma((2, NFULL + NPART, PAIRS)),
+    ]
+    if direct:
+        scratch += [dma((UNITS, 9)), dma((UNITS, 9)), dma((UNITS,))]
+    scratch += [dma((16,))]
+    weights = list(shards) if direct else [wq_whole]
+    return pl.pallas_call(
+        functools.partial(forward_kernel, images, direct),
+        out_shape=outs,
+        in_specs=[vmem, vmem] + [any_spec] * len(weights) + [vmem, vmem],
+        out_specs=[any_spec] * len(outs),
+        scratch_shapes=scratch,
+        compiler_params=pltpu.CompilerParams(
+            collective_id=0, has_side_effects=True, vmem_limit_bytes=VMEM_LIMIT
+        ),
+        name="forward_attention",
+    )(x3, c3, *weights, vec, rel)
+
+
+def grad_block(ref, w, t, f, part=None):
     rows, cols = ((192, 384), (192, 384), (384, 768), (768, 384))[w]
     row_at, col_at = (f, t) if w == 2 else (t, f)
     start, size = row_at * rows, rows
@@ -188,174 +534,6 @@
     if w == 0:
         return ref.at[:, row_slice, col_slice]
     return ref.at[row_slice, col_slice]
-
-
-def shard_half(ref, w, part):
-    size = (96, 96, 192, 384)[w]
-    if w == 0:
-        return ref.at[:, pl.ds(part * size, size)]
-    return ref.at[pl.ds(part * size, size)]
-
-
-def remote(src, dst, dest, send_sem, recv_sem):
-    return pltpu.make_async_remote_copy(
-        src_ref=src, dst_ref=dst, send_sem=send_sem, recv_sem=recv_sem, device_id=dest, device_id_type=MESH
-    )
-
-
-class Gather:
-    def __init__(self, shards, wholes, me, ss, rs, ls):
-        self.shards, self.wholes = shards, wholes
-        self.ss, self.rs, self.ls = ss, rs, ls
-        f, c, t = me
-        y = (t + 2) % 4
-        s = t + 1 - 2 * (t % 2)
-        self.me = me
-        self.other_f, self.other_y, self.other_s = 1 - f, y, s
-        self.to_x, self.to_y, self.to_s = (1 - f, c, t), (f, c, y), (f, c, s)
-
-    def copy(self, w, k):
-        f, _, t = self.me
-        g, y = self.other_f, self.other_y
-        whole = self.wholes[w]
-        own = self.shards[w]
-        if k < 3:
-            src, dst = own, block(whole, w, t, f)
-            dest = (self.to_x, self.to_y, self.to_s)[k]
-        elif k == 3:
-            src = dst = block(whole, w, t, g, 0)
-            dest = self.to_y
-        elif k == 4:
-            src = dst = block(whole, w, y, f, 1)
-            dest = self.to_x
-        elif k == 5:
-            src = dst = block(whole, w, t, g)
-            dest = self.to_s
-        elif k == 6:
-            src = dst = block(whole, w, y, f)
-            dest = self.to_s
-        else:
-            src = dst = block(whole, w, y, g, k - 7)
-            dest = self.to_s
-        return remote(src, dst, dest, self.ss.at[w, k], self.rs.at[w, k])
-
-    def landed(self, w, k):
-        f, _, t = self.me
-        g, y, s = self.other_f, self.other_y, self.other_s
-        sy = (s + 2) % 4
-        whole = self.wholes[w]
-        place = (
-            (t, g, None), (y, f, None), (s, f, None),
-            (y, g, 0), (y, g, 1),
-            (s, g, None), (sy, f, None), (sy, g, 0), (sy, g, 1),
-        )[k]
-        return block(whole, w, *place)
-
-    def wait_recv(self, w, k):
-        dst = self.landed(w, k)
-        pltpu.make_async_copy(dst, dst, self.rs.at[w, k]).wait()
-
-    def wait_send(self, w, k):
-        src = self.landed(w, k)
-        pltpu.make_async_copy(src, src, self.ss.at[w, k]).wait()
-
-    def start_own(self, w):
-        f, _, t = self.me
-        for k in range(3):
-            self.copy(w, k).start()
-        pltpu.make_async_copy(self.shards[w], block(self.wholes[w], w, t, f), self.ls.at[w]).start()
-
-    def forward_first(self, w):
-        self.wait_recv(w, 0)
-        self.copy(w, 3).start()
-        self.copy(w, 5).start()
-        self.wait_recv(w, 1)
-        self.copy(w, 4).start()
-        self.copy(w, 6).start()
-
-    def forward_second(self, w):
-        self.wait_recv(w, 3)
-        self.copy(w, 7).start()
-        self.wait_recv(w, 4)
-        self.copy(w, 8).start()
-
-    def finish(self, w):
-        f, _, t = self.me
-        for k in (2, 5, 6, 7, 8):
-            self.wait_recv(w, k)
-        for k in range(9):
-            self.wait_send(w, k)
-        pltpu.make_async_copy(self.shards[w], block(self.wholes[w], w, t, f), self.ls.at[w]).wait()
-
-
-def gather_kernel(images, with_weights, *refs):
-    if with_weights:
-        x_ref, c_ref, wq, wp, wu, wd, xw, cw, gq, gp, gu, gd, stage, ss, rs, gss, grs, gls = refs
-    else:
-        x_ref, c_ref, xw, cw, stage, ss, rs = refs
-    me = coords()
-    f, ctx, tp = me
-    extra = ((1 - f, ctx, tp),) if with_weights else ()
-    group_barrier(extra)
-    pack = pack_matrix()
-    if with_weights:
-        gather = Gather((wq, wp, wu, wd), (gq, gp, gu, gd), me, gss, grs, gls)
-    for a, (src, out) in enumerate(((x_ref, xw), (c_ref, cw))):
-        for i in range(images):
-            for u in range(2):
-                stage[a, i, u] = jnp.dot(
-                    pack, src[i, pl.ds(u * 128, 128)], preferred_element_type=F32
-                ).astype(BF)
-        start_pieces(stage, out, a, images, me, ss, rs)
-        if with_weights and a == 0:
-            for w in range(4):
-                gather.start_own(w)
-    if with_weights:
-        for w in range(4):
-            gather.forward_first(w)
-        for w in range(4):
-            gather.forward_second(w)
-    for a, out in enumerate((xw, cw)):
-        wait_pieces(out, a, me, rs)
-        finish_piece_sends(stage, a, images, me, ss)
-    if with_weights:
-        for w in range(4):
-            gather.finish(w)
-
-
-def gather_in(x3, c3, shards):
-    images = x3.shape[0]
-    any_spec = pl.BlockSpec(memory_space=pl.ANY)
-    vmem = pl.BlockSpec(memory_space=pltpu.VMEM)
-    with_weights = shards is not None
-    token_shape = jax.ShapeDtypeStruct((ROWS, D), BF)
-    out_shape = [token_shape, token_shape]
-    scratch = [
-        pltpu.VMEM((2, images, 2, PIECE, D), BF),
-        pltpu.SemaphoreType.DMA((2, images * 10)),
-        pltpu.SemaphoreType.DMA((2, NFULL + NPART, PAIRS)),
-    ]
-    args = [x3, c3]
-    if with_weights:
-        args += list(shards)
-        out_shape += [
-            jax.ShapeDtypeStruct(s, BF) for s in ((3, D, D), (D, D), (D, 4 * D), (4 * D, D))
-        ]
-        scratch += [pltpu.SemaphoreType.DMA((4, 9)), pltpu.SemaphoreType.DMA((4, 9)), pltpu.SemaphoreType.DMA((4,))]
-    return pl.pallas_call(
-        functools.partial(gather_kernel, images, with_weights),
-        out_shape=out_shape,
-        in_specs=[vmem, vmem] + [any_spec] * (len(args) - 2),
-        out_specs=[any_spec] * len(out_shape),
-        scratch_shapes=scratch,
-        compiler_params=pltpu.CompilerParams(
-            collective_id=0, has_side_effects=True, vmem_limit_bytes=VMEM_LIMIT
-        ),
-        name="tokens_and_weights_in",
-    )(*args)
-
-
-STEP_ROWS = (576, 192, 768, 768)
 
 
 def add_rows(dst, src, rows, cols):
@@ -450,7 +628,7 @@
             for n, t_there in enumerate((s, sy)):
                 for h in range(2):
                     first[w, n, h] = send(
-                        block(grads[w], w, t_there, h), r1[w].at[n, h], to_s, s1.at[w, n, h], v1.at[w, n, h]
+                        grad_block(grads[w], w, t_there, h), r1[w].at[n, h], to_s, s1.at[w, n, h], v1.at[w, n, h]
                     )
         few = few_start(0)
 
@@ -459,27 +637,27 @@
             for n, t_here in enumerate((tp, y)):
                 for h in range(2):
                     first[w, n, h].wait_recv()
-                    add_view(block(grads[w], w, t_here, h), r1[w].at[n, h], w)
+                    add_view(grad_block(grads[w], w, t_here, h), r1[w].at[n, h], w)
             phase1[w] = (
-                send(block(grads[w], w, tp, g, 0), ra[w].at[0], to_x, s2.at[w, 0], v2.at[w, 0]),
-                send(block(grads[w], w, y, g, 0), ra[w].at[1], to_x, s2.at[w, 1], v2.at[w, 1]),
-                send(block(grads[w], w, y, f, 1), ra[w].at[2], to_y, s2.at[w, 2], v2.at[w, 2]),
-                send(block(grads[w], w, y, g, 1), ra[w].at[3], to_y, s2.at[w, 3], v2.at[w, 3]),
+                send(grad_block(grads[w], w, tp, g, 0), ra[w].at[0], to_x, s2.at[w, 0], v2.at[w, 0]),
+                send(grad_block(grads[w], w, y, g, 0), ra[w].at[1], to_x, s2.at[w, 1], v2.at[w, 1]),
+                send(grad_block(grads[w], w, y, f, 1), ra[w].at[2], to_y, s2.at[w, 2], v2.at[w, 2]),
+                send(grad_block(grads[w], w, y, g, 1), ra[w].at[3], to_y, s2.at[w, 3], v2.at[w, 3]),
             )
         few_finish(few, 0)
         few = few_start(1)
         phase2 = {}
         for w in order:
             views = (
-                block(grads[w], w, tp, f, 0), block(grads[w], w, y, f, 0),
-                block(grads[w], w, tp, f, 1), block(grads[w], w, tp, g, 1),
+                grad_block(grads[w], w, tp, f, 0), grad_block(grads[w], w, y, f, 0),
+                grad_block(grads[w], w, tp, f, 1), grad_block(grads[w], w, tp, g, 1),
             )
             for k in range(4):
                 phase1[w][k].wait_recv()
                 add_view(views[k], ra[w].at[k], w)
             phase2[w] = (
-                send(block(grads[w], w, y, f, 0), ra[w].at[4], to_y, s2.at[w, 4], v2.at[w, 4]),
-                send(block(grads[w], w, tp, g, 1), ra[w].at[5], to_x, s2.at[w, 5], v2.at[w, 5]),
+                send(grad_block(grads[w], w, y, f, 0), ra[w].at[4], to_y, s2.at[w, 4], v2.at[w, 4]),
+                send(grad_block(grads[w], w, tp, g, 1), ra[w].at[5], to_x, s2.at[w, 5], v2.at[w, 5]),
             )
         few_finish(few, 1)
         few = few_start(2)
@@ -492,14 +670,14 @@
         for w in order:
             for k in range(2):
                 phase2[w][k].wait_recv()
-                add_view(block(grads[w], w, tp, f, k), ra[w].at[4 + k], w)
-            mine = block(grads[w], w, tp, f)
+                add_view(grad_block(grads[w], w, tp, f, k), ra[w].at[4 + k], w)
+            mine = grad_block(grads[w], w, tp, f)
 
             @pl.when(outer)
             def _(w=w, mine=mine):
                 remote(mine, rz[w].at[0], in_peer, s3.at[w, 0], v3.at[w, 0]).start()
         for w in order:
-            mine = block(grads[w], w, tp, f)
+            mine = grad_block(grads[w], w, tp, f)
 
             @pl.when(inner)
             def _(w=w, mine=mine):
@@ -507,7 +685,7 @@
                 add_view(mine, rz[w].at[0], w)
                 remote(mine, rz[w].at[1], mid_peer, s3.at[w, 0], v3.at[w, 1]).start()
         for w in order:
-            mine = block(grads[w], w, tp, f)
+            mine = grad_block(grads[w], w, tp, f)
 
             @pl.when(inner)
             def _(w=w, mine=mine):
@@ -627,7 +805,7 @@
     return jnp.concatenate([part, jnp.broadcast_to(fill, (FULL - rows, 128)).astype(BF)], axis=0)
 
 
-def attention_slot(qkv, rel_cols, bias_v, e_at, o_ref, p_ref, p_at, base, rows, narrow, x_scr):
+def attention_slot(qkv, rel_cols, bias_v, e_at, o_ref, p_ref, base, rows, narrow, x_scr):
     a_row, b_row = row_places(rows, narrow)
     q_all = qkv[pl.ds(base, rows), pl.ds(0, D)]
     lane = lax.broadcasted_iota(jnp.int32, (rows, 128), 1) % SEG
@@ -652,7 +830,7 @@
             s = nt(q, k * (half_mask(hh) * 0.125)) + nt(x, e_at[h % 4])
             p = jnp.exp(s - jnp.max(s, axis=-1, keepdims=True))
             p = (p * (1.0 / jnp.sum(p, axis=-1, keepdims=True))).astype(BF)
-            p_ref[p_at * HEADS + h] = p
+            p_ref[pl.ds(base, rows), pl.ds(h * 256, FULL)] = p
             out = out + jnp.dot(p, v * half_mask(hh), preferred_element_type=F32)
         o_ref[pl.ds(base, rows), pl.ds(hp * 128, 128)] = out.astype(BF)
 
@@ -664,36 +842,7 @@
     return jnp.where(is_narrow, 1, 0)
 
 
-def attention_kernel(qkv, rel_cols, bias_v, e_ref, o_ref, pf_ref, pp_ref, x_scr):
-    @pl.loop(0, NFULL)
-    def _(n):
-        attention_slot(qkv, rel_cols, bias_v, e_ref.at[0], o_ref, pf_ref, n,
-                       pl.multiple_of(n * FULL, 16), FULL, None, x_scr)
-
-    @pl.loop(0, NPART)
-    def _(n):
-        attention_slot(qkv, rel_cols, bias_v, e_ref.at[1 + n], o_ref, pp_ref, n,
-                       pl.multiple_of(PBASE + n * PART, 16), PART, narrow_flag(n), x_scr)
-
-
-def attention(qkv, rel_cols, bias_v, e):
-    vmem = pl.BlockSpec(memory_space=pltpu.VMEM)
-    return pl.pallas_call(
-        attention_kernel,
-        out_shape=[
-            jax.ShapeDtypeStruct((ROWS, D), BF),
-            jax.ShapeDtypeStruct((NFULL * HEADS, FULL, FULL), BF),
-            jax.ShapeDtypeStruct((NPART * HEADS, PART, FULL), BF),
-        ],
-        in_specs=[vmem] * 4,
-        out_specs=[vmem] * 3,
-        scratch_shapes=[pltpu.VMEM((FULL, GROUPS * 256), BF)],
-        compiler_params=pltpu.CompilerParams(vmem_limit_bytes=VMEM_LIMIT),
-        name="attention_forward",
-    )(qkv, rel_cols, bias_v, e)
-
-
-def attention_back_slot(qkv, do_ref, rel_cols, bias_v, e_at, p_ref, p_at, dqkv, d_scr, acc_scr, pad_acc,
+def attention_back_slot(qkv, do_ref, rel_cols, bias_v, e_at, p_ref, dqkv, d_scr, acc_scr, pad_acc,
                         rel_acc, base, rows, narrow):
     a_row, b_row = row_places(rows, narrow)
     for g in range(GROUPS):
@@ -711,7 +860,7 @@
                 mask = half_mask(hh)
                 do_m = do * mask
                 dp = nt(do_m, v)
-                p_low = p_ref[p_at * HEADS + h]
+                p_low = p_ref[pl.ds(base, rows), pl.ds(h * 256, FULL)]
                 t = p_low.astype(F32)
                 tp = t * dp
                 ds = (tp - t * jnp.sum(tp, axis=-1, keepdims=True)).astype(BF)
@@ -736,19 +885,19 @@
     rel_acc[...] += tn(d, q_all)
 
 
-def attention_back_kernel(qkv, do_ref, rel_cols, bias_v, e_ref, pf_ref, pp_ref, dqkv, pad_ref, rel_ref,
+def attention_back_kernel(qkv, do_ref, rel_cols, bias_v, e_ref, p_ref, dqkv, pad_ref, rel_ref,
                           d_scr, acc_scr, rel_acc):
     pad_ref[...] = jnp.zeros_like(pad_ref)
     rel_acc[...] = jnp.zeros_like(rel_acc)
 
     @pl.loop(0, NFULL)
     def _(n):
-        attention_back_slot(qkv, do_ref, rel_cols, bias_v, e_ref.at[0], pf_ref, n, dqkv, d_scr, acc_scr, pad_ref,
+        attention_back_slot(qkv, do_ref, rel_cols, bias_v, e_ref.at[0], p_ref, dqkv, d_scr, acc_scr, pad_ref,
                             rel_acc, pl.multiple_of(n * FULL, 16), FULL, None)
 
     @pl.loop(0, NPART)
     def _(n):
-        attention_back_slot(qkv, do_ref, rel_cols, bias_v, e_ref.at[1 + n], pp_ref, n, dqkv, d_scr, acc_scr, pad_ref,
+        attention_back_slot(qkv, do_ref, rel_cols, bias_v, e_ref.at[1 + n], p_ref, dqkv, d_scr, acc_scr, pad_ref,
                             rel_acc, pl.multiple_of(PBASE + n * PART, 16), PART, narrow_flag(n))
 
     lane = lax.broadcasted_iota(jnp.int32, (SEG, D), 1) // HEAD_DIM
@@ -759,7 +908,7 @@
         rel_ref[axis] = total
 
 
-def attention_back(qkv, do, rel_cols, bias_v, e, pf, pp):
+def attention_back(qkv, do, rel_cols, bias_v, e, p):
     vmem = pl.BlockSpec(memory_space=pltpu.VMEM)
     return pl.pallas_call(
         attention_back_kernel,
@@ -768,7 +917,7 @@
             jax.ShapeDtypeStruct((1, D), F32),
             jax.ShapeDtypeStruct((2, SEG, D), F32),
         ],
-        in_specs=[vmem] * 7,
+        in_specs=[vmem] * 6,
         out_specs=[vmem] * 3,
         scratch_shapes=[
             pltpu.VMEM((FULL, D), BF),
@@ -777,15 +926,13 @@
         ],
         compiler_params=pltpu.CompilerParams(vmem_limit_bytes=VMEM_LIMIT),
         name="attention_backward",
-    )(qkv, do, rel_cols, bias_v, e, pf, pp)
-
-
-def slot_tables():
+    )(qkv, do, rel_cols, bias_v, e, p)
+
+
+def real_rows():
     _, ctx, tp = coords()
     r = jnp.arange(FULL)
-    full_real = (r % 16) < WIN
-    real = [full_real] * NFULL
-    keys = [(r // 16, r % 16, full_real)]
+    real = [(r % 16) < WIN] * NFULL
     for k in range(NPART):
         q = (3 - ctx) * 8 + tp * 2 + k
         bottom = q < 15
@@ -795,34 +942,7 @@
         real.append(
             jnp.where(corner, rp < 64, jnp.where(right, rp < 112, bottom & (rp % 16 < WIN)))
         )
-        a_right = jnp.where(r < 112, r // 8, (r - 112) // 8)
-        b_right = jnp.where(r < 112, r % 8, 8 + (r - 112) % 8)
-        a_corner = jnp.where(r < 64, r // 8, jnp.where(r < 128, (r - 64) // 8, 8 + (r - 128) // 16))
-        b_corner = jnp.where(r < 64, r % 8, jnp.where(r < 128, 8 + (r - 64) % 8, (r - 128) % 16))
-        a = jnp.where(corner, a_corner, jnp.where(right, a_right, r // 16))
-        b = jnp.where(corner, b_corner, jnp.where(right, b_right, r % 16))
-        keys.append((a, b, b < WIN))
-    a = jnp.stack([x[0] for x in keys])[:, None, :, None]
-    b = jnp.stack([x[1] for x in keys])[:, None, :, None]
-    ok = jnp.stack([x[2] for x in keys])[:, None, :, None]
-    col = jnp.arange(256)[None, None, None, :]
-    head = jnp.arange(4)[None, :, None, None]
-    mine = ((col % 128) // SEG) == head
-    j = col % 16
-    pos = jnp.where(col < 128, a, b)
-    one = (mine & ok & (j == pos) & (j < WIN)).astype(F32)
-    out = (mine & jnp.logical_not(ok) & (col < 128) & (col % SEG == 15)).astype(F32) * MASKED
-    return jnp.concatenate(real)[:, None], (one + out).astype(BF)
-
-
-def relative_columns(rel_h, rel_w):
-    parts = []
-    eye = jnp.eye(HEADS, dtype=BF)
-    for rel in (rel_h, rel_w):
-        rev = jnp.pad(rel[::-1], ((0, SEG - rel.shape[0]), (0, 0))).T
-        wide = eye[:, None, :, None] * rev[None, :, None, :]
-        parts.append(wide.reshape(D, HEADS * SEG))
-    return jnp.concatenate(parts, axis=1)
+    return jnp.concatenate(real)[:, None]
 
 
 def norm_stats(v):
@@ -876,24 +996,20 @@
     x3 = jnp.transpose(block_input, (1, 0, 2))
     c3 = jnp.transpose(cotangent, (1, 0, 2))
     shards = (jnp.transpose(w_qkv, (0, 2, 1)), w_proj, w_up, w_down)
+    zero = jnp.zeros_like(ln1_gain)
+    bias_row = jnp.concatenate([qkv_bias[0], zero, qkv_bias[1]])
+    vec = jnp.stack([jnp.tile(ln1_gain, 3), jnp.tile(ln1_bias, 3), bias_row]).astype(F32)
+    rel = jnp.pad(jnp.stack([rel_h, rel_w]), ((0, 0), (0, SEG - rel_h.shape[0]), (0, 0)))
     if direct:
-        xw, cw, wq, wp, wu, wd = gather_in(x3, c3, shards)
+        x_low, cot_low, n1, qkv, attended, probs, wq, wp, wu, wd, e, rel_cols = forward(x3, c3, shards, None, vec, rel)
     else:
-        xw, cw = gather_in(x3, c3, None)
         wq, wp, wu, wd = whole_weights(shards)
+        x_low, cot_low, n1, qkv, attended, probs, e, rel_cols = forward(x3, c3, None, wq, vec, rel)
     wq = wq.reshape(3 * D, D)
-    real, e = slot_tables()
-    rel_cols = relative_columns(rel_h, rel_w)
-    g1, b1, g2, b2 = (v.astype(F32) for v in (ln1_gain, ln1_bias, ln2_gain, ln2_bias))
-    x = jnp.where(real, xw, 0).astype(F32)
-    cot_low = jnp.where(real, cw, 0)
-    cot = cot_low.astype(F32)
-    bias_three = jnp.concatenate([qkv_bias[0], jnp.zeros_like(qkv_bias[0]), qkv_bias[1]]).astype(F32)
-
+    real = real_rows()
+    g1, g2, b2 = (v.astype(F32) for v in (ln1_gain, ln2_gain, ln2_bias))
+    x, cot = x_low.astype(F32), cot_low.astype(F32)
     xhat1, r1 = norm_stats(x)
-    n1 = jnp.where(real, xhat1 * g1 + b1, 0.0).astype(BF)
-    qkv = (mm(n1, wq, "mk,nk->mn") + bias_three).astype(BF)
-    attended, pf, pp = attention(qkv, rel_cols, qkv_bias[1:2], e)
     middle = x + mm(attended, wp) + proj_bias.astype(F32)
     xhat2, r2 = norm_stats(middle)
     n2 = (xhat2 * g2 + b2).astype(BF)
@@ -915,7 +1031,7 @@
     d_proj_bias = jnp.sum(branch, axis=0, dtype=F32)
     d_wp = mm(attended, branch, "km,kn->mn").astype(BF)
     d_att = mm(branch, wp, "mk,nk->mn").astype(BF)
-    dqkv, d_pad, d_rel = attention_back(qkv, d_att, rel_cols, qkv_bias[1:2], e, pf, pp)
+    dqkv, d_pad, d_rel = attention_back(qkv, d_att, rel_cols, qkv_bias[1:2].astype(F32), e, probs)
     d_wq = mm(dqkv, n1, "km,kn->mn").astype(BF).reshape(3, D, D)
     sums = jnp.sum(dqkv, axis=0, dtype=F32)
     d_n1 = mm(dqkv, wq)

time: 477 us -> 424 us (0.89)
  Pallas kernels: 338 us -> 304 us
  local copies, waits for them, and re-layouts: 22.3 us -> 14.4 us
  other arithmetic: 18.7 us -> 12.2 us
  matrix products: 92.6 us -> 87.6 us
    pallas_call x2 -> x1, Pallas kernels: 130 us -> 96.1 us  [forward(): pl.pallas_call(functools.partial(forward_kernel, images, direct), out_sha...]
    mul x4 -> x0, local copies, waits for them, and re-layouts: 7.93 us -> none  [relative_columns(): wide = eye[:, None, :, None] * rev[None, :, None, :]]
    dot_general x12 -> x11, matrix products: 92.6 us -> 87.6 us  [mm(): return jnp.einsum(dims, a, b, preferred_element_type=F32)]
where the time goes in v2:
time: 424 us; the launch traced here: 420 us
  Pallas kernels  304 us (72%)
  matrix products  87.6 us (21%)
  local copies, waits for them, and re-layouts  14.4 us (3%)
  other arithmetic  12.2 us (3%)
    pallas_call x1, Pallas kernels, send_back(): pl.pallas_call(functools.partial(reduce_kernel, images, with_weights), ou...  178 us
    pallas_call x1, Pallas kernels, forward(): pl.pallas_call(functools.partial(forward_kernel, images, direct), out_sha...  96.1 us
    dot_general x11, matrix products, mm(): return jnp.einsum(dims, a, b, preferred_element_type=F32)  87.6 us
    pallas_call x1, Pallas kernels, attention_back(): pl.pallas_call(attention_back_kernel, out_shape=[jax.ShapeDtypeStruct((RO...  29.5 us

profile of v2, /device:TPU:14, one launch (start us, length us, event | category | flops | bytes accessed | tf_op | source)
XLA Modules:
  0.0 419.7 jit_solution(15278525180989371970)
XLA Ops:
  0.6 0.0 copy-start
  0.7 1.3 slice_reduce_fusion
  2.1 0.7 broadcast_bitcast_fusion.1
  2.8 0.7 maximum_convert_fusion.refs_6_
  3.4 1.3 fusion.23.refs_7_
  4.8 96.1 %forward_attention.1 = (bf16[928,768]{1,0:T(8,128)(2,1)}, bf16[928,768]{1,0:T(8,128)(2,1)}, bf16[928,768]{1,0:T(8,128)(2,1)}, bf16[928,2304]{1,0:T(8,128)(2,1)},...) custom-call(bf16[3,256,768]{2,1,0:T(8,128)(2,1)} %bitcast.70, ...), custom_call_target="tpu_custom_call" | custom-call | tf_op jit(solution)/shard_map/forward_attention/pallas_call | solution.py:512
  100.9 0.0 copy-done.17
  100.9 0.0 slice-start.4
  100.9 0.0 slice-start.5
  100.9 3.7 fusion.30
  104.6 0.0 copy-start.18
  104.6 0.0 copy-start.15
  104.6 0.0 copy-start.19
  104.7 0.0 slice-start
  104.7 0.5 multiply_reduce_fusion.2
  105.1 0.2 copy-done.18
  105.3 0.0 copy-done.15
  105.4 0.0 copy-done.19
  105.4 0.0 slice-start.1
  105.5 15.7 %multiply_convert_fusion = (bf16[928,3072]{1,0:T(8,128)(2,1)}, f32[928,3072]{1,0:T(8,128)}) fusion(f32[3072]{0:T(1024)S(1)} %convert_element_type.82, bf16[768,3072]{1,0:T(8,128)(2,1)S(1)} %bitcast.88, f32[928,768]{1,0:T(8,128)S(1)} %get-tuple-element.87, f32[768]{0:T(1024)S(1)} %convert_element_type.80, f32[768]{0:T(1024)S(1)} %convert_element_type.79, ...), kind=kOutput, calls=%fused_computation.10 | convolution fusion | flops 4447985664 | bytes 24700160 | tf_op jit(solution)/shard_map/mk,kn->mn/dot_general | solution.py:971
  121.2 14.9 %convert_reduce_fusion = (f32[3072]{0:T(1024)S(1)}, bf16[928,3072]{1,0:T(8,128)(2,1)S(1)}) fusion(f32[928,3072]{1,0:T(8,128)} %get-tuple-element.89, f32[3072]{0:T(1024)S(1)} %convert_element_type.82, bf16[928,768]{1,0:T(8,128)(2,1)S(1)} %copy-done.8, bf16[3072,768]{1,0:T(8,128)(2,1)S(1)} %bitcast.84), kind=kOutput, calls=%fused_computation.9 | convolution fusion | flops 4458673152 | bytes 23273472 | tf_op jit(solution)/shard_map/mk,nk->mn/dot_general | solution.py:971
  136.1 5.3 %multiply_reduce_fusion = (f32[768]{0:T(1024)S(1)}, f32[928]{0:T(1024)S(1)}, f32[928]{0:T(1024)S(1)}, f32[768]{0:T(1024)S(1)}, f32[928,768]{1,0:T(8,128)S(1)}) fusion(f32[928,768]{1,0:T(8,128)S(1)} %get-tuple-element.87, f32[928]{0:T(1024)S(1)} %add_rsqrt_fusion.1, f32[928]{0:T(1024)S(1)} %broadcast_multiply_fusion.5, f32[768]{0:T(1024)S(1)} %convert_element_type.79, ...), kind=kOutput, calls=%fused_computation.34 | convolution fusion | flops 4385263616 | bytes 16145920 | tf_op jit(solution)/shard_map/mk,nk->mn/dot_general | solution.py:971
  141.5 0.0 copy-done.3
  141.5 0.0 copy-start.23
  141.5 1.9 convert_reduce_fusion.4
  143.4 0.0 copy-start.5
  143.4 0.0 copy-done.23
  143.4 2.5 convolution_convert_fusion.3.do_ref
  145.8 29.5 %attention_backward.1 = (bf16[928,2304]{1,0:T(8,128)(2,1)}, f32[1,768]{1,0:T(1,128)}, f32[2,32,768]{2,1,0:T(8,128)}) custom-call(bf16[928,2304]{1,0:T(8,128)(2,1)} %get-tuple-element.44.qkv, bf16[928,768]{1,0:T(8,128)(2,1)} %convolution_convert_fusion.3.do_ref, bf16[768,768]{1,0:T(8,128)(2,1)} %get-tuple-element.45.rel_cols, ...), custom_call_target="tpu_custom_call" | custom-call | tf_op jit(solution)/shard_map/attention_backward/pallas_call | solution.py:913
  175.3 0.1 concatenate.10
  175.4 0.0 copy-done.2
  175.4 0.3 convert_reduce_fusion.2
  175.7 0.6 fusion.19
  176.3 0.0 copy-done.14
  176.3 8.8 %fusion.18 = (f32[768]{0:T(1024)S(1)}, f32[928]{0:T(1024)S(1)}, f32[928]{0:T(1024)S(1)}, f32[768]{0:T(1024)S(1)}, f32[928,768]{1,0:T(8,128)}) fusion(bf16[928,768]{1,0:T(8,128)(2,1)S(1)} %copy-done.2, f32[928]{0:T(1024)S(1)} %add_rsqrt_fusion, f32[928]{0:T(1024)S(1)} %broadcast_multiply_fusion.2, pred[928]{0:T(1024)(128)(4,1)S(1)} %concatenate.10, ...), kind=kOutput, calls=%fused_computation.31 | convolution fusion | flops 3292688896 | bytes 12116384 | tf_op jit(solution)/shard_map/mk,kn->mn/dot_general | solution.py:971
  185.2 2.9 convert_reduce_fusion.1
  188.0 0.0 copy-done.16
  188.1 1.0 reshape.115
  189.1 0.1 reduce_sum.164
  189.3 0.1 reshape.116
  189.4 0.6 pad_bitcast_fusion.refs_6_
  190.0 9.7 %convolution_convert_fusion.refs_5_ = bf16[3072,768]{1,0:T(8,128)(2,1)} fusion(bf16[928,3072]{1,0:T(8,128)(2,1)} %get-tuple-element.88, bf16[928,768]{1,0:T(8,128)(2,1)S(1)} %copy-done.8), kind=kOutput, calls=%fused_computation.12 | convolution fusion | flops 4381212672 | bytes 11845632 | tf_op jit(solution)/shard_map/km,kn->mn/dot_general | solution.py:971
  199.8 9.9 %convolution_convert_fusion.1.refs_4_ = bf16[768,3072]{1,0:T(8,128)(2,1)} fusion(bf16[928,3072]{1,0:T(8,128)(2,1)} %copy-done.24, f32[928,768]{1,0:T(8,128)S(1)} %copy-done.4, f32[768]{0:T(1024)S(1)} %convert_element_type.80, f32[768]{0:T(1024)S(1)} %convert_element_type.79, f32[928]{0:T(1024)S(1)} %add_rsqrt_fusion.1, f32[928]{0:T(1024)S(1)} %broadcast_multiply_fusion.5), kind=kOutput, calls=%fused_computation.13 | convolution fusion | flops 4384776192 | bytes 13284608 | tf_op jit(solution)/shard_map/km,kn->mn/dot_general | solution.py:971
  209.7 0.0 copy-done.6
  209.7 0.0 slice-start.2
  209.7 0.0 slice-start.6
  209.7 2.5 convolution_convert_fusion.4.refs_3_
  212.2 8.9 %convolution_convert_fusion.2 = bf16[2304,768]{1,0:T(8,128)(2,1)} fusion(bf16[928,2304]{1,0:T(8,128)(2,1)} %get-tuple-element.48, bf16[928,768]{1,0:T(8,128)(2,1)S(1)} %copy-done.21), kind=kOutput, calls=%fused_computation.14 | convolution fusion | flops 3285909504 | bytes 9240576 | tf_op jit(solution)/shard_map/km,kn->mn/dot_general | solution.py:971
  221.1 0.0 copy-start.20
  221.1 2.1 fusion.16.refs_1_
  223.3 5.7 %add_convert_fusion.refs_0_ = bf16[928,768]{1,0:T(8,128)(2,1)} fusion(f32[928,768]{1,0:T(8,128)S(1)} %copy-done.4, bf16[928,3072]{1,0:T(8,128)(2,1)S(1)} %bitcast.91, bf16[3072,768]{1,0:T(8,128)(2,1)S(1)} %bitcast.86, f32[768]{0:T(1024)S(1)} %convert_element_type.84), kind=kOutput, calls=%fused_computation.38 | convolution fusion | flops 4380991488 | bytes 14699520 | tf_op jit(solution)/shard_map/mk,kn->mn/dot_general | solution.py:971
  228.9 178.5 %tokens_and_gradients_out.1 = (bf16[3,256,768]{2,1,0:T(8,128)(2,1)}, bf16[3,256,768]{2,1,0:T(8,128)(2,1)}, f32[3,192,384]{2,1,0:T(8,128)}, f32[192,384]{1,0:T(8,...) custom-call(bf16[928,768]{1,0:T(8,128)(2,1)} %add_convert_fusion.refs_0_, ...), custom_call_target="tpu_custom_call" | custom-call | tf_op jit(solution)/shard_map/tokens_and_gradients_out/pallas_call | solution.py:759
  407.4 1.5 slice_bitcast_fusion.3
  409.0 0.6 pad_maximum_fusion.1
  409.6 0.7 slice.102
  410.3 0.1 reshape.118
  410.4 0.6 slice_bitcast_fusion
  411.0 1.3 slice_bitcast_fusion.2
  412.3 2.4 copy.56
  414.7 1.0 copy.57
  415.8 0.9 copy.58
  416.7 0.7 copy.59
  417.4 1.0 copy.60
  418.4 1.0 copy.61
  (84 shorter events, 0.3 us)
Async XLA Ops:
  0.6 2.1 copy-start
  0.7 100.2 %copy-start.17 = (bf16[768]{0:T(1024)(128)(2,1)S(1)}, bf16[768]{0:T(1024)(128)(2,1)}, u32[]{:S(2)}) copy-start(bf16[768]{0:T(1024)(128)(2,1)} %param.24) | copy-start | bytes 4612
  100.9 4.6 %slice-start.4 = ((s8[4718592]{0:T(1024)(128)(4,1)}), s8[4194304]{0:T(1024)(128)(4,1)S(1)}, s32[]{:S(2)}) async-start(s8[4718592]{0:T(1024)(128)(4,1)} %bitcast.87), calls=%async_computation.4 | async-start | bytes 8388608
  100.9 4.5 %slice-start.5 = ((s8[4718592]{0:T(1024)(128)(4,1)}), s8[524288]{0:T(1024)(128)(4,1)S(1)}, s32[]{:S(2)}) async-start(s8[4718592]{0:T(1024)(128)(4,1)} %bitcast.87), calls=%async_computation.5 | async-start | bytes 1048576
  104.6 36.9 %copy-start.3 = (f32[928,768]{1,0:T(8,128)}, f32[928,768]{1,0:T(8,128)S(1)}, u32[]{:S(2)}) copy-start(f32[928,768]{1,0:T(8,128)S(1)} %get-tuple-element.87) | copy-start | bytes 8552452
  104.6 0.7 copy-start.18
  104.6 0.7 copy-start.15
  104.6 0.8 copy-start.19
  104.7 16.5 %slice-start = ((s8[4718592]{0:T(1024)(128)(4,1)}), s8[524288]{0:T(1024)(128)(4,1)S(1)}, s32[]{:S(2)}) async-start(s8[4718592]{0:T(1024)(128)(4,1)} %bitcast.83), calls=%async_computation | async-start | bytes 1048576
  105.4 15.8 %copy-start.8 = (bf16[928,768]{1,0:T(8,128)(2,1)S(1)}, bf16[928,768]{1,0:T(8,128)(2,1)}, u32[]{:S(2)}) copy-start(bf16[928,768]{1,0:T(8,128)(2,1)} %get-tuple-element.43) | copy-start | bytes 4276228
  105.4 15.8 %slice-start.1 = ((s8[4718592]{0:T(1024)(128)(4,1)}), s8[4194304]{0:T(1024)(128)(4,1)S(1)}, s32[]{:S(2)}) async-start(s8[4718592]{0:T(1024)(128)(4,1)} %bitcast.83), calls=%async_computation.1 | async-start | bytes 8388608
  136.1 5.3 %copy-start.24 = (bf16[928,3072]{1,0:T(8,128)(2,1)}, bf16[928,3072]{1,0:T(8,128)(2,1)S(1)}, u32[]{:S(2)}) copy-start(bf16[928,3072]{1,0:T(8,128)(2,1)S(1)} %get-tuple-element.93) | copy-start | bytes 17104900
  141.5 1.9 copy-start.23
  143.4 2.5 copy-start.5
  145.8 29.6 %copy-start.2 = (bf16[928,768]{1,0:T(8,128)(2,1)S(1)}, bf16[928,768]{1,0:T(8,128)(2,1)}, u32[]{:S(2)}) copy-start(bf16[928,768]{1,0:T(8,128)(2,1)} %get-tuple-element.38) | copy-start | bytes 4276228
  175.3 1.0 copy-start.14
  185.2 2.9 copy-start.16
  190.0 9.8 %copy-start.4 = (f32[928,768]{1,0:T(8,128)S(1)}, f32[928,768]{1,0:T(8,128)}, u32[]{:S(2)}) copy-start(f32[928,768]{1,0:T(8,128)} %copy-done.3) | copy-start | bytes 8552452
  199.8 9.9 %copy-start.6 = (f32[928,768]{1,0:T(8,128)S(1)}, f32[928,768]{1,0:T(8,128)}, u32[]{:S(2)}) copy-start(f32[928,768]{1,0:T(8,128)} %copy-done.5) | copy-start | bytes 8552452
  199.8 9.9 %copy-start.22 = (bf16[928,768]{1,0:T(8,128)(2,1)S(1)}, bf16[928,768]{1,0:T(8,128)(2,1)}, u32[]{:S(2)}) copy-start(bf16[928,768]{1,0:T(8,128)(2,1)} %get-tuple-element.39) | copy-start | bytes 4276228
  209.7 2.5 copy-start.21
  209.7 13.5 %slice-start.2 = ((s8[4718592]{0:T(1024)(128)(4,1)}), s8[4194304]{0:T(1024)(128)(4,1)S(1)}, s32[]{:S(2)}) async-start(s8[4718592]{0:T(1024)(128)(4,1)} %bitcast.85), calls=%async_computation.2 | async-start | bytes 8388608
  209.7 13.5 %slice-start.6 = ((s8[5701632]{0:T(1024)(128)(4,1)}), s8[4194304]{0:T(1024)(128)(4,1)S(1)}, s32[]{:S(2)}) async-start(s8[5701632]{0:T(1024)(128)(4,1)} %bitcast.90), calls=%async_computation.6 | async-start | bytes 8388608
  212.2 9.0 %copy-start.7 = (f32[928,768]{1,0:T(8,128)S(1)}, f32[928,768]{1,0:T(8,128)}, u32[]{:S(2)}) copy-start(f32[928,768]{1,0:T(8,128)} %get-tuple-element.91) | copy-start | bytes 8552452
  212.2 11.1 %slice-start.3 = ((s8[4718592]{0:T(1024)(128)(4,1)}), s8[524288]{0:T(1024)(128)(4,1)S(1)}, s32[]{:S(2)}) async-start(s8[4718592]{0:T(1024)(128)(4,1)} %bitcast.85), calls=%async_computation.3 | async-start | bytes 1048576
  212.2 11.1 %slice-start.7 = ((s8[5701632]{0:T(1024)(128)(4,1)}), s8[1507328]{0:T(1024)(128)(4,1)S(1)}, s32[]{:S(2)}) async-start(s8[5701632]{0:T(1024)(128)(4,1)} %bitcast.90), calls=%async_computation.7 | async-start | bytes 3014656
  221.1 2.1 copy-start.20
  407.4 7.3 %copy-start.11 = (bf16[3,256,768]{2,1,0:T(8,128)(2,1)S(1)}, bf16[3,256,768]{2,1,0:T(8,128)(2,1)}, u32[]{:S(2)}) copy-start(bf16[3,256,768]{2,1,0:T(8,128)(2,1)} %get-tuple-element.54) | copy-start | bytes 3538948
  407.4 8.3 %copy-start.12 = (f32[3,192,384]{2,1,0:T(8,128)S(1)}, f32[3,192,384]{2,1,0:T(8,128)}, u32[]{:S(2)}) copy-start(f32[3,192,384]{2,1,0:T(8,128)} %get-tuple-element.56) | copy-start | bytes 2654212
  412.3 4.3 %copy-start.13 = (f32[192,384]{1,0:T(8,128)S(1)}, f32[192,384]{1,0:T(8,128)}, u32[]{:S(2)}) copy-start(f32[192,384]{1,0:T(8,128)} %get-tuple-element.120) | copy-start | bytes 884740
  414.7 2.7 copy-start.10
  415.8 2.7 copy-start.9
  415.8 3.7 copy-start.1

commit v3 on v2

--- a/solution.py
+++ b/solution.py
@@ -31,6 +31,7 @@
 SEG = 32
 MASKED = -1e9
 VMEM_LIMIT = 60 * 2**20
+VMEM_BACK = 63 * 2**20
 
 
 def coords():
@@ -183,11 +184,12 @@
 
 def block(ref, w, t, f, part=None):
     rows, cols = BLOCKS[w]
-    row_at, col_at = (f, t) if w == 4 else (t, f)
     start, size = part if part is not None else (0, rows)
+    if w == 4:
+        return ref.at[pl.ds(pl.multiple_of(t * D + f * rows + start, 16), size)]
     return ref.at[
-        pl.ds(pl.multiple_of(row_at * rows + start, 16), size),
-        pl.ds(pl.multiple_of(col_at * cols, 128), cols),
+        pl.ds(pl.multiple_of(t * rows + start, 16), size),
+        pl.ds(pl.multiple_of(f * cols, 128), cols),
     ]
 
 
@@ -495,7 +497,7 @@
     tokens = shape((ROWS, D), BF)
     outs = [tokens, tokens, tokens, shape((ROWS, 3 * D), BF), tokens, shape((ROWS, HEADS * 256), BF)]
     if direct:
-        outs += [shape(s, BF) for s in ((3, D, D), (D, D), (D, 4 * D), (4 * D, D))]
+        outs += [shape(s, BF) for s in ((3, D, D), (D, D), (4 * D, D), (4 * D, D))]
     outs += [shape((1 + NPART, 4, FULL, 256), BF), shape((D, D), BF)]
     scratch = [
         pltpu.VMEM((2, images, 2, PIECE, D), BF),
@@ -520,253 +522,6 @@
         ),
         name="forward_attention",
     )(x3, c3, *weights, vec, rel)
-
-
-def grad_block(ref, w, t, f, part=None):
-    rows, cols = ((192, 384), (192, 384), (384, 768), (768, 384))[w]
-    row_at, col_at = (f, t) if w == 2 else (t, f)
-    start, size = row_at * rows, rows
-    if part is not None:
-        size = rows // 2
-        start = start + part * size
-    row_slice = pl.ds(pl.multiple_of(start, 16), size)
-    col_slice = pl.ds(pl.multiple_of(col_at * cols, 128), cols)
-    if w == 0:
-        return ref.at[:, row_slice, col_slice]
-    return ref.at[row_slice, col_slice]
-
-
-def add_rows(dst, src, rows, cols):
-    size = 96 if rows % 96 == 0 else 64
-
-    @pl.loop(0, rows // size)
-    def _(n):
-        here = pl.ds(pl.multiple_of(n * size, 16), size)
-        dst[here] = (dst[here].astype(F32) + src[here].astype(F32)).astype(BF)
-
-
-def add_view(dst, src, w):
-    if w == 0:
-        for k in range(3):
-            view = dst.at[k]
-            add_rows(view, src.at[k], view.shape[0], view.shape[1])
-    else:
-        add_rows(dst, src, dst.shape[0], dst.shape[1])
-
-
-def copy_f32(dst, src, w):
-    if w == 0:
-        for k in range(3):
-            copy_f32(dst.at[k], src.at[k], 1)
-        return
-    rows = dst.shape[0]
-    size = 96 if rows % 96 == 0 else 64
-
-    @pl.loop(0, rows // size)
-    def _(n):
-        here = pl.ds(pl.multiple_of(n * size, 16), size)
-        dst[here] = src[here].astype(F32)
-
-
-HALF_SHAPES = ((3, 96, 384), (96, 384), (192, 768), (384, 384))
-SHARD_SHAPES = ((3, 192, 384), (192, 384), (384, 768), (768, 384))
-
-
-def reduce_kernel(images, with_weights, *refs):
-    if with_weights:
-        (y_ref, g_ref, gq, gp, gu, gd, few_ref, y_out, g_out, oq, op, ou, od, few_out,
-         stage, ss, rs, r1q, r1p, r1u, r1d, raq, rap, rau, rad, rzq, rzp, rzu, rzd,
-         few_in, s1, v1, s2, v2, s3, v3, fs, fr) = refs
-    else:
-        y_ref, g_ref, y_out, g_out, stage, ss, rs = refs
-    me = coords()
-    f, ctx, tp = me
-    group_barrier(((1 - f, ctx, tp),) if with_weights else ())
-
-    places = window_places(ctx, tp)
-    pairs = ((y_ref, y_out), (g_ref, g_out))
-    for a, (src_ref, _) in enumerate(pairs):
-        for n, (slot, p, rows, exists, image, u, c, d_ctx, d_tp, row) in enumerate(places):
-            def go(a=a, n=n, rows=rows, image=image, u=u, c=c, d_ctx=d_ctx, d_tp=d_tp, row=row, src_ref=src_ref):
-                src = src_ref.at[pl.ds(row, rows)]
-                dst = stage.at[a, image, u, pl.ds(pl.multiple_of(c * 32, 16), rows)]
-                send_or_copy(src, dst, (d_ctx, d_tp), me, ss.at[a, n], rs.at[a, image, u, c])
-            if exists is None:
-                go()
-            else:
-                pl.when(exists)(go)
-
-    if with_weights:
-        grads = (gq, gp, gu, gd)
-        outs = (oq, op, ou, od)
-        r1, ra, rz = (r1q, r1p, r1u, r1d), (raq, rap, rau, rad), (rzq, rzp, rzu, rzd)
-        g, y, s = 1 - f, (tp + 2) % 4, tp + 1 - 2 * (tp % 2)
-        sy = (s + 2) % 4
-        to_x, to_y, to_s = (g, ctx, tp), (f, ctx, y), (f, ctx, s)
-        order = (3, 2, 1, 0)
-        waits = []
-
-        def send(src, dst, dest, send_sem, recv_sem):
-            cp = remote(src, dst, dest, send_sem, recv_sem)
-            cp.start()
-            waits.append(cp)
-            return cp
-
-        few_out[...] = few_ref[...]
-        few_steps = (to_s, to_x, to_y, (f, ctx + 1 - 2 * (ctx % 2), tp), (f, (ctx + 2) % 4, tp))
-
-        def few_start(n):
-            few_in[5 + n] = few_out[...]
-            return send(few_in.at[5 + n], few_in.at[n], few_steps[n], fs.at[n], fr.at[n])
-
-        def few_finish(cp, n):
-            cp.wait_recv()
-            few_out[...] = few_out[...] + few_in[n]
-
-        first = {}
-        for w in order:
-            for n, t_there in enumerate((s, sy)):
-                for h in range(2):
-                    first[w, n, h] = send(
-                        grad_block(grads[w], w, t_there, h), r1[w].at[n, h], to_s, s1.at[w, n, h], v1.at[w, n, h]
-                    )
-        few = few_start(0)
-
-        phase1 = {}
-        for w in order:
-            for n, t_here in enumerate((tp, y)):
-                for h in range(2):
-                    first[w, n, h].wait_recv()
-                    add_view(grad_block(grads[w], w, t_here, h), r1[w].at[n, h], w)
-            phase1[w] = (
-                send(grad_block(grads[w], w, tp, g, 0), ra[w].at[0], to_x, s2.at[w, 0], v2.at[w, 0]),
-                send(grad_block(grads[w], w, y, g, 0), ra[w].at[1], to_x, s2.at[w, 1], v2.at[w, 1]),
-                send(grad_block(grads[w], w, y, f, 1), ra[w].at[2], to_y, s2.at[w, 2], v2.at[w, 2]),
-                send(grad_block(grads[w], w, y, g, 1), ra[w].at[3], to_y, s2.at[w, 3], v2.at[w, 3]),
-            )
-        few_finish(few, 0)
-        few = few_start(1)
-        phase2 = {}
-        for w in order:
-            views = (
-                grad_block(grads[w], w, tp, f, 0), grad_block(grads[w], w, y, f, 0),
-                grad_block(grads[w], w, tp, f, 1), grad_block(grads[w], w, tp, g, 1),
-            )
-            for k in range(4):
-                phase1[w][k].wait_recv()
-                add_view(views[k], ra[w].at[k], w)
-            phase2[w] = (
-                send(grad_block(grads[w], w, y, f, 0), ra[w].at[4], to_y, s2.at[w, 4], v2.at[w, 4]),
-                send(grad_block(grads[w], w, tp, g, 1), ra[w].at[5], to_x, s2.at[w, 5], v2.at[w, 5]),
-            )
-        few_finish(few, 1)
-        few = few_start(2)
-
-        outer = (ctx == 0) | (ctx == 3)
-        inner = jnp.logical_not(outer)
-        mid_peer = (f, 3 - ctx, tp)
-        in_peer = (f, jnp.where(ctx == 0, 1, 2), tp)
-        out_peer = (f, jnp.where(ctx == 1, 0, 3), tp)
-        for w in order:
-            for k in range(2):
-                phase2[w][k].wait_recv()
-                add_view(grad_block(grads[w], w, tp, f, k), ra[w].at[4 + k], w)
-            mine = grad_block(grads[w], w, tp, f)
-
-            @pl.when(outer)
-            def _(w=w, mine=mine):
-                remote(mine, rz[w].at[0], in_peer, s3.at[w, 0], v3.at[w, 0]).start()
-        for w in order:
-            mine = grad_block(grads[w], w, tp, f)
-
-            @pl.when(inner)
-            def _(w=w, mine=mine):
-                pltpu.make_async_copy(rz[w].at[0], rz[w].at[0], v3.at[w, 0]).wait()
-                add_view(mine, rz[w].at[0], w)
-                remote(mine, rz[w].at[1], mid_peer, s3.at[w, 0], v3.at[w, 1]).start()
-        for w in order:
-            mine = grad_block(grads[w], w, tp, f)
-
-            @pl.when(inner)
-            def _(w=w, mine=mine):
-                pltpu.make_async_copy(rz[w].at[1], rz[w].at[1], v3.at[w, 1]).wait()
-                add_view(rz[w].at[1], mine, w)
-                remote(rz[w].at[1], rz[w].at[2], out_peer, s3.at[w, 1], v3.at[w, 2]).start()
-                copy_f32(outs[w], rz[w].at[1], w)
-        few_finish(few, 2)
-        few = few_start(3)
-        for w in order:
-            @pl.when(outer)
-            def _(w=w):
-                pltpu.make_async_copy(rz[w].at[2], rz[w].at[2], v3.at[w, 2]).wait()
-                copy_f32(outs[w], rz[w].at[2], w)
-        few_finish(few, 3)
-        few = few_start(4)
-        few_finish(few, 4)
-
-        for cp in waits:
-            cp.wait_send()
-        for w in order:
-            one = rz[w].at[0]
-            pltpu.make_async_copy(one, one, s3.at[w, 0]).wait()
-
-            @pl.when(inner)
-            def _(one=one, w=w):
-                pltpu.make_async_copy(one, one, s3.at[w, 1]).wait()
-
-    unpack = pack_matrix()
-    for a, (src_ref, out_ref) in enumerate(pairs):
-        for i in range(images):
-            for u in range(2):
-                for c in range(5):
-                    rows = 32 if c < 4 else 16
-                    dst = stage.at[a, i, u, pl.ds(c * 32, rows)]
-                    pltpu.make_async_copy(dst, dst, rs.at[a, i, u, c]).wait()
-                out_ref[i, pl.ds(u * 128, 128)] = lax.dot_general(
-                    unpack, stage[a, i, u], (((0,), (0,)), ((), ())), preferred_element_type=F32
-                ).astype(BF)
-        for n, (slot, p, rows, exists, image, u, c, d_ctx, d_tp, row) in enumerate(places):
-            def done(a=a, n=n, rows=rows, d_ctx=d_ctx, d_tp=d_tp, row=row, src_ref=src_ref):
-                wait_sent(src_ref.at[pl.ds(row, rows)], (d_ctx, d_tp), me, ss.at[a, n])
-            if exists is None:
-                done()
-            else:
-                pl.when(exists)(done)
-
-
-def send_back(y, g, images, grads=None, few=None):
-    vmem = pl.BlockSpec(memory_space=pltpu.VMEM)
-    with_weights = grads is not None
-    n_places = NFULL * PAIRS + NPART * (4 + PAIRS)
-    token = jax.ShapeDtypeStruct((images, 256, D), BF)
-    out_shape = [token, token]
-    args = [y, g]
-    dma = pltpu.SemaphoreType.DMA
-    scratch = [
-        pltpu.VMEM((2, images, 2, PIECE, D), BF),
-        dma((2, n_places)),
-        dma((2, images, 2, 5)),
-    ]
-    if with_weights:
-        args += list(grads) + [few]
-        out_shape += [jax.ShapeDtypeStruct(s, F32) for s in SHARD_SHAPES]
-        out_shape += [jax.ShapeDtypeStruct(few.shape, F32)]
-        scratch += [pltpu.VMEM((2, 2) + s, BF) for s in SHARD_SHAPES]
-        scratch += [pltpu.VMEM((6,) + s, BF) for s in HALF_SHAPES]
-        scratch += [pltpu.VMEM((3,) + s, BF) for s in SHARD_SHAPES]
-        scratch += [pltpu.VMEM((10,) + few.shape, F32)]
-        scratch += [dma((4, 2, 2)), dma((4, 2, 2)), dma((4, 6)), dma((4, 6)), dma((4, 2)), dma((4, 3)), dma((5,)), dma((5,))]
-    return pl.pallas_call(
-        functools.partial(reduce_kernel, images, with_weights),
-        out_shape=out_shape,
-        in_specs=[vmem] * len(args),
-        out_specs=[vmem] * len(out_shape),
-        scratch_shapes=scratch,
-        compiler_params=pltpu.CompilerParams(
-            collective_id=1, has_side_effects=True, vmem_limit_bytes=VMEM_LIMIT
-        ),
-        name="tokens_and_gradients_out",
-    )(*args)
 
 
 def barrel(x, shift, left):
@@ -842,16 +597,18 @@
     return jnp.where(is_narrow, 1, 0)
 
 
-def attention_back_slot(qkv, do_ref, rel_cols, bias_v, e_at, p_ref, dqkv, d_scr, acc_scr, pad_acc,
-                        rel_acc, base, rows, narrow):
+def attention_back_slot(qkv, do_ref, rel_cols, bias_v, e_at, p_ref, d_scr, acc_scr, pad_acc, rel_acc, base, rows, narrow):
     a_row, b_row = row_places(rows, narrow)
+    here = pl.ds(base, rows)
     for g in range(GROUPS):
         dx = jnp.zeros((rows, 256), F32)
         for hp in (2 * g, 2 * g + 1):
-            q = qkv[pl.ds(base, rows), pl.ds(hp * 128, 128)]
+            cols = pl.ds(hp * 128, 128)
+            k_cols, v_cols = pl.ds(D + hp * 128, 128), pl.ds(2 * D + hp * 128, 128)
+            q = qkv[here, cols]
             k = key_rows(qkv, base, rows, D + hp * 128, jnp.zeros((1, 128), BF))
-            v = key_rows(qkv, base, rows, 2 * D + hp * 128, bias_v[:, pl.ds(hp * 128, 128)])
-            do = do_ref[pl.ds(base, rows), pl.ds(hp * 128, 128)]
+            v = key_rows(qkv, base, rows, 2 * D + hp * 128, bias_v[:, cols])
+            do = do_ref[here, cols]
             dq = jnp.zeros((rows, 128), F32)
             dk = jnp.zeros((FULL, 128), F32)
             dv = jnp.zeros((FULL, 128), F32)
@@ -860,7 +617,7 @@
                 mask = half_mask(hh)
                 do_m = do * mask
                 dp = nt(do_m, v)
-                p_low = p_ref[pl.ds(base, rows), pl.ds(h * 256, FULL)]
+                p_low = p_ref[pl.ds(0, rows), pl.ds(h * 256, FULL)]
                 t = p_low.astype(F32)
                 tp = t * dp
                 ds = (tp - t * jnp.sum(tp, axis=-1, keepdims=True)).astype(BF)
@@ -868,93 +625,540 @@
                 dx = dx + jnp.dot(ds, e_at[h % 4], preferred_element_type=F32)
                 dk = dk + tn(ds, q * (mask * 0.125))
                 dv = dv + tn(p_low, do_m)
-            acc_scr[pl.ds(0, rows), pl.ds(hp * 128, 128)] = dq
-            dqkv[pl.ds(base, rows), pl.ds(D + hp * 128, 128)] = dk[:rows].astype(BF)
-            dqkv[pl.ds(base, rows), pl.ds(2 * D + hp * 128, 128)] = dv[:rows].astype(BF)
+            acc_scr[pl.ds(0, rows), cols] = dq
+            qkv[here, k_cols] = dk[:rows].astype(BF)
+            qkv[here, v_cols] = dv[:rows].astype(BF)
             if rows < FULL:
-                pad_acc[:, pl.ds(hp * 128, 128)] += jnp.sum(dv[rows:], axis=0, keepdims=True)
+                pad_acc[:, cols] += jnp.sum(dv[rows:], axis=0, keepdims=True)
         lane = lax.broadcasted_iota(jnp.int32, (rows, 128), 1) % SEG
         for axis, pos in ((0, a_row), (1, b_row)):
             v = jnp.where(lane < WIN, dx[:, axis * 128:(axis + 1) * 128], 0.0)
             v = barrel(v, jnp.maximum(13 - pos, 0), False)
             d_scr[pl.ds(0, rows), pl.ds(axis * 384 + g * 128, 128)] = v.astype(BF)
     d = d_scr[pl.ds(0, rows), :]
-    q_all = qkv[pl.ds(base, rows), pl.ds(0, D)]
-    dq = acc_scr[pl.ds(0, rows), :] + nt(d, rel_cols[...])
-    dqkv[pl.ds(base, rows), pl.ds(0, D)] = dq.astype(BF)
-    rel_acc[...] += tn(d, q_all)
-
-
-def attention_back_kernel(qkv, do_ref, rel_cols, bias_v, e_ref, p_ref, dqkv, pad_ref, rel_ref,
-                          d_scr, acc_scr, rel_acc):
-    pad_ref[...] = jnp.zeros_like(pad_ref)
-    rel_acc[...] = jnp.zeros_like(rel_acc)
-
-    @pl.loop(0, NFULL)
+    rel_acc[pl.ds(0, D)] += tn(d, qkv[here, pl.ds(0, D)])
+    qkv[here, pl.ds(0, D)] = (acc_scr[pl.ds(0, rows), :] + nt(d, rel_cols[...])).astype(BF)
+
+
+TILE = (D, D, 192, 192, 192, 192)
+HALVES = ((384, D), (D, 384), (192, 384), (192, 384), (192, 384), (192, 384))
+CHUNK = ROWS // 2
+SUMS = 16
+FEW = 12 * 6 + 2 * SEG
+
+
+def add_rows(dst, src):
+    rows = dst.shape[0]
+    size = 64
+
+    @pl.loop(0, rows // size)
     def _(n):
-        attention_back_slot(qkv, do_ref, rel_cols, bias_v, e_ref.at[0], p_ref, dqkv, d_scr, acc_scr, pad_ref,
-                            rel_acc, pl.multiple_of(n * FULL, 16), FULL, None)
-
-    @pl.loop(0, NPART)
-    def _(n):
-        attention_back_slot(qkv, do_ref, rel_cols, bias_v, e_ref.at[1 + n], p_ref, dqkv, d_scr, acc_scr, pad_ref,
-                            rel_acc, pl.multiple_of(PBASE + n * PART, 16), PART, narrow_flag(n))
-
-    lane = lax.broadcasted_iota(jnp.int32, (SEG, D), 1) // HEAD_DIM
+        here = pl.ds(pl.multiple_of(n * size, 16), size)
+        dst[here] = (dst[here].astype(F32) + src[here].astype(F32)).astype(BF)
+
+
+class Reduce:
+    def __init__(self, grads, me, outs, r1, rx, ry, rz, s1, v1, s2, v2, s3, v3, sz, vz, so):
+        self.grads, self.outs = grads, outs
+        self.r1u, self.r1d, self.r1p = r1
+        self.rx, self.ry, self.rz = rx, ry, rz
+        self.s1, self.v1, self.s2, self.v2, self.s3, self.v3 = s1, v1, s2, v2, s3, v3
+        self.sz, self.vz, self.so = sz, vz, so
+        f, ctx, tp = me
+        self.f, self.g = f, 1 - f
+        self.c, self.own = tp % 2, tp // 2
+        self.to_s = (f, ctx, tp + 1 - 2 * self.c)
+        self.to_x = (1 - f, ctx, tp)
+        self.to_y = (f, ctx, (tp + 2) % 4)
+        self.outer = (ctx == 0) | (ctx == 3)
+        self.inner = jnp.logical_not(self.outer)
+        self.to_mid = (f, 3 - ctx, tp)
+        self.to_in = (f, jnp.where(ctx == 0, 1, 2), tp)
+        self.to_out = (f, jnp.where(ctx == 1, 0, 3), tp)
+
+    def tile(self, w, t):
+        return self.grads[w].at[pl.ds(pl.multiple_of(t * TILE[w], 16), TILE[w])]
+
+    def half(self, w, t, f):
+        if w == 0:
+            return self.grads[w].at[pl.ds(pl.multiple_of(t * D + f * 384, 16), 384)]
+        return self.grads[w].at[
+            pl.ds(pl.multiple_of(t * TILE[w], 16), TILE[w]), pl.ds(pl.multiple_of(f * 384, 128), 384)
+        ]
+
+    def landing(self, w, j):
+        if w < 2:
+            return (self.r1u, self.r1d)[w].at[j]
+        if w == 2:
+            return self.r1p.at[j]
+        return self.r1d.at[(w - 3) // 2, pl.ds(((w - 3) % 2) * 384 + j * 192, 192)]
+
+    def core_copy(self, w, j):
+        src = self.tile(w, 1 - self.c + 2 * j)
+        return remote(src, self.landing(w, j), self.to_s, self.s1.at[w, j], self.v1.at[w, j])
+
+    def core_send(self, w, j):
+        self.core_copy(w, j).start()
+
+    def x_copy(self, w, j):
+        src = self.half(w, self.c + 2 * j, self.g)
+        return remote(src, self.rx[w].at[j], self.to_x, self.s2.at[w, j], self.v2.at[w, j])
+
+    def core_add(self, w, j):
+        self.core_copy(w, j).wait_recv()
+        add_rows(self.tile(w, self.c + 2 * j), self.landing(w, j))
+        self.x_copy(w, j).start()
+
+    def y_copy(self, w):
+        src = self.half(w, self.c + 2 * (1 - self.own), self.f)
+        return remote(src, self.ry[w], self.to_y, self.s3.at[w], self.v3.at[w])
+
+    def x_add(self, w, j):
+        self.x_copy(w, j).wait_recv()
+        add_rows(self.half(w, self.c + 2 * j, self.f), self.rx[w].at[j])
+
+        @pl.when(self.own != j)
+        def _():
+            self.y_copy(w).start()
+
+    def mine(self, w):
+        return self.half(w, self.c + 2 * self.own, self.f)
+
+    def y_add(self, w):
+        self.y_copy(w).wait_recv()
+        add_rows(self.mine(w), self.ry[w])
+
+        @pl.when(self.outer)
+        def _():
+            remote(self.mine(w), self.rz[w].at[0], self.to_in, self.sz.at[w, 0], self.vz.at[w, 0]).start()
+
+    def z_wait(self, w, slot, sem):
+        view = self.rz[w].at[slot]
+        pltpu.make_async_copy(view, view, sem).wait()
+
+    def z_mid(self, w):
+        @pl.when(self.inner)
+        def _():
+            self.z_wait(w, 0, self.vz.at[w, 0])
+            add_rows(self.mine(w), self.rz[w].at[0])
+            remote(self.mine(w), self.rz[w].at[1], self.to_mid, self.sz.at[w, 0], self.vz.at[w, 1]).start()
+
+    def z_out(self, w):
+        @pl.when(self.inner)
+        def _():
+            self.z_wait(w, 1, self.vz.at[w, 1])
+            add_rows(self.rz[w].at[1], self.mine(w))
+            remote(self.rz[w].at[1], self.rz[w].at[0], self.to_out, self.sz.at[w, 1], self.vz.at[w, 2]).start()
+            pltpu.make_async_copy(self.rz[w].at[1], self.outs[w], self.so.at[w]).start()
+
+    def z_end(self, w):
+        @pl.when(self.outer)
+        def _():
+            self.z_wait(w, 0, self.vz.at[w, 2])
+            pltpu.make_async_copy(self.rz[w].at[0], self.outs[w], self.so.at[w]).start()
+
+    def sent(self, w):
+        for j in range(2):
+            self.core_copy(w, j).wait_send()
+            self.x_copy(w, j).wait_send()
+        self.y_copy(w).wait_send()
+        self.z_wait(w, 0, self.sz.at[w, 0])
+
+        @pl.when(self.inner)
+        def _():
+            self.z_wait(w, 0, self.sz.at[w, 1])
+
+        pltpu.make_async_copy(self.rz[w].at[0], self.outs[w], self.so.at[w]).wait()
+
+
+def backward_kernel(images, direct, *refs):
+    it = iter(refs)
+
+    def take(n):
+        return [next(it) for _ in range(n)]
+
+    x_h, c_h, n1_h, qkv_h, att_h, p_h, wq_h, wp_h, wu_h, wd_h, e_h, rel_h, vec = take(13)
+    staged, few_out = take(2)
+    outs = take(6)
+    cot, att, n2, xhat2, hid, dg = take(6)
+    x = hid
+    acc, dn2 = take(2)
+    wu, wd, wp, wq, dwq, qkv, p_buf, e, rel_cols, d_scr, acc_scr = take(11)
+    bias_v, pad_acc, sums, r2, real = take(5)
+    ls, ss, rs = take(3)
+    if direct:
+        r1 = take(3)
+        rx, ry, rz = take(6), take(6), take(6)
+        few_in, = take(1)
+        sems = take(9)
+        few_s, few_r = take(2)
+    me = coords()
+    f, ctx, tp = me
+    loads = {}
+
+    def load(name, src, dst):
+        loads[name] = pltpu.make_async_copy(src, dst, ls.at[len(loads)])
+        loads[name].start()
+
+    load("att", att_h, att)
+    load("wp", wp_h, wp)
+    load("x", x_h, x)
+    load("wu", wu_h, wu)
+    load("wd", wd_h, wd)
+    load("cot", c_h, cot)
+    load("qkv", qkv_h, qkv)
+    load("e", e_h, e)
+    load("rel", rel_h, rel_cols)
+    load("wq", wq_h, wq)
+
+    def p_copy(slot):
+        base, rows = (slot * FULL, FULL) if slot < NFULL else (PBASE + (slot - NFULL) * PART, PART)
+        return pltpu.make_async_copy(
+            p_h.at[pl.ds(base, rows)], p_buf.at[slot % 2, pl.ds(0, rows)], ls.at[12 + slot % 2]
+        )
+
+    p_copy(0).start()
+    p_copy(1).start()
+    group_barrier(((1 - f, ctx, tp),) if direct else ())
+    grads = (wu, wd, wp, dwq.at[0], dwq.at[1], dwq.at[2])
+    red = Reduce(grads, me, outs, r1, rx, ry, rz, *sems) if direct else None
+    c = tp % 2
+    sums[...] = jnp.zeros_like(sums)
+    pad_acc[...] = jnp.zeros_like(pad_acc)
+    bias_v[...] = vec[5:6, :]
+    for slot, base, rows in slots():
+        real[pl.ds(base, rows)] = jnp.where(row_real(slot, rows), 1.0, 0.0)
+
+    def row_chunks(body):
+        @pl.loop(0, ROWS // CHUNK)
+        def _(n):
+            body(pl.ds(pl.multiple_of(n * CHUNK, 16), CHUNK))
+
+    for name in ("att", "wp", "x"):
+        loads[name].wait()
+
+    def project(here):
+        mid = x[here].astype(F32) + jnp.dot(att[here], wp[...], preferred_element_type=F32) + vec[3:4, :]
+        mean = jnp.mean(mid, axis=-1, keepdims=True)
+        centered = mid - mean
+        r = lax.rsqrt(jnp.mean(centered * centered, axis=-1, keepdims=True) + EPSILON)
+        xhat = centered * r
+        r2[here] = r
+        xhat2[here] = xhat.astype(BF)
+        n2[here] = (xhat * vec[1:2, :] + vec[2:3, :]).astype(BF)
+        acc[here] = mid + vec[4:5, :]
+        dn2[here] = jnp.zeros((CHUNK, D), F32)
+
+    row_chunks(project)
+
+    for name in ("wu", "wd", "cot"):
+        loads[name].wait()
+    for t in range(4):
+        base = t * D
+
+        @pl.loop(0, 3)
+        def _(j, base=base, t=t):
+            units = pl.ds(pl.multiple_of(j * 256, 128), 256)
+            gate = jnp.dot(n2[...], wu[pl.ds(base, D), units], preferred_element_type=F32)
+            up_bias = jnp.where(j == 0, vec[6 + t:7 + t, 0:256], jnp.where(
+                j == 1, vec[6 + t:7 + t, 256:512], vec[6 + t:7 + t, 512:768]))
+            hidden, slope = gelu_both(gate + up_bias)
+            hid[:, units] = hidden.astype(BF)
+            there = pl.ds(pl.multiple_of(base + j * 256, 16), 256)
+            d_gate = (nt(cot[...], wd[there, :]) * slope).astype(BF)
+            dg[:, units] = d_gate
+            sums[pl.ds(8 + t, 1), units] = jnp.sum(d_gate.astype(F32), axis=0, keepdims=True)
+
+        tile = pl.ds(base, D)
+
+        def through(here, tile=tile):
+            acc[here] += jnp.dot(hid[here], wd[tile, :], preferred_element_type=F32)
+            dn2[here] += nt(dg[here], wu[tile, :])
+
+        row_chunks(through)
+
+        @pl.loop(0, 3)
+        def _(j, base=base):
+            part = pl.ds(pl.multiple_of(j * 256, 128), 256)
+            there = pl.ds(pl.multiple_of(base + j * 256, 16), 256)
+            wd[there, :] = tn(hid[:, part], cot[...]).astype(BF)
+            wu[there, :] = tn(n2[:, part], dg[...]).astype(BF)
+
+        if direct:
+            @pl.when(c != t % 2)
+            def _(t=t):
+                red.core_send(1, t // 2)
+                red.core_send(0, t // 2)
+
+            if t:
+                @pl.when(c == (t - 1) % 2)
+                def _(t=t):
+                    red.core_add(1, (t - 1) // 2)
+                    red.core_add(0, (t - 1) // 2)
+
+    def back_two(here):
+        n = dn2[here]
+        xhat = xhat2[here].astype(F32)
+        c_rows = cot[here].astype(F32)
+        m = n * vec[1:2, :]
+        sums[5:6, :] += jnp.sum(n * xhat, axis=0, keepdims=True)
+        sums[6:7, :] += jnp.sum(n, axis=0, keepdims=True)
+        sums[7:8, :] += jnp.sum(c_rows, axis=0, keepdims=True)
+        mean = jnp.mean(m, axis=-1, keepdims=True)
+        mean_x = jnp.mean(m * xhat, axis=-1, keepdims=True)
+        d_mid = c_rows + r2[here] * (m - mean - xhat * mean_x)
+        dn2[here] = d_mid
+        branch = d_mid.astype(BF)
+        n2[here] = branch
+        sums[4:5, :] += jnp.sum(branch.astype(F32), axis=0, keepdims=True)
+        dg[here] = acc[here].astype(BF)
+        hid[here] = nt(branch, wp[...]).astype(BF)
+
+    row_chunks(back_two)
+    places = window_places(ctx, tp)
+
+    def tokens_out(a, src_ref):
+        for n, (slot, p, rows, exists, image, u, col, d_ctx, d_tp, row) in enumerate(places):
+            def go(n=n, rows=rows, image=image, u=u, col=col, d_ctx=d_ctx, d_tp=d_tp, row=row):
+                src = src_ref.at[pl.ds(row, rows)]
+                dst = staged.at[a, image, u, pl.ds(pl.multiple_of(col * 32, 16), rows)]
+                send_or_copy(src, dst, (d_ctx, d_tp), me, ss.at[a, n], rs.at[a, image, u, col])
+            if exists is None:
+                go()
+            else:
+                pl.when(exists)(go)
+
+    def tokens_done(a, src_ref):
+        for i in range(images):
+            for u in range(2):
+                for col in range(5):
+                    dst = staged.at[a, i, u, pl.ds(col * 32, 32 if col < 4 else 16)]
+                    pltpu.make_async_copy(dst, dst, rs.at[a, i, u, col]).wait()
+        for n, (slot, p, rows, exists, image, u, col, d_ctx, d_tp, row) in enumerate(places):
+            def done(n=n, rows=rows, d_ctx=d_ctx, d_tp=d_tp, row=row):
+                wait_sent(src_ref.at[pl.ds(row, rows)], (d_ctx, d_tp), me, ss.at[a, n])
+            if exists is None:
+                done()
+            else:
+                pl.when(exists)(done)
+
+    tokens_out(0, dg)
+
+    @pl.loop(0, 3)
+    def _(j):
+        part = pl.ds(pl.multiple_of(j * 256, 128), 256)
+        wp[pl.ds(pl.multiple_of(j * 256, 16), 256), :] = tn(att[:, part], n2[...]).astype(BF)
+
+    if direct:
+        @pl.when(c == 1)
+        def _():
+            red.core_add(1, 1)
+            red.core_add(0, 1)
+
+        red.core_send(2, 0)
+        red.core_send(2, 1)
+        red.x_add(1, 0)
+
+    load_n1 = pltpu.make_async_copy(n1_h, n2, ls.at[11])
+    load_n1.start()
+    load_x = pltpu.make_async_copy(x_h, xhat2, ls.at[14])
+    load_x.start()
+    for name in ("qkv", "e", "rel"):
+        loads[name].wait()
+    acc[pl.ds(0, D)] = jnp.zeros((D, D), F32)
+    for slot, base, rows in slots():
+        p_copy(slot).wait()
+        kind = 0 if slot < NFULL else 1 + slot - NFULL
+        narrow = None if slot < NFULL else narrow_flag(slot - NFULL)
+        attention_back_slot(qkv, hid, rel_cols, bias_v, e.at[kind], p_buf.at[slot % 2], d_scr, acc_scr,
+                            pad_acc, acc, base, rows, narrow)
+        if slot + 2 < NFULL + NPART:
+            p_copy(slot + 2).start()
+        if direct:
+            if slot == 0:
+                red.x_add(0, 0)
+                red.core_add(2, 0)
+                red.core_add(2, 1)
+            elif slot == 2:
+                red.x_add(1, 1)
+            elif slot == 3:
+                red.y_add(1)
+
+    load_n1.wait()
+    load_x.wait()
+    loads["wq"].wait()
+    for w in range(3):
+        @pl.loop(0, 3)
+        def _(j, w=w):
+            part = pl.ds(pl.multiple_of(w * D + j * 256, 128), 256)
+            d_cols = qkv[:, part]
+            dwq[w, pl.ds(pl.multiple_of(j * 256, 16), 256), :] = tn(d_cols, n2[...]).astype(BF)
+
+        if direct:
+            red.core_send(3 + w, 0)
+            red.core_send(3 + w, 1)
+
+    def back_one(here):
+        d_qkv = qkv[here, :]
+        n = jnp.zeros((CHUNK, D), F32)
+        for w in range(3):
+            n = n + jnp.dot(d_qkv[:, w * D:(w + 1) * D], wq[w], preferred_element_type=F32)
+        sums[2:3, :] += jnp.sum(d_qkv[:, :D].astype(F32), axis=0, keepdims=True)
+        sums[3:4, :] += jnp.sum(d_qkv[:, 2 * D:].astype(F32), axis=0, keepdims=True)
+        n = n * real[here]
+        rows = xhat2[here].astype(F32)
+        centered = rows - jnp.mean(rows, axis=-1, keepdims=True)
+        r = lax.rsqrt(jnp.mean(centered * centered, axis=-1, keepdims=True) + EPSILON)
+        xhat = centered * r
+        sums[0:1, :] += jnp.sum(n * xhat, axis=0, keepdims=True)
+        sums[1:2, :] += jnp.sum(n, axis=0, keepdims=True)
+        m = n * vec[0:1, :]
+        mean = jnp.mean(m, axis=-1, keepdims=True)
+        mean_x = jnp.mean(m * xhat, axis=-1, keepdims=True)
+        cot[here] = (dn2[here] + r * (m - mean - xhat * mean_x)).astype(BF)
+
+    if direct:
+        for w in range(3):
+            red.core_add(3 + w, 0)
+            red.core_add(3 + w, 1)
+        red.x_add(0, 1)
+        red.y_add(0)
+        red.z_mid(1)
+    row_chunks(back_one)
+    tokens_out(1, cot)
+
+    sums[3:4, :] += pad_acc[...]
+    order = (0, 1, 2, 3, 4, 5, 6, 7, 8, 9, 10, 11)
+    for n, row in enumerate(order):
+        for k in range(6):
+            few_out[pl.ds(n * 6 + k, 1), :] = sums[pl.ds(row, 1), pl.ds(k * 128, 128)]
+    lane = lax.broadcasted_iota(jnp.int32, (SEG, 128), 1) // HEAD_DIM
     for axis in range(2):
-        total = jnp.zeros((SEG, D), F32)
+        total = jnp.zeros((SEG, 128), F32)
         for h in range(HEADS):
-            total = total + jnp.where(lane == h, rel_acc[pl.ds(axis * 384 + h * SEG, SEG), :], 0.0)
-        rel_ref[axis] = total
-
-
-def attention_back(qkv, do, rel_cols, bias_v, e, p):
+            piece = acc[pl.ds(axis * 384 + h * SEG, SEG), pl.ds((h // 2) * 128, 128)]
+            total = total + jnp.where(lane == h % 2, piece, 0.0)
+        few_out[pl.ds(72 + axis * SEG, SEG), :] = total
+
+    if direct:
+        steps = (red.to_s, red.to_x, red.to_y, (f, ctx + 1 - 2 * (ctx % 2), tp), (f, (ctx + 2) % 4, tp))
+
+        def few_copy(n):
+            return remote(few_in.at[5 + n], few_in.at[n], steps[n], few_s.at[n], few_r.at[n])
+
+        def few_start(n):
+            few_in[5 + n] = few_out[...]
+            few_copy(n).start()
+
+        def few_add(n):
+            few_copy(n).wait_recv()
+            few_out[...] = few_out[...] + few_in[n]
+
+        few_start(0)
+        for w in (2, 3, 4, 5):
+            red.x_add(w, 0)
+            red.x_add(w, 1)
+        red.z_out(1)
+        red.z_mid(0)
+        few_add(0)
+        few_start(1)
+        for w in (2, 3, 4, 5):
+            red.y_add(w)
+        few_add(1)
+        few_start(2)
+        for w in (2, 3, 4, 5):
+            red.z_mid(w)
+        few_add(2)
+        few_start(3)
+        for w in (0, 2, 3, 4, 5):
+            red.z_out(w)
+        few_add(3)
+        few_start(4)
+        for w in (1, 0, 2, 3, 4, 5):
+            red.z_end(w)
+        few_add(4)
+        for w in range(6):
+            red.sent(w)
+        for n in range(5):
+            few_copy(n).wait_send()
+    else:
+        for n, src in enumerate((wu, wd, wp, dwq.at[0], dwq.at[1], dwq.at[2])):
+            cp = pltpu.make_async_copy(src, outs[n], ls.at[n])
+            cp.start()
+            cp.wait()
+    tokens_done(0, dg)
+    tokens_done(1, cot)
+
+
+def backward(inputs, vec, images, direct):
+    any_spec = pl.BlockSpec(memory_space=pl.ANY)
     vmem = pl.BlockSpec(memory_space=pltpu.VMEM)
+    dma = pltpu.SemaphoreType.DMA
+    shape = jax.ShapeDtypeStruct
+    n_places = NFULL * PAIRS + NPART * (4 + PAIRS)
+    wholes = ((4 * D, D), (4 * D, D), (D, D), (D, D), (D, D), (D, D))
+    out_shape = [shape((2, images, 2, PIECE, D), BF), shape((FEW, 128), F32)]
+    out_shape += [shape(s, BF) for s in (HALVES if direct else wholes)]
+    v = pltpu.VMEM
+    scratch = [v((ROWS, D), BF)] * 6 + [v((ROWS, D), F32)] * 2
+    scratch += [
+        v((4 * D, D), BF), v((4 * D, D), BF), v((D, D), BF), v((3, D, D), BF), v((3, D, D), BF),
+        v((ROWS, 3 * D), BF), v((2, FULL, HEADS * 256), BF), v((1 + NPART, 4, FULL, 256), BF), v((D, D), BF),
+        v((FULL, D), BF), v((FULL, D), F32),
+        v((1, D), F32), v((1, D), F32), v((SUMS, D), F32), v((ROWS, 1), F32), v((ROWS, 1), F32),
+        dma((15,)), dma((2, n_places)), dma((2, images, 2, 5)),
+    ]
+    if direct:
+        scratch += [v((2, D, D), BF), v((2, D, D), BF), v((2, 192, D), BF)]
+        scratch += [v((2,) + s, BF) for s in HALVES]
+        scratch += [v(s, BF) for s in HALVES]
+        scratch += [v((2,) + s, BF) for s in HALVES]
+        scratch += [v((10, FEW, 128), F32)]
+        scratch += [dma((6, 2)), dma((6, 2)), dma((6, 2)), dma((6, 2)), dma((6,)), dma((6,)), dma((6, 2)), dma((6, 3)), dma((6,))]
+        scratch += [dma((5,)), dma((5,))]
     return pl.pallas_call(
-        attention_back_kernel,
-        out_shape=[
-            jax.ShapeDtypeStruct((ROWS, 3 * D), BF),
-            jax.ShapeDtypeStruct((1, D), F32),
-            jax.ShapeDtypeStruct((2, SEG, D), F32),
-        ],
-        in_specs=[vmem] * 6,
-        out_specs=[vmem] * 3,
-        scratch_shapes=[
-            pltpu.VMEM((FULL, D), BF),
-            pltpu.VMEM((FULL, D), F32),
-            pltpu.VMEM((D, D), F32),
-        ],
+        functools.partial(backward_kernel, images, direct),
+        out_shape=out_shape,
+        in_specs=[any_spec] * len(inputs) + [vmem],
+        out_specs=[any_spec, vmem] + [any_spec] * 6,
+        scratch_shapes=scratch,
+        compiler_params=pltpu.CompilerParams(
+            collective_id=1, has_side_effects=True, vmem_limit_bytes=VMEM_BACK
+        ),
+        name="backward",
+    )(*inputs, vec)
+
+
+def results_kernel(images, staged, *refs):
+    n = (len(refs) - 2) // 2
+    grads, outs = refs[:n], refs[n + 2:]
+    unpack = pack_matrix()
+    for a in range(2):
+        for i in range(images):
+            for u in range(2):
+                refs[n + a][i, pl.ds(u * 128, 128)] = tn(unpack, staged[a, i, u]).astype(BF)
+    for src, dst in zip(grads, outs):
+        rows = src.shape[0]
+
+        @pl.loop(0, rows // 64)
+        def _(k, src=src, dst=dst):
+            here = pl.ds(pl.multiple_of(k * 64, 16), 64)
+            dst[here] = src[here].astype(F32)
+
+
+def results(staged, grads):
+    images = staged.shape[1]
+    vmem = pl.BlockSpec(memory_space=pltpu.VMEM)
+    tokens = jax.ShapeDtypeStruct((images, 256, D), BF)
+    outs = [tokens, tokens] + [jax.ShapeDtypeStruct(g.shape, F32) for g in grads]
+    return pl.pallas_call(
+        functools.partial(results_kernel, images),
+        out_shape=outs,
+        in_specs=[vmem] * (1 + len(grads)),
+        out_specs=[vmem] * len(outs),
         compiler_params=pltpu.CompilerParams(vmem_limit_bytes=VMEM_LIMIT),
-        name="attention_backward",
-    )(qkv, do, rel_cols, bias_v, e, p)
-
-
-def real_rows():
-    _, ctx, tp = coords()
-    r = jnp.arange(FULL)
-    real = [(r % 16) < WIN] * NFULL
-    for k in range(NPART):
-        q = (3 - ctx) * 8 + tp * 2 + k
-        bottom = q < 15
-        corner = bottom & (q % 5 == 4)
-        right = (q >= 15) & (q < 27)
-        rp = r[:PART]
-        real.append(
-            jnp.where(corner, rp < 64, jnp.where(right, rp < 112, bottom & (rp % 16 < WIN)))
-        )
-    return jnp.concatenate(real)[:, None]
-
-
-def norm_stats(v):
-    mean = jnp.mean(v, axis=-1, keepdims=True)
-    centered = v - mean
-    r = lax.rsqrt(jnp.mean(centered * centered, axis=-1, keepdims=True) + EPSILON)
-    return centered * r, r
-
-
-def norm_back(n, xhat, r, gain):
-    m = n * gain
-    return r * (m - jnp.mean(m, -1, keepdims=True) - xhat * jnp.mean(m * xhat, -1, keepdims=True))
+        name="results",
+    )(staged, *grads)
 
 
 def gelu_both(u):
@@ -967,10 +1171,6 @@
     return u * phi, phi + u * e * (1.0 / math.sqrt(2 * math.pi))
 
 
-def mm(a, b, dims="mk,kn->mn"):
-    return jnp.einsum(dims, a, b, preferred_element_type=F32)
-
-
 def whole_weights(shards):
     wq, wp, wu, wd = shards
     wq = lax.all_gather(lax.all_gather(wq, "fsdp", axis=2, tiled=True), "tp", axis=1, tiled=True)
@@ -981,11 +1181,10 @@
 
 
 def summed_weights(grads):
-    dims = ((1, 2), (0, 1), (1, 0), (0, 1))
     out = []
-    for grad, (t_dim, f_dim) in zip(grads, dims):
-        part = lax.psum_scatter(grad, "tp", scatter_dimension=t_dim, tiled=True)
-        part = lax.psum_scatter(part, "fsdp", scatter_dimension=f_dim, tiled=True)
+    for w, grad in enumerate(grads):
+        part = lax.psum_scatter(grad, "tp", scatter_dimension=0, tiled=True)
+        part = lax.psum_scatter(part, "fsdp", scatter_dimension=0 if w == 0 else 1, tiled=True)
         out.append(lax.psum(part, "ctx").astype(F32))
     return out
 
@@ -999,70 +1198,30 @@
     zero = jnp.zeros_like(ln1_gain)
     bias_row = jnp.concatenate([qkv_bias[0], zero, qkv_bias[1]])
     vec = jnp.stack([jnp.tile(ln1_gain, 3), jnp.tile(ln1_bias, 3), bias_row]).astype(F32)
+    vec_back = jnp.stack(
+        [ln1_gain, ln2_gain, ln2_bias, proj_bias, down_bias, qkv_bias[1]]
+        + list(up_bias.reshape(4, D)) + [zero] * 6
+    ).astype(F32)
     rel = jnp.pad(jnp.stack([rel_h, rel_w]), ((0, 0), (0, SEG - rel_h.shape[0]), (0, 0)))
     if direct:
-        x_low, cot_low, n1, qkv, attended, probs, wq, wp, wu, wd, e, rel_cols = forward(x3, c3, shards, None, vec, rel)
+        x, cot, n1, qkv, att, probs, wq, wp, wu, wd, e, rel_cols = forward(x3, c3, shards, None, vec, rel)
     else:
         wq, wp, wu, wd = whole_weights(shards)
-        x_low, cot_low, n1, qkv, attended, probs, e, rel_cols = forward(x3, c3, None, wq, vec, rel)
-    wq = wq.reshape(3 * D, D)
-    real = real_rows()
-    g1, g2, b2 = (v.astype(F32) for v in (ln1_gain, ln2_gain, ln2_bias))
-    x, cot = x_low.astype(F32), cot_low.astype(F32)
-    xhat1, r1 = norm_stats(x)
-    middle = x + mm(attended, wp) + proj_bias.astype(F32)
-    xhat2, r2 = norm_stats(middle)
-    n2 = (xhat2 * g2 + b2).astype(BF)
-    gate_in = mm(n2, wu) + up_bias.astype(F32)
-    hidden, slope = gelu_both(gate_in)
-    hidden = hidden.astype(BF)
-    out = (middle + mm(hidden, wd) + down_bias.astype(F32)).astype(BF)
-
-    d_down_bias = jnp.sum(cot, axis=0)
-    d_wd = mm(hidden, cot_low, "km,kn->mn").astype(BF)
-    d_gate = (mm(cot_low, wd, "mk,nk->mn") * slope).astype(BF)
-    d_wu = mm(n2, d_gate, "km,kn->mn").astype(BF)
-    d_up_bias = jnp.sum(d_gate, axis=0, dtype=F32)
-    d_n2 = mm(d_gate, wu, "mk,nk->mn")
-    d_g2 = jnp.sum(d_n2 * xhat2, axis=0)
-    d_b2 = jnp.sum(d_n2, axis=0)
-    d_middle = cot + norm_back(d_n2, xhat2, r2, g2)
-    branch = d_middle.astype(BF)
-    d_proj_bias = jnp.sum(branch, axis=0, dtype=F32)
-    d_wp = mm(attended, branch, "km,kn->mn").astype(BF)
-    d_att = mm(branch, wp, "mk,nk->mn").astype(BF)
-    dqkv, d_pad, d_rel = attention_back(qkv, d_att, rel_cols, qkv_bias[1:2].astype(F32), e, probs)
-    d_wq = mm(dqkv, n1, "km,kn->mn").astype(BF).reshape(3, D, D)
-    sums = jnp.sum(dqkv, axis=0, dtype=F32)
-    d_n1 = mm(dqkv, wq)
-    d_g1 = jnp.sum(jnp.where(real, d_n1 * xhat1, 0.0), axis=0)
-    d_b1 = jnp.sum(jnp.where(real, d_n1, 0.0), axis=0)
-    d_x = (d_middle + norm_back(d_n1, xhat1, r1, g1)).astype(BF)
-    d_rel = d_rel.reshape(2, SEG, HEADS, HEAD_DIM).sum(axis=2)[:, :27][:, ::-1]
-
-    few = (d_g1, d_b1, sums[:D], sums[2 * D:] + d_pad[0], d_rel.reshape(-1), d_proj_bias, d_g2, d_b2, d_up_bias, d_down_bias)
-    sizes = [v.shape[0] for v in few]
-    flat = jnp.concatenate(few)
-    pad = -flat.shape[0] % 1024
-    flat = jnp.pad(flat, (0, pad)).reshape(-1, 128)
-    grads = (d_wq, d_wp, d_wu, d_wd)
-    if direct:
-        out3, dx3, oq, op, ou, od, flat = send_back(out, d_x, images, grads, flat)
+        wu = jnp.swapaxes(wu.reshape(D, 4, D), 0, 1).reshape(4 * D, D)
+        x, cot, n1, qkv, att, probs, e, rel_cols = forward(x3, c3, None, wq, vec, rel)
+    staged, few, *grads = backward((x, cot, n1, qkv, att, probs, wq, wp, wu, wd, e, rel_cols), vec_back, images, direct)
+    if direct:
+        out3, dx3, ou, od, op, oq, ok, ov = results(staged, grads)
     else:
-        out3, dx3 = send_back(out, d_x, images)
-        oq, op, ou, od = summed_weights(grads)
-        flat = lax.psum(flat, ("fsdp", "ctx", "tp"))
-    flat = flat.reshape(-1)
-    parts, at = [], 0
-    for size in sizes:
-        parts.append(flat[at:at + size])
-        at += size
-    s_g1, s_b1, s_q, s_v, s_rel, s_proj, s_g2, s_b2, s_up, s_down = parts
-    s_rel = s_rel.reshape(2, 27, HEAD_DIM)
+        out3, dx3 = results(staged, ())
+        ou, od, op, oq, ok, ov = summed_weights(grads)
+        few = lax.psum(few, ("fsdp", "ctx", "tp"))
+    rows = few[:72].reshape(12, D)
+    rel_sum = few[72:].reshape(2, SEG, 2, HEAD_DIM).sum(axis=2)[:, :27][:, ::-1]
     return (
-        jnp.transpose(out3, (1, 0, 2)), jnp.transpose(dx3, (1, 0, 2)), s_g1, s_b1,
-        jnp.transpose(oq, (0, 2, 1)), jnp.stack([s_q, s_v]), s_rel[0], s_rel[1],
-        op, s_proj, s_g2, s_b2, ou, s_up, od, s_down,
+        jnp.transpose(out3, (1, 0, 2)), jnp.transpose(dx3, (1, 0, 2)), rows[0], rows[1],
+        jnp.transpose(jnp.stack([oq, ok, ov]), (0, 2, 1)), rows[2:4], rel_sum[0], rel_sum[1],
+        op, rows[4], rows[5], rows[6], ou, rows[8:].reshape(4 * D), od, rows[7],
     )
 
 

time: 424 us -> 317 us (0.75)
  the two profiles are of different devices: /device:TPU:14 before, /device:TPU:0 now
where the time goes in v3:
time: 317 us; the launch traced here: 313 us
  Pallas kernels  295 us (93%)
  local copies, waits for them, and re-layouts  12 us (4%)
  other arithmetic  4.8 us (2%)
    pallas_call x1, Pallas kernels, backward(): pl.pallas_call(functools.partial(backward_kernel, images, direct), out_sh...  199 us
    pallas_call x1, Pallas kernels, forward(): pl.pallas_call(functools.partial(forward_kernel, images, direct), out_sha...  89.6 us

profile of v3, /device:TPU:0, one launch (start us, length us, event | category | flops | bytes accessed | tf_op | source)
XLA Modules:
  0.0 312.5 jit_solution(17461116369715983089)
XLA Ops:
  0.6 0.0 copy-start
  0.7 0.7 stack.56
  1.4 0.7 stack.54
  2.0 0.7 stack.55
  2.7 0.7 stack.57
  3.4 0.7 tile.16
  4.1 0.0 copy-done
  4.1 0.7 broadcast_bitcast_fusion.1
  4.8 0.8 slice_reduce_fusion
  5.7 0.8 fusion.4
  6.5 0.1 stack.60
  6.6 0.7 maximum_convert_fusion.refs_6_
  7.2 1.3 fusion.2.refs_7_
  8.6 0.6 convert_element_type.9.refs_12_
  9.2 89.6 %forward_attention.1 = (bf16[928,768]{1,0:T(8,128)(2,1)}, bf16[928,768]{1,0:T(8,128)(2,1)}, bf16[928,768]{1,0:T(8,128)(2,1)}, bf16[928,2304]{1,0:T(8,128)(2,1)},...) custom-call(bf16[3,256,768]{2,1,0:T(8,128)(2,1)} %bitcast.36, ...), custom_call_target="tpu_custom_call" | custom-call | tf_op jit(solution)/shard_map/forward_attention/pallas_call | solution.py:514
  98.8 199.2 %backward.1 = (bf16[2,3,2,144,768]{4,3,2,1,0:T(8,128)(2,1)}, f32[136,128]{1,0:T(8,128)}, bf16[384,768]{1,0:T(8,128)(2,1)}, bf16[768,384]{1,0:T(8,128)(2,1)}, bf1...) custom-call(bf16[928,768]{1,0:T(8,128)(2,1)} %get-tuple-element.44.refs_0, ...), custom_call_target="tpu_custom_call" | custom-call | tf_op jit(solution)/shard_map/backward/pallas_call | solution.py:1119
  298.0 0.7 slice.76
  298.7 0.6 slice.77
  299.3 1.3 slice_bitcast_fusion
  300.6 1.4 slice_bitcast_fusion.1
  302.0 0.8 slice.78
  302.8 0.1 reshape.61
  302.9 0.1 reduce_sum.9
  303.0 0.6 slice.82
  303.6 0.6 slice.80
  304.2 5.9 %results.1 = (bf16[3,256,768]{2,1,0:T(8,128)(2,1)}, bf16[3,256,768]{2,1,0:T(8,128)(2,1)}, f32[384,768]{1,0:T(8,128)}, f32[768,384]{1,0:T(8,128)}, f32[192,384]{1...) custom-call(bf16[2,3,2,144,768]{4,3,2,1,0:T(8,128)(2,1)} %get-tuple-element.56.staged, ...), custom_call_target="tpu_custom_call" | custom-call | tf_op jit(solution)/shard_map/results/pallas_call | solution.py:1154
  310.2 2.1 maximum_bitcast_fusion
  (13 shorter events, 0.1 us)
Async XLA Ops:
  0.6 3.5 %copy-start = (bf16[768]{0:T(1024)(128)(2,1)S(1)}, bf16[768]{0:T(1024)(128)(2,1)}, u32[]{:S(2)}) copy-start(bf16[768]{0:T(1024)(128)(2,1)} %param.18) | copy-start | bytes 4612

commit v4 on v3

v4 whole, which is shorter than its diff:
```python
import functools
import math

import jax
import jax.numpy as jnp
from jax import lax
from jax.experimental import pallas as pl
from jax.experimental.pallas import tpu as pltpu
from jax.sharding import PartitionSpec as P

HEAD_DIM = 64
HEADS = 12
WIN = 14
SIDE = 64
BANDS = 4
PAIRS = 7
D = 768
EPSILON = 1e-06
MESH = pl.DeviceIdType.MESH
BF = jnp.bfloat16
F32 = jnp.float32

FULL = 224
PART = 128
NFULL = 3
NPART = 2
PBASE = NFULL * FULL
ROWS = PBASE + NPART * PART
PIECE = 144
HALF_HEADS = 6
HALF = HALF_HEADS * HEAD_DIM
RELS = 2 * WIN - 1
SEG = 32
MASKED = -1e9
VMEM_LIMIT = 60 * 2**20
VMEM_BACK = 63 * 2**20


def coords():
    return lax.axis_index("fsdp"), lax.axis_index("ctx"), lax.axis_index("tp")


def part_kind(ctx, tp, k, images):
    return (3 - ctx) * 8 + tp * 2 + k


def pack_matrix():
    row = lax.broadcasted_iota(jnp.int32, (PIECE, 128), 0)
    col = lax.broadcasted_iota(jnp.int32, (PIECE, 128), 1)
    wide = row < 128
    c = jnp.where(wide, row // 32, 4)
    u = jnp.where(wide, (row % 32) // 16, (row - 128) // 8)
    b = jnp.where(wide, row % 16, (row - 128) % 8)
    source = u * SIDE + c * WIN + b
    return ((source == col) & (b < WIN)).astype(BF)


def piece_places(ctx, tp, images):
    dev = ctx * 4 + tp
    out = []
    for i in range(images):
        for u in range(2):
            m = dev * 2 + u
            band = m // PAIRS
            p = m % PAIRS
            low = band == BANDS
            for c in range(5):
                q_low = i * 5 + c
                if c < 4:
                    f = i * 4 + c
                    d_ctx = jnp.where(low, 3 - q_low // 8, band)
                    d_tp = jnp.where(low, (q_low % 8) // 2, f // 3)
                    slot = jnp.where(low, NFULL + q_low % 2, f % 3)
                    d_row = jnp.where(low, PBASE + (q_low % 2) * PART, (f % 3) * FULL) + p * 32
                    out.append((i, u, c, d_ctx, d_tp, d_row, slot, p))
                else:
                    q = jnp.where(low, q_low, 15 + (3 - band) * 3 + i)
                    d_ctx = 3 - q // 8
                    d_tp = (q % 8) // 2
                    d_row = PBASE + (q % 2) * PART + p * 16
                    out.append((i, u, c, d_ctx, d_tp, d_row, NFULL + q % 2, p))
    return out


def window_places(ctx, tp):
    out = []
    for k in range(NFULL):
        f = tp * 3 + k
        for p in range(PAIRS):
            m = ctx * PAIRS + p
            dev = m // 2
            out.append((k, p, 32, None, f // 4, m % 2, f % 4, dev // 4, dev % 4, k * FULL + p * 32))
    for k in range(NPART):
        q = (3 - ctx) * 8 + tp * 2 + k
        bottom = q < 15
        corner = bottom & (q % 5 == 4)
        right = (q >= 15) & (q < 27)
        qr = jnp.where(right, q - 15, 0)
        band = jnp.where(bottom, BANDS, 3 - qr // 3)
        image = jnp.where(bottom, q // 5, qr % 3)
        base = PBASE + k * PART
        for p in range(PAIRS):
            m = band * PAIRS + p
            dev = jnp.minimum(m // 2, 15)
            place = (image, m % 2, dev // 4, dev % 4)
            if p < 4:
                wide = bottom & jnp.logical_not(corner)
                out.append((NFULL + k, p, 32, wide, image, m % 2, q % 5, dev // 4, dev % 4, base + p * 32))
            narrow = (corner | right) if p < 4 else right
            out.append((NFULL + k, p, 16, narrow, image, m % 2, 4, dev // 4, dev % 4, base + p * 16))
    return out


def group_barrier(extra=()):
    f, c, t = coords()
    sem = pltpu.get_barrier_semaphore()
    count = 0
    for dc in range(4):
        for dt in range(4):
            if dc == 0 and dt == 0:
                continue
            pl.semaphore_signal(sem, inc=1, device_id=(f, (c + dc) % 4, (t + dt) % 4), device_id_type=MESH)
            count += 1
    for dest in extra:
        pl.semaphore_signal(sem, inc=1, device_id=dest, device_id_type=MESH)
        count += 1
    pl.semaphore_wait(sem, count)


def send_or_copy(src, dst, dest, me, send_sem, recv_sem):
    (d_ctx, d_tp), (f, ctx, tp) = dest, me
    here = (d_ctx == ctx) & (d_tp == tp)

    @pl.when(here)
    def _():
        pltpu.make_async_copy(src, dst, recv_sem).start()

    @pl.when(jnp.logical_not(here))
    def _():
        pltpu.make_async_remote_copy(
            src_ref=src, dst_ref=dst, send_sem=send_sem, recv_sem=recv_sem,
            device_id=(f, d_ctx, d_tp), device_id_type=MESH,
        ).start()


def wait_sent(src, dest, me, send_sem):
    (d_ctx, d_tp), (f, ctx, tp) = dest, me
    away = jnp.logical_not((d_ctx == ctx) & (d_tp == tp))

    @pl.when(away)
    def _():
        pltpu.make_async_copy(src, src, send_sem).wait()


def start_pieces(stage, out, a, images, me, ss, rs):
    _, ctx, tp = me
    for n, (i, u, c, d_ctx, d_tp, d_row, slot, p) in enumerate(piece_places(ctx, tp, images)):
        rows = 32 if c < 4 else 16
        src = stage.at[a, i, u, pl.ds(c * 32, rows)]
        dst = out.at[pl.ds(pl.multiple_of(d_row, 16), rows)]
        send_or_copy(src, dst, (d_ctx, d_tp), me, ss.at[a, n], rs.at[a, slot, p])


def finish_piece_sends(stage, a, images, me, ss):
    _, ctx, tp = me
    for n, (i, u, c, d_ctx, d_tp, d_row, slot, p) in enumerate(piece_places(ctx, tp, images)):
        rows = 32 if c < 4 else 16
        wait_sent(stage.at[a, i, u, pl.ds(c * 32, rows)], (d_ctx, d_tp), me, ss.at[a, n])


def wait_pieces(out, a, me, rs):
    _, ctx, tp = me
    for slot, p, rows, exists, *_rest, row in window_places(ctx, tp):
        dst = out.at[pl.ds(row, rows)]
        wait = pltpu.make_async_copy(dst, dst, rs.at[a, slot, p]).wait
        if exists is None:
            wait()
        else:
            pl.when(exists)(wait)


UNITS = 6
BLOCKS = ((192, 384), (192, 384), (192, 384), (192, 384), (384, 768), (768, 384))
Z_UNITS = (4, 5)


def block(ref, w, t, f, part=None):
    rows, cols = BLOCKS[w]
    start, size = part if part is not None else (0, rows)
    if w == 4:
        return ref.at[pl.ds(pl.multiple_of(t * D + f * rows + start, 16), size)]
    return ref.at[
        pl.ds(pl.multiple_of(t * rows + start, 16), size),
        pl.ds(pl.multiple_of(f * cols, 128), cols),
    ]


def remote(src, dst, dest, send_sem, recv_sem):
    return pltpu.make_async_remote_copy(
        src_ref=src, dst_ref=dst, send_sem=send_sem, recv_sem=recv_sem, device_id=dest, device_id_type=MESH
    )


class Gather:
    def __init__(self, shards, wholes, me, ss, rs, ls):
        self.shards, self.wholes = shards, wholes
        self.ss, self.rs, self.ls = ss, rs, ls
        f, c, t = me
        self.me = me
        self.g, self.y, self.s = 1 - f, (t + 2) % 4, t + 1 - 2 * (t % 2)
        self.to_x, self.to_y, self.to_s = (self.g, c, t), (f, c, self.y), (f, c, self.s)
        self.to_z = (f, c + 1 - 2 * (c % 2), t)
        self.parity = c % 2

    def copies(self, w):
        return range(13) if w in Z_UNITS else range(7)

    def part(self, w, theirs=False):
        if w not in Z_UNITS:
            return None
        half = BLOCKS[w][0] // 2
        return ((1 - self.parity if theirs else self.parity) * half, half)

    def own(self, w, part):
        if part is None:
            return self.shards[w]
        return self.shards[w].at[pl.ds(pl.multiple_of(part[0], 16), part[1])]

    def copy(self, w, k):
        f, _, t = self.me
        g, y = self.g, self.y
        whole = self.wholes[w]
        part, other = self.part(w), self.part(w, True)
        if k < 3:
            part = None if k == 2 else part
            src, dst = self.own(w, part), block(whole, w, t, f, part)
            dest = (self.to_x, self.to_y, self.to_s)[k]
        else:
            src = dst = block(whole, w, *(
                (y, f, part), (t, g, part), (y, f, part), (y, g, part),
                (t, g, part), (y, f, part), (y, g, part), (t, g, other), (y, f, other), (y, g, other),
            )[k - 3])
            dest = (self.to_x,) + (self.to_s,) * 3 + (self.to_z,) * 3 + (self.to_s,) * 3
            dest = dest[k - 3]
        return remote(src, dst, dest, self.ss.at[w, k], self.rs.at[w, k])

    def landed(self, w, k):
        f, _, t = self.me
        g, y, s = self.g, self.y, self.s
        sy = (s + 2) % 4
        part, other = self.part(w), self.part(w, True)
        place = (
            (t, g, part), (y, f, part), (s, f), (y, g, part), (s, g, part), (sy, f, part), (sy, g, part),
            (t, g, other), (y, f, other), (y, g, other), (s, g, other), (sy, f, other), (sy, g, other),
        )[k]
        return block(self.wholes[w], w, *place)

    def wait_recv(self, w, k):
        dst = self.landed(w, k)
        pltpu.make_async_copy(dst, dst, self.rs.at[w, k]).wait()

    def start_own(self, w, ks=(0, 1, 2)):
        f, _, t = self.me
        for k in ks:
            self.copy(w, k).start()
        if 2 in ks:
            pltpu.make_async_copy(self.shards[w], block(self.wholes[w], w, t, f), self.ls.at[w]).start()

    def on(self, w, arrived, sends):
        self.wait_recv(w, arrived)
        for k in sends:
            if k in self.copies(w):
                self.copy(w, k).start()

    def forward_x(self, w):
        self.on(w, 0, (7, 4))

    def forward_y(self, w):
        self.on(w, 1, (3, 8, 5))

    def forward_second(self, w):
        self.on(w, 3, (9, 6))

    def forward_z(self, w):
        for k in range(3):
            self.on(w, 7 + k, (10 + k,))

    def arrived(self, w, ks=(2, 4, 5, 6, 10, 11, 12)):
        f, _, t = self.me
        for k in ks:
            if k in self.copies(w):
                self.wait_recv(w, k)
        if 2 in ks:
            pltpu.make_async_copy(self.shards[w], block(self.wholes[w], w, t, f), self.ls.at[w]).wait()

    def sent(self, w):
        for k in self.copies(w):
            self.copy(w, k).wait_send()


def part_facts(k):
    _, ctx, tp = coords()
    q = (3 - ctx) * 8 + tp * 2 + k
    bottom = q < 15
    corner = bottom & (q % 5 == 4)
    right = (q >= 15) & (q < 27)
    return bottom, corner, right


def row_real(slot, rows):
    r = lax.broadcasted_iota(jnp.int32, (rows, 1), 0)
    wide = (r % 16) < WIN
    if slot < NFULL:
        return wide
    bottom, corner, right = part_facts(slot - NFULL)
    limit = jnp.where(corner, 64, jnp.where(right, 112, jnp.where(bottom, PART, 0)))
    narrow = jnp.where(corner | right, 1, 0)
    return (r < limit) & (wide | (narrow > 0))


def key_places(kind, shape):
    r = lax.broadcasted_iota(jnp.int32, shape, 0)
    a, b = r // 16, r % 16
    if kind == 0:
        return a, b
    _, corner, right = part_facts(kind - 1)
    corner, right = jnp.where(corner, 1, 0), jnp.where(right, 1, 0)
    a_right = jnp.where(r < 112, r // 8, (r - 112) // 8)
    b_right = jnp.where(r < 112, r % 8, 8 + (r - 112) % 8)
    a_corner = jnp.where(r < 64, r // 8, jnp.where(r < 128, (r - 64) // 8, 8 + (r - 128) // 16))
    b_corner = jnp.where(r < 64, r % 8, jnp.where(r < 128, 8 + (r - 64) % 8, (r - 128) % 16))
    a = jnp.where(corner > 0, a_corner, jnp.where(right > 0, a_right, a))
    b = jnp.where(corner > 0, b_corner, jnp.where(right > 0, b_right, b))
    return a, b


def build_keys(e_ref):
    shape = (FULL, 128)
    col = lax.broadcasted_iota(jnp.int32, shape, 1)
    j = col % 16
    for kind in range(1 + NPART):
        a, b = key_places(kind, shape)
        ok = b < WIN
        along_a = jnp.where(ok & (j == a) & (j < WIN), 1.0, 0.0)
        along_a = jnp.where(jnp.logical_not(ok) & (col % SEG == 15), MASKED, along_a)
        along_b = jnp.where(ok & (j == b) & (j < WIN), 1.0, 0.0)
        for head in range(3):
            mine = col // SEG == head
            e_ref[kind, head, :, pl.ds(0, 128)] = jnp.where(mine, along_a, 0.0).astype(BF)
            e_ref[kind, head, :, pl.ds(128, 128)] = jnp.where(mine, along_b, 0.0).astype(BF)


def build_relative(rel_refs, out_ref):
    out_ref[...] = jnp.zeros(out_ref.shape, BF)
    i = lax.broadcasted_iota(jnp.int32, (RELS, 128), 0)
    lane = lax.broadcasted_iota(jnp.int32, (RELS, 128), 1)
    turn = (lane % SEG == 26 - i).astype(BF)
    lane64 = lax.broadcasted_iota(jnp.int32, (HEAD_DIM, 128), 1) // SEG
    for axis in range(2):
        rev = tn(rel_refs[axis][...], turn)
        for h in range(HALF_HEADS):
            out_ref[pl.ds(h * HEAD_DIM, HEAD_DIM), pl.ds((h // 3) * 256 + axis * 128, 128)] = (
                jnp.where(lane64 == h % 3, rev, 0.0).astype(BF)
            )


def slots():
    return [(k, k * FULL, FULL) for k in range(NFULL)] + [
        (NFULL + k, PBASE + k * PART, PART) for k in range(NPART)
    ]


def half_cols(start, half):
    return pl.ds(pl.multiple_of(start + half * HALF, 128), HALF)


def norm(rows):
    centered = rows - jnp.mean(rows, axis=-1, keepdims=True)
    r = lax.rsqrt(jnp.mean(centered * centered, axis=-1, keepdims=True) + EPSILON)
    return centered * r, r


def forward_kernel(images, direct, *refs):
    it = iter(refs)

    def take(n):
        return [next(it) for _ in range(n)]

    x_ref, c_ref = take(2)
    weights = take(4 if direct else 2)
    g1_ref, b1_ref, qkv_b, g2_ref, b2_ref, pb_ref, db_ref, relh_ref, relw_ref = take(9)
    x_o, c_o, n1_o, qkv_o, att_o, p_o, mid_o, xhat_o, n2_o, r2_o = take(10)
    if direct:
        wq_o, wp_o, wu, wd = take(4)
    e_o, rel_o = take(2)
    stage, xw, cw, n1, qkv, att, p_buf, mid, xhat2, n2, r2 = take(11)
    wq, wp, e, rel_blk, x_scr, bias_v, vec, ss, rs = take(9)
    if direct:
        gss, grs, gls = take(3)
    os, = take(1)
    me = coords()
    f, ctx, tp = me
    pack = pack_matrix()

    def stage_tokens(a, src):
        for i in range(images):
            for u in range(2):
                stage[a, i, u] = jnp.dot(
                    pack, src[i, pl.ds(u * 128, 128)], preferred_element_type=F32
                ).astype(BF)

    out_copies = []

    def write(src, dst):
        cp = pltpu.make_async_copy(src, dst, os.at[len(out_copies)])
        cp.start()
        out_copies.append(cp)

    stage_tokens(0, x_ref)
    group_barrier(((1 - f, ctx, tp),) if direct else ())
    start_pieces(stage, xw, 0, images, me, ss, rs)
    if direct:
        wq_s, wp_s, wu_s, wd_s = weights
        shards = (wq_s.at[0], wq_s.at[1], wq_s.at[2], wp_s, wu_s, wd_s)
        gather = Gather(shards, (wq.at[0], wq.at[1], wq.at[2], wp, wu, wd), me, gss, grs, gls)
        for w in range(3):
            gather.start_own(w, (0, 2))
    else:
        load = (pltpu.make_async_copy(weights[0], wq, os.at[18]), pltpu.make_async_copy(weights[1], wp, os.at[19]))
        for cp in load:
            cp.start()
    build_keys(e)
    build_relative((relh_ref, relw_ref), rel_blk)
    write(e, e_o)
    write(rel_blk, rel_o)
    rows = [g1_ref[...], b1_ref[...], qkv_b[0, :], None, qkv_b[1, :], g2_ref[...], b2_ref[...], pb_ref[...], db_ref[...]]
    for n, row in enumerate(rows):
        vec[n:n + 1, :] = jnp.zeros((1, D), F32) if row is None else row.astype(F32).reshape(1, D)
    bias_v[...] = vec[4:5, :]
    stage_tokens(1, c_ref)
    if direct:
        for w in range(3):
            gather.on(w, 0, (4,))
    wait_pieces(xw, 0, me, rs)
    if direct:
        for w in range(3):
            gather.start_own(w, (1,))
    for slot, base, rows in slots():
        here = pl.ds(base, rows)
        real = row_real(slot, rows)
        x = jnp.where(real, xw[here].astype(F32), 0.0)
        xw[here] = x.astype(BF)
        xhat, _ = norm(x)
        n1[here] = jnp.where(real, xhat * vec[0:1, :] + vec[1:2, :], 0.0).astype(BF)
    write(xw, x_o)
    write(n1, n1_o)
    if direct:
        for w in range(3):
            gather.arrived(w, (2, 4))
        gather.start_own(4)
    else:
        for cp in load:
            cp.wait()
        start_pieces(stage, cw, 1, images, me, ss, rs)

    for turn in range(2):
        half = tp // 2 if turn == 0 else 1 - tp // 2

        @pl.loop(0, 3)
        def _(n, half=half):
            out = nt(n1[...], wq[n, half_cols(0, half), :]) + vec[pl.ds(2 + n, 1), half_cols(0, half)]
            qkv[:, half_cols(n * D, half)] = out.astype(BF)

        @pl.loop(0, NFULL)
        def _(n, half=half, turn=turn):
            attention_half(qkv, rel_blk, bias_v, e.at[0], att, p_buf, pl.multiple_of(n * FULL, 16), FULL, None, x_scr, half)
            if not direct:
                return
            if turn == 0:
                @pl.when(n == 0)
                def _():
                    for w in range(3):
                        gather.on(w, 1, (3, 5))
                    gather.start_own(3)
                    gather.start_own(5)

                @pl.when(n == 1)
                def _():
                    gather.forward_x(4)
                    start_pieces(stage, cw, 1, images, me, ss, rs)

                @pl.when(n == 2)
                def _():
                    gather.forward_y(4)
                    for w in range(3):
                        gather.on(w, 3, (6,))
            else:
                @pl.when(n == 0)
                def _():
                    gather.forward_x(3)
                    gather.forward_y(3)
                    gather.forward_x(5)

                @pl.when(n == 1)
                def _():
                    gather.forward_y(5)
                    gather.forward_second(4)

                @pl.when(n == 2)
                def _():
                    gather.forward_second(3)

        @pl.loop(0, NPART)
        def _(n, half=half):
            attention_half(qkv, rel_blk, bias_v, e.at[1 + n], att, p_buf,
                           pl.multiple_of(PBASE + n * PART, 16), PART, narrow_flag(n), x_scr, half)

        if direct:
            if turn == 0:
                for w in range(3):
                    gather.arrived(w, (5, 6))
                write(wq, wq_o)
            else:
                gather.forward_second(5)
                gather.forward_z(4)

    write(qkv, qkv_o)
    write(att, att_o)
    write(p_buf, p_o)
    if direct:
        gather.arrived(3)
        write(wp, wp_o)

    @pl.loop(0, ROWS // CHUNK)
    def _(n):
        here = pl.ds(pl.multiple_of(n * CHUNK, 16), CHUNK)
        middle = xw[here].astype(F32) + jnp.dot(att[here], wp[...], preferred_element_type=F32) + vec[7:8, :]
        xhat, r = norm(middle)
        r2[here] = r
        xhat2[here] = xhat.astype(BF)
        n2[here] = (xhat * vec[5:6, :] + vec[6:7, :]).astype(BF)
        mid[here] = middle + vec[8:9, :]

    for src, dst in ((n2, n2_o), (mid, mid_o), (xhat2, xhat_o), (r2, r2_o)):
        write(src, dst)
    if direct:
        gather.forward_z(5)
    wait_pieces(cw, 1, me, rs)
    for slot, base, rows in slots():
        here = pl.ds(base, rows)
        cw[here] = jnp.where(row_real(slot, rows), cw[here].astype(F32), 0.0).astype(BF)
    write(cw, c_o)
    if direct:
        for w in (4, 5):
            gather.arrived(w)
        for w in range(UNITS):
            gather.sent(w)
    for a in range(2):
        finish_piece_sends(stage, a, images, me, ss)
    for cp in out_copies:
        cp.wait()


def forward(x3, c3, shards, whole, small):
    images = x3.shape[0]
    any_spec = pl.BlockSpec(memory_space=pl.ANY)
    vmem = pl.BlockSpec(memory_space=pltpu.VMEM)
    direct = whole is None
    dma = pltpu.SemaphoreType.DMA
    shape = jax.ShapeDtypeStruct
    tokens = shape((ROWS, D), BF)
    keys = (1 + NPART, 3, FULL, 256)
    outs = [tokens, tokens, tokens, shape((ROWS, 3 * D), BF), tokens, shape((ROWS, HEADS * 256), BF)]
    outs += [shape((ROWS, D), F32), tokens, tokens, shape((ROWS, 1), F32)]
    if direct:
        outs += [shape(s, BF) for s in ((3, D, D), (D, D), (4 * D, D), (4 * D, D))]
    outs += [shape(keys, BF), shape((HALF, 512), BF)]
    v = pltpu.VMEM
    scratch = [v((2, images, 2, PIECE, D), BF)] + [v((ROWS, D), BF)] * 3
    scratch += [v((ROWS, 3 * D), BF), v((ROWS, D), BF), v((ROWS, HEADS * 256), BF)]
    scratch += [v((ROWS, D), F32), v((ROWS, D), BF), v((ROWS, D), BF), v((ROWS, 1), F32)]
    scratch += [v((3, D, D), BF), v((D, D), BF), v(keys, BF), v((HALF, 512), BF), v((FULL, 512), BF)]
    scratch += [v((1, D), F32), v((16, D), F32)]
    scratch += [dma((2, images * 10)), dma((2, NFULL + NPART, PAIRS))]
    if direct:
        scratch += [dma((UNITS, 13)), dma((UNITS, 13)), dma((UNITS,))]
    scratch += [dma((20,))]
    weights = list(shards) if direct else list(whole)
    return pl.pallas_call(
        functools.partial(forward_kernel, images, direct),
        out_shape=outs,
        in_specs=[vmem, vmem] + [any_spec] * len(weights) + [vmem] * len(small),
        out_specs=[any_spec] * len(outs),
        scratch_shapes=scratch,
        compiler_params=pltpu.CompilerParams(
            collective_id=0, has_side_effects=True, vmem_limit_bytes=VMEM_LIMIT
        ),
        name="forward",
    )(x3, c3, *weights, *small)


def barrel(x, shift, left):
    lanes = x.shape[-1]
    for bit in (1, 2, 4, 8):
        moved = pltpu.roll(x, lanes - bit if left else bit, 1)
        x = jnp.where((shift // bit) % 2 == 1, moved, x)
    return x


def row_places(rows, narrow):
    r = lax.broadcasted_iota(jnp.int32, (rows, 128), 0)
    if narrow is None:
        return r // 16, r % 16
    is_narrow = narrow > 0
    return jnp.where(is_narrow, r // 8, r // 16), jnp.where(is_narrow, r % 8, r % 16)


def half_mask(hh):
    lane = lax.broadcasted_iota(jnp.int32, (1, 128), 1)
    return ((lane // 64) == hh).astype(BF)


def nt(a, b):
    return lax.dot_general(a, b, (((1,), (1,)), ((), ())), preferred_element_type=F32)


def tn(a, b):
    return lax.dot_general(a, b, (((0,), (0,)), ((), ())), preferred_element_type=F32)


def key_rows(ref, base, rows, col, fill):
    part = ref[pl.ds(base, rows), pl.ds(pl.multiple_of(col, 128), 128)]
    if rows == FULL:
        return part
    return jnp.concatenate([part, jnp.broadcast_to(fill, (FULL - rows, 128)).astype(BF)], axis=0)


def attention_half(qkv, rel_blk, bias_v, e_at, o_ref, p_ref, base, rows, narrow, x_scr, half):
    a_row, b_row = row_places(rows, narrow)
    here = pl.ds(base, rows)
    q_all = qkv[here, half_cols(0, half)]
    lane = lax.broadcasted_iota(jnp.int32, (rows, 128), 1) % SEG
    raw = jnp.dot(q_all, rel_blk[...], preferred_element_type=F32)
    for g in range(2):
        for axis, pos in ((0, a_row), (1, b_row)):
            at = g * 256 + axis * 128
            v = barrel(raw[:, at:at + 128], jnp.maximum(13 - pos, 0), True)
            hi = v.astype(BF).astype(F32)
            lo = pltpu.roll(v - hi, 16, 1)
            mix = jnp.where(lane < WIN, hi, jnp.where(lane >= 16, lo, 0.0))
            if axis == 0:
                mix = jnp.where(lane == 15, 1.0, mix)
            x_scr[pl.ds(0, rows), pl.ds(at, 128)] = mix.astype(BF)
    for hp in range(3):
        cols = pl.ds(pl.multiple_of(half * HALF + hp * 128, 128), 128)
        q = q_all[:, hp * 128:(hp + 1) * 128]
        k = key_rows(qkv, base, rows, D + half * HALF + hp * 128, jnp.zeros((1, 128), BF))
        v = key_rows(qkv, base, rows, 2 * D + half * HALF + hp * 128, bias_v[:, cols])
        out = jnp.zeros((rows, 128), F32)
        for hh in range(2):
            h = hp * 2 + hh
            x = x_scr[pl.ds(0, rows), pl.ds((h // 3) * 256, 256)]
            s = nt(q, k * (half_mask(hh) * 0.125)) + nt(x, e_at[h % 3])
            p = jnp.exp(s - jnp.max(s, axis=-1, keepdims=True))
            p = (p * (1.0 / jnp.sum(p, axis=-1, keepdims=True))).astype(BF)
            p_ref[here, pl.ds(pl.multiple_of((half * HALF_HEADS + h) * 256, 128), FULL)] = p
            out = out + jnp.dot(p, v * half_mask(hh), preferred_element_type=F32)
        o_ref[here, cols] = out.astype(BF)


def narrow_flag(k):
    _, ctx, tp = coords()
    q = (3 - ctx) * 8 + tp * 2 + k
    is_narrow = ((q < 15) & (q % 5 == 4)) | ((q >= 15) & (q < 27))
    return jnp.where(is_narrow, 1, 0)


def attention_back_half(qkv, do_ref, rel_blk, bias_v, e_at, p_ref, d_scr, acc_scr, pad_acc, rel_acc, base, rows,
                        narrow, half):
    a_row, b_row = row_places(rows, narrow)
    here = pl.ds(base, rows)
    dx = [jnp.zeros((rows, 256), F32)] * 2
    for hp in range(3):
        cols = pl.ds(pl.multiple_of(half * HALF + hp * 128, 128), 128)
        k_at, v_at = D + half * HALF + hp * 128, 2 * D + half * HALF + hp * 128
        q = qkv[here, cols]
        k = key_rows(qkv, base, rows, k_at, jnp.zeros((1, 128), BF))
        v = key_rows(qkv, base, rows, v_at, bias_v[:, cols])
        do = do_ref[here, cols]
        dq = jnp.zeros((rows, 128), F32)
        dk = jnp.zeros((FULL, 128), F32)
        dv = jnp.zeros((FULL, 128), F32)
        for hh in range(2):
            h = hp * 2 + hh
            mask = half_mask(hh)
            do_m = do * mask
            dp = nt(do_m, v)
            p_low = p_ref[pl.ds(0, rows), pl.ds(h * 256, FULL)]
            t = p_low.astype(F32)
            tp = t * dp
            ds = (tp - t * jnp.sum(tp, axis=-1, keepdims=True)).astype(BF)
            dq = dq + jnp.dot(ds, k * (mask * 0.125), preferred_element_type=F32)
            dx[h // 3] = dx[h // 3] + jnp.dot(ds, e_at[h % 3], preferred_element_type=F32)
            dk = dk + tn(ds, q * (mask * 0.125))
            dv = dv + tn(p_low, do_m)
        acc_scr[pl.ds(0, rows), pl.ds(hp * 128, 128)] = dq
        qkv[here, pl.ds(pl.multiple_of(k_at, 128), 128)] = dk[:rows].astype(BF)
        qkv[here, pl.ds(pl.multiple_of(v_at, 128), 128)] = dv[:rows].astype(BF)
        if rows < FULL:
            pad_acc[:, cols] += jnp.sum(dv[rows:], axis=0, keepdims=True)
    lane = lax.broadcasted_iota(jnp.int32, (rows, 128), 1) % SEG
    for g in range(2):
        for axis, pos in ((0, a_row), (1, b_row)):
            v = jnp.where(lane < WIN, dx[g][:, axis * 128:(axis + 1) * 128], 0.0)
            v = barrel(v, jnp.maximum(13 - pos, 0), False)
            d_scr[pl.ds(0, rows), pl.ds(g * 256 + axis * 128, 128)] = v.astype(BF)
    d = d_scr[pl.ds(0, rows), :]
    rel_acc[pl.ds(0, 512), pl.ds(0, HALF)] += tn(d, qkv[here, half_cols(0, half)])
    qkv[here, half_cols(0, half)] = (acc_scr[pl.ds(0, rows), :] + nt(d, rel_blk[...])).astype(BF)


TILE = (D, D, 192, 192, 192, 192)
HALVES = ((384, D), (D, 384), (192, 384), (192, 384), (192, 384), (192, 384))
Z_PIECES = (2, 2, 1, 1, 1, 1)
CHUNK = ROWS // 2
SUMS = 16
FEW = 12 * 6 + 2 * SEG


def add_rows(dst, src):
    rows = dst.shape[0]
    size = 64

    @pl.loop(0, rows // size)
    def _(n):
        here = pl.ds(pl.multiple_of(n * size, 16), size)
        dst[here] = (dst[here].astype(F32) + src[here].astype(F32)).astype(BF)


class Reduce:
    def __init__(self, grads, me, outs, r1, rx, ry, rz, s1, v1, s2, v2, s3, v3, sz, vz, so):
        self.grads, self.outs = grads, outs
        self.r1u, self.r1d, self.r1p = r1
        self.rx, self.ry, self.rz = rx, ry, rz
        self.s1, self.v1, self.s2, self.v2, self.s3, self.v3 = s1, v1, s2, v2, s3, v3
        self.sz, self.vz, self.so = sz, vz, so
        f, ctx, tp = me
        self.f, self.g = f, 1 - f
        self.c, self.own = tp % 2, tp // 2
        self.to_s = (f, ctx, tp + 1 - 2 * self.c)
        self.to_x = (1 - f, ctx, tp)
        self.to_y = (f, ctx, (tp + 2) % 4)
        self.outer = (ctx == 0) | (ctx == 3)
        self.inner = jnp.logical_not(self.outer)
        self.to_mid = (f, 3 - ctx, tp)
        self.to_in = (f, jnp.where(ctx == 0, 1, 2), tp)
        self.to_out = (f, jnp.where(ctx == 1, 0, 3), tp)

    def tile(self, w, t):
        return self.grads[w].at[pl.ds(pl.multiple_of(t * TILE[w], 16), TILE[w])]

    def half(self, w, t, f):
        if w == 0:
            return self.grads[w].at[pl.ds(pl.multiple_of(t * D + f * 384, 16), 384)]
        return self.grads[w].at[
            pl.ds(pl.multiple_of(t * TILE[w], 16), TILE[w]), pl.ds(pl.multiple_of(f * 384, 128), 384)
        ]

    def landing(self, w, j):
        if w < 2:
            return (self.r1u, self.r1d)[w].at[j]
        if w == 2:
            return self.r1p.at[j]
        return self.r1d.at[(w - 3) // 2, pl.ds(pl.multiple_of(((w - 3) % 2) * 384 + j * 192, 16), 192)]

    def core_copy(self, w, j):
        src = self.tile(w, 1 - self.c + 2 * j)
        return remote(src, self.landing(w, j), self.to_s, self.s1.at[w, j], self.v1.at[w, j])

    def core_send(self, w, j):
        self.core_copy(w, j).start()

    def x_copy(self, w, j):
        src = self.half(w, self.c + 2 * j, self.g)
        return remote(src, self.rx[w].at[j], self.to_x, self.s2.at[w, j], self.v2.at[w, j])

    def core_add(self, w, j):
        self.core_copy(w, j).wait_recv()
        add_rows(self.tile(w, self.c + 2 * j), self.landing(w, j))
        self.x_copy(w, j).start()

    def y_copy(self, w):
        src = self.half(w, self.c + 2 * (1 - self.own), self.f)
        return remote(src, self.ry[w], self.to_y, self.s3.at[w], self.v3.at[w])

    def x_add(self, w, j):
        self.x_copy(w, j).wait_recv()
        add_rows(self.half(w, self.c + 2 * j, self.f), self.rx[w].at[j])

        @pl.when(self.own != j)
        def _():
            self.y_copy(w).start()

    def mine(self, w):
        return self.half(w, self.c + 2 * self.own, self.f)

    def y_add(self, w):
        self.y_copy(w).wait_recv()
        add_rows(self.mine(w), self.ry[w])

        for h in range(Z_PIECES[w]):
            self.z_in(w, h)

    def z_view(self, ref, w, h):
        size = HALVES[w][0] // Z_PIECES[w]
        return ref.at[pl.ds(h * size, size)]

    def z_mine(self, w, h):
        t, size = self.c + 2 * self.own, HALVES[w][0] // Z_PIECES[w]
        if w == 0:
            return self.grads[w].at[pl.ds(pl.multiple_of(t * D + self.f * 384 + h * size, 16), size)]
        return self.grads[w].at[
            pl.ds(pl.multiple_of(t * TILE[w] + h * size, 16), size), pl.ds(pl.multiple_of(self.f * 384, 128), 384)
        ]

    def z_slot(self, w, slot, h):
        return self.z_view(self.rz[w].at[slot], w, h)

    def z_in(self, w, h):
        @pl.when(self.outer)
        def _():
            remote(
                self.z_mine(w, h), self.z_slot(w, 0, h), self.to_in, self.sz.at[w, h, 0], self.vz.at[w, h, 0]
            ).start()

    def z_wait(self, w, h, sem):
        view = self.z_slot(w, 0, h)
        pltpu.make_async_copy(view, view, sem).wait()

    def z_mid(self, w, h):
        @pl.when(self.inner)
        def _():
            self.z_wait(w, h, self.vz.at[w, h, 0])
            mine = self.z_mine(w, h)
            add_rows(mine, self.z_slot(w, 0, h))
            remote(mine, self.z_slot(w, 1, h), self.to_mid, self.sz.at[w, h, 0], self.vz.at[w, h, 1]).start()

    def z_out(self, w, h):
        @pl.when(self.inner)
        def _():
            self.z_wait(w, h, self.vz.at[w, h, 1])
            total = self.z_slot(w, 1, h)
            add_rows(total, self.z_mine(w, h))
            remote(total, self.z_slot(w, 0, h), self.to_out, self.sz.at[w, h, 1], self.vz.at[w, h, 2]).start()
            pltpu.make_async_copy(total, self.z_view(self.outs[w], w, h), self.so.at[w, h]).start()

    def z_end(self, w, h):
        @pl.when(self.outer)
        def _():
            self.z_wait(w, h, self.vz.at[w, h, 2])
            pltpu.make_async_copy(self.z_slot(w, 0, h), self.z_view(self.outs[w], w, h), self.so.at[w, h]).start()

    def sent(self, w):
        for j in range(2):
            self.core_copy(w, j).wait_send()
            self.x_copy(w, j).wait_send()
        self.y_copy(w).wait_send()
        for h in range(Z_PIECES[w]):
            self.z_wait(w, h, self.sz.at[w, h, 0])

            @pl.when(self.inner)
            def _(h=h):
                self.z_wait(w, h, self.sz.at[w, h, 1])

            self.z_wait(w, h, self.so.at[w, h])


def backward_kernel(images, direct, *refs):
    it = iter(refs)

    def take(n):
        return [next(it) for _ in range(n)]

    x_h, c_h, n1_h, qkv_h, att_h, p_h, mid_h, xhat_h, n2_h, r2_h, wq_h, wp_h, wu_h, wd_h, e_h, rel_h = take(16)
    g1_ref, g2_ref, qkv_b, up_ref = take(4)
    staged, few_out = take(2)
    outs = take(4)
    outs = outs[:3] + [outs[3].at[pl.ds(k * 192, 192)] if direct else outs[3].at[k] for k in range(3)]
    cot, att, n2, xhat2, hid, dg = take(6)
    acc, dn2 = take(2)
    wu, wd, wp, wq, dwq, qkv, p_buf, e, rel_blk, d_scr, acc_scr = take(11)
    bias_v, pad_acc, sums, r2, real, vec = take(6)
    ls, ss, rs = take(3)
    if direct:
        r1 = take(3)
        rx, ry, rz = take(6), take(6), take(6)
        few_in, = take(1)
        sems = take(9)
        few_s, few_r = take(2)
    me = coords()
    f, ctx, tp = me
    c, own = tp % 2, tp // 2
    pair_at = (1 - own, own)
    tile_at = [2 * pair_at[n // 2] + n % 2 for n in range(4)]
    loads = {}

    def load(name, src, dst):
        loads[name] = pltpu.make_async_copy(src, dst, ls.at[len(loads)])
        loads[name].start()

    def rows_of(t):
        return pl.ds(pl.multiple_of(t * D, 16), D)

    load("n2", n2_h, n2)
    for n, t in enumerate(tile_at):
        load(("wu", n), wu_h.at[rows_of(t)], wu.at[rows_of(t)])
        if n == 0:
            load("cot", c_h, cot)
        load(("wd", n), wd_h.at[rows_of(t)], wd.at[rows_of(t)])
        if n == 0:
            load("acc", mid_h, acc)
    load("xhat", xhat_h, xhat2)
    load("r2", r2_h, r2)
    load("wp", wp_h, wp)
    load("att", att_h, att)
    load("qkv", qkv_h, qkv)
    load("e", e_h, e)
    load("rel", rel_h, rel_blk)
    load("wq", wq_h, wq)
    steps = [(turn, slot) for turn in range(2) for slot in range(NFULL + NPART)]

    def p_copy(n):
        turn, slot = steps[n]
        base, rows = (slot * FULL, FULL) if slot < NFULL else (PBASE + (slot - NFULL) * PART, PART)
        cols = pl.ds(pl.multiple_of(pair_at[turn] * HALF_HEADS * 256, 128), HALF_HEADS * 256)
        return pltpu.make_async_copy(
            p_h.at[pl.ds(base, rows), cols], p_buf.at[n % 2, pl.ds(0, rows)], ls.at[20 + n % 2]
        )

    p_copy(0).start()
    p_copy(1).start()
    group_barrier(((1 - f, ctx, tp),) if direct else ())
    grads = (wu, wd, wp, dwq.at[0], dwq.at[1], dwq.at[2])
    red = Reduce(grads, me, outs, r1, rx, ry, rz, *sems) if direct else None
    sums[...] = jnp.zeros_like(sums)
    pad_acc[...] = jnp.zeros_like(pad_acc)
    vec[0:1, :] = g1_ref[...].astype(F32).reshape(1, D)
    vec[5:6, :] = g2_ref[...].astype(F32).reshape(1, D)
    bias_v[...] = qkv_b[1, :].astype(F32).reshape(1, D)
    up_all = up_ref[...].astype(F32)
    for k in range(4):
        vec[9 + k:10 + k, :] = up_all[k * D:(k + 1) * D].reshape(1, D)
    for slot, base, rows in slots():
        real[pl.ds(base, rows)] = jnp.where(row_real(slot, rows), 1.0, 0.0)

    def row_chunks(body):
        @pl.loop(0, ROWS // CHUNK)
        def _(n):
            body(pl.ds(pl.multiple_of(n * CHUNK, 16), CHUNK))

    for name in ("n2", "cot"):
        loads[name].wait()
    for n in range(4):
        loads["wu", n].wait()
        loads["wd", n].wait()
        pair = pair_at[n // 2]
        t = tile_at[n]
        base = pl.multiple_of(t * D, 16)

        @pl.loop(0, 3)
        def _(j, base=base, t=t):
            units = pl.ds(pl.multiple_of(j * 256, 128), 256)
            gate = jnp.dot(n2[...], wu[pl.ds(base, D), units], preferred_element_type=F32)
            hidden, slope = gelu_both(gate + vec[pl.ds(9 + t, 1), units])
            hid[:, units] = hidden.astype(BF)
            there = pl.ds(pl.multiple_of(base + j * 256, 16), 256)
            d_gate = (nt(cot[...], wd[there, :]) * slope).astype(BF)
            dg[:, units] = d_gate
            sums[pl.ds(8 + t, 1), units] = jnp.sum(d_gate.astype(F32), axis=0, keepdims=True)

        if direct and n:
            @pl.when(c == (n - 1) % 2)
            def _(n=n):
                red.core_add(1, pair_at[(n - 1) // 2])
                red.core_add(0, pair_at[(n - 1) // 2])

        tile = pl.ds(base, D)

        if n == 0:
            loads["acc"].wait()

        def through(here, tile=tile, n=n):
            acc[here] += jnp.dot(hid[here], wd[tile, :], preferred_element_type=F32)
            more = nt(dg[here], wu[tile, :])
            dn2[here] = dn2[here] + more if n else more

        row_chunks(through)

        @pl.loop(0, 3)
        def _(j, base=base):
            part = pl.ds(pl.multiple_of(j * 256, 128), 256)
            there = pl.ds(pl.multiple_of(base + j * 256, 16), 256)
            wd[there, :] = tn(hid[:, part], cot[...]).astype(BF)
            wu[there, :] = tn(n2[:, part], dg[...]).astype(BF)

        if direct:
            @pl.when(c != n % 2)
            def _(pair=pair):
                red.core_send(1, pair)
                red.core_send(0, pair)

    if direct:
        red.x_add(1, pair_at[0])
        red.x_add(0, pair_at[0])

    for name in ("xhat", "r2", "wp", "att"):
        loads[name].wait()
    load_n1 = pltpu.make_async_copy(n1_h, n2, ls.at[22])
    load_n1.start()

    def back_two(here):
        n = dn2[here]
        xhat = xhat2[here].astype(F32)
        c_rows = cot[here].astype(F32)
        m = n * vec[5:6, :]
        sums[5:6, :] += jnp.sum(n * xhat, axis=0, keepdims=True)
        sums[6:7, :] += jnp.sum(n, axis=0, keepdims=True)
        sums[7:8, :] += jnp.sum(c_rows, axis=0, keepdims=True)
        mean = jnp.mean(m, axis=-1, keepdims=True)
        mean_x = jnp.mean(m * xhat, axis=-1, keepdims=True)
        d_mid = c_rows + r2[here] * (m - mean - xhat * mean_x)
        dn2[here] = d_mid
        branch = d_mid.astype(BF)
        xhat2[here] = branch
        sums[4:5, :] += jnp.sum(branch.astype(F32), axis=0, keepdims=True)
        dg[here] = acc[here].astype(BF)
        hid[here] = nt(branch, wp[...]).astype(BF)

    for n in range(ROWS // CHUNK):
        back_two(pl.ds(n * CHUNK, CHUNK))
        if direct and n == 0:
            @pl.when(c == 1)
            def _():
                red.core_add(1, own)
                red.core_add(0, own)
    places = window_places(ctx, tp)

    def tokens_out(a, src_ref):
        for n, (slot, p, rows, exists, image, u, col, d_ctx, d_tp, row) in enumerate(places):
            def go(n=n, rows=rows, image=image, u=u, col=col, d_ctx=d_ctx, d_tp=d_tp, row=row):
                src = src_ref.at[pl.ds(row, rows)]
                dst = staged.at[a, image, u, pl.ds(pl.multiple_of(col * 32, 16), rows)]
                send_or_copy(src, dst, (d_ctx, d_tp), me, ss.at[a, n], rs.at[a, image, u, col])
            if exists is None:
                go()
            else:
                pl.when(exists)(go)

    def tokens_done(a, src_ref):
        for i in range(images):
            for u in range(2):
                for col in range(5):
                    dst = staged.at[a, i, u, pl.ds(col * 32, 32 if col < 4 else 16)]
                    pltpu.make_async_copy(dst, dst, rs.at[a, i, u, col]).wait()
        for n, (slot, p, rows, exists, image, u, col, d_ctx, d_tp, row) in enumerate(places):
            def done(n=n, rows=rows, d_ctx=d_ctx, d_tp=d_tp, row=row):
                wait_sent(src_ref.at[pl.ds(row, rows)], (d_ctx, d_tp), me, ss.at[a, n])
            if exists is None:
                done()
            else:
                pl.when(exists)(done)

    @pl.loop(0, 3)
    def _(j):
        part = pl.ds(pl.multiple_of(j * 256, 128), 256)
        wp[pl.ds(pl.multiple_of(j * 256, 16), 256), :] = tn(att[:, part], xhat2[...]).astype(BF)

    if direct:
        red.core_send(2, 0)
        red.core_send(2, 1)

    load_x = pltpu.make_async_copy(x_h, xhat2, ls.at[23])
    load_x.start()
    for name in ("qkv", "e", "rel"):
        loads[name].wait()
    load_n1.wait()
    acc[pl.ds(0, 512), pl.ds(0, HALF)] = jnp.zeros((512, HALF), F32)
    for n, (turn, slot) in enumerate(steps):
        pair = pair_at[turn]
        p_copy(n).wait()
        base, rows = (slot * FULL, FULL) if slot < NFULL else (PBASE + (slot - NFULL) * PART, PART)
        kind = 0 if slot < NFULL else 1 + slot - NFULL
        narrow = None if slot < NFULL else narrow_flag(slot - NFULL)
        attention_back_half(qkv, hid, rel_blk, bias_v, e.at[kind], p_buf.at[n % 2], d_scr, acc_scr,
                            pad_acc, acc, base, rows, narrow, pair)
        if n + 2 < len(steps):
            p_copy(n + 2).start()
        if slot == NFULL + NPART - 1:
            for w in range(3):
                d_cols = half_cols(w * D, pair)
                dwq[w, half_cols(0, pair), :] = tn(qkv[:, d_cols], n2[...]).astype(BF)
                if direct:
                    red.core_send(3 + w, pair)
        if n == 2:
            tokens_out(0, dg)
        if not direct:
            continue
        if n == 0:
            red.core_add(2, 0)
            red.core_add(2, 1)
        elif n == 5:
            for w in (3, 4, 5):
                red.core_add(w, pair_at[0])
        elif n == 6:
            red.x_add(1, own)
            red.y_add(1)
        elif n == 7:
            red.x_add(0, own)
            red.y_add(0)
        elif n == 8:
            red.z_mid(1, 0)
        elif n == 9:
            red.z_mid(1, 1)
            for w in (3, 4, 5):
                red.core_add(w, own)

    load_x.wait()
    loads["wq"].wait()

    def back_one(here):
        d_qkv = qkv[here, :]
        n = jnp.zeros((CHUNK, D), F32)
        for w in range(3):
            n = n + jnp.dot(d_qkv[:, w * D:(w + 1) * D], wq[w], preferred_element_type=F32)
        sums[2:3, :] += jnp.sum(d_qkv[:, :D].astype(F32), axis=0, keepdims=True)
        sums[3:4, :] += jnp.sum(d_qkv[:, 2 * D:].astype(F32), axis=0, keepdims=True)
        n = n * real[here]
        rows = xhat2[here].astype(F32)
        centered = rows - jnp.mean(rows, axis=-1, keepdims=True)
        r = lax.rsqrt(jnp.mean(centered * centered, axis=-1, keepdims=True) + EPSILON)
        xhat = centered * r
        sums[0:1, :] += jnp.sum(n * xhat, axis=0, keepdims=True)
        sums[1:2, :] += jnp.sum(n, axis=0, keepdims=True)
        m = n * vec[0:1, :]
        mean = jnp.mean(m, axis=-1, keepdims=True)
        mean_x = jnp.mean(m * xhat, axis=-1, keepdims=True)
        cot[here] = (dn2[here] + r * (m - mean - xhat * mean_x)).astype(BF)

    if direct:
        red.x_add(2, 0)
        red.x_add(2, 1)
        red.z_mid(0, 0)
        red.z_out(1, 0)
    back_one(pl.ds(0, CHUNK))
    if direct:
        red.z_mid(0, 1)
        red.z_out(1, 1)
        for w in (3, 4, 5):
            red.x_add(w, pair_at[0])
        red.y_add(2)
    back_one(pl.ds(CHUNK, CHUNK))
    tokens_out(1, cot)

    sums[3:4, :] += pad_acc[...]
    order = (0, 1, 2, 3, 4, 5, 6, 7, 8, 9, 10, 11)
    for n, row in enumerate(order):
        for k in range(6):
            few_out[pl.ds(n * 6 + k, 1), :] = sums[pl.ds(row, 1), pl.ds(k * 128, 128)]
    lane = lax.broadcasted_iota(jnp.int32, (SEG, 128), 1) // HEAD_DIM
    for axis in range(2):
        total = jnp.zeros((SEG, 128), F32)
        for h in range(HALF_HEADS):
            piece = acc[pl.ds((h // 3) * 256 + axis * 128 + (h % 3) * SEG, SEG), pl.ds((h // 2) * 128, 128)]
            total = total + jnp.where(lane == h % 2, piece, 0.0)
        few_out[pl.ds(72 + axis * SEG, SEG), :] = total

    if direct:
        steps = (red.to_s, red.to_x, red.to_y, (f, ctx + 1 - 2 * (ctx % 2), tp), (f, (ctx + 2) % 4, tp))

        def few_copy(n):
            return remote(few_in.at[5 + n], few_in.at[n], steps[n], few_s.at[n], few_r.at[n])

        def few_start(n):
            few_in[5 + n] = few_out[...]
            few_copy(n).start()

        def few_add(n):
            few_copy(n).wait_recv()
            few_out[...] = few_out[...] + few_in[n]

        few_start(0)
        red.z_end(1, 0)
        red.z_out(0, 0)
        red.z_mid(2, 0)
        for w in (3, 4, 5):
            red.x_add(w, own)
        few_add(0)
        few_start(1)
        red.y_add(3)
        red.z_end(1, 1)
        red.z_out(0, 1)
        red.z_end(0, 0)
        red.y_add(4)
        red.z_mid(3, 0)
        red.z_out(2, 0)
        few_add(1)
        few_start(2)
        red.y_add(5)
        red.z_mid(4, 0)
        red.z_out(3, 0)
        red.z_end(0, 1)
        red.z_end(2, 0)
        few_add(2)
        few_start(3)
        red.z_mid(5, 0)
        red.z_out(4, 0)
        red.z_end(3, 0)
        few_add(3)
        few_start(4)
        red.z_out(5, 0)
        red.z_end(4, 0)
        red.z_end(5, 0)
        few_add(4)
        for w in range(6):
            red.sent(w)
        for n in range(5):
            few_copy(n).wait_send()
    else:
        for n, src in enumerate((wu, wd, wp, dwq.at[0], dwq.at[1], dwq.at[2])):
            cp = pltpu.make_async_copy(src, outs[n], ls.at[n])
            cp.start()
            cp.wait()
    tokens_done(0, dg)
    tokens_done(1, cot)


def backward(inputs, small, images, direct):
    any_spec = pl.BlockSpec(memory_space=pl.ANY)
    vmem = pl.BlockSpec(memory_space=pltpu.VMEM)
    dma = pltpu.SemaphoreType.DMA
    shape = jax.ShapeDtypeStruct
    n_places = NFULL * PAIRS + NPART * (4 + PAIRS)
    wholes = ((4 * D, D), (4 * D, D), (D, D), (D, D), (D, D), (D, D))
    out_shape = [shape((2, images, 2, PIECE, D), BF), shape((FEW, 128), F32)]
    out_shape += [shape(s, BF) for s in (HALVES if direct else wholes)[:3]]
    out_shape += [shape((576, 384) if direct else (3, D, D), BF)]
    v = pltpu.VMEM
    scratch = [v((ROWS, D), BF)] * 6 + [v((ROWS, D), F32)] * 2
    scratch += [
        v((4 * D, D), BF), v((4 * D, D), BF), v((D, D), BF), v((3, D, D), BF), v((3, D, D), BF),
        v((ROWS, 3 * D), BF), v((2, FULL, HALF_HEADS * 256), BF), v((1 + NPART, 3, FULL, 256), BF), v((HALF, 512), BF),
        v((FULL, 512), BF), v((FULL, HALF), F32),
        v((1, D), F32), v((1, D), F32), v((SUMS, D), F32), v((ROWS, 1), F32), v((ROWS, 1), F32), v((16, D), F32),
        dma((24,)), dma((2, n_places)), dma((2, images, 2, 5)),
    ]
    if direct:
        scratch += [v((2, D, D), BF), v((2, D, D), BF), v((2, 192, D), BF)]
        scratch += [v((2,) + s, BF) for s in HALVES]
        scratch += [v(s, BF) for s in HALVES]
        scratch += [v((2,) + s, BF) for s in HALVES]
        scratch += [v((10, FEW, 128), F32)]
        scratch += [dma((6, 2)), dma((6, 2)), dma((6, 2)), dma((6, 2)), dma((6,)), dma((6,)), dma((6, 2, 2)), dma((6, 2, 3)), dma((6, 2))]
        scratch += [dma((5,)), dma((5,))]
    return pl.pallas_call(
        functools.partial(backward_kernel, images, direct),
        out_shape=out_shape,
        in_specs=[any_spec] * len(inputs) + [vmem] * len(small),
        out_specs=[any_spec, vmem] + [any_spec] * 4,
        scratch_shapes=scratch,
        compiler_params=pltpu.CompilerParams(
            collective_id=1, has_side_effects=True, vmem_limit_bytes=VMEM_BACK
        ),
        name="backward",
    )(*inputs, *small)


SMALL = (0, 1, 4, 5, 6, 7)


def results_kernel(images, n_grads, staged, few, *refs):
    grads, refs = refs[:n_grads], refs[n_grads:]
    tokens, small, (qv, up, rel_h, rel_w), outs = refs[:2], refs[2:8], refs[8:12], refs[12:]
    unpack = pack_matrix()
    for a in range(2):
        for i in range(images):
            for u in range(2):
                tokens[a][i, pl.ds(u * 128, 128)] = tn(unpack, staged[a, i, u]).astype(BF)
    for row, out in zip(SMALL, small):
        out[...] = few[pl.ds(row * 6, 6), :]
    for n in range(2):
        for k in range(6):
            qv[pl.ds(n, 1), pl.ds(k * 128, 128)] = few[pl.ds((2 + n) * 6 + k, 1), :]
    up[...] = few[pl.ds(48, 24), :]
    for axis, out in enumerate((rel_h, rel_w)):
        table = few[pl.ds(72 + axis * SEG, SEG), :]
        table = table + pltpu.roll(table, HEAD_DIM, 1)
        for j in range(RELS):
            out[pl.ds(j, 1), :] = table[26 - j:27 - j, :HEAD_DIM]
    for src, dst in zip(grads, outs):
        rows = src.shape[0]

        @pl.loop(0, rows // 64)
        def _(k, src=src, dst=dst):
            here = pl.ds(pl.multiple_of(k * 64, 16), 64)
            dst[here] = src[here].astype(F32)


def results(staged, few, grads):
    images = staged.shape[1]
    vmem = pl.BlockSpec(memory_space=pltpu.VMEM)
    shape = jax.ShapeDtypeStruct
    outs = [shape((images, 256, D), BF)] * 2 + [shape((6, 128), F32)] * 6
    outs += [shape((2, D), F32), shape((24, 128), F32), shape((RELS, HEAD_DIM), F32), shape((RELS, HEAD_DIM), F32)]
    outs += [shape(g.shape, F32) for g in grads]
    return pl.pallas_call(
        functools.partial(results_kernel, images, len(grads)),
        out_shape=outs,
        in_specs=[vmem] * (2 + len(grads)),
        out_specs=[vmem] * len(outs),
        compiler_params=pltpu.CompilerParams(vmem_limit_bytes=VMEM_LIMIT),
        name="results",
    )(staged, few, *grads)


def gelu_both(u):
    x = jnp.abs(u) * math.sqrt(0.5)
    t = 1.0 / (1.0 + 0.3275911 * x)
    e = jnp.exp(-0.5 * u * u)
    poly = t * (0.254829592 + t * (-0.284496736 + t * (1.421413741 + t * (-1.453152027 + t * 1.061405429))))
    tail = 0.5 * poly * e
    phi = jnp.where(u >= 0, 1.0 - tail, tail)
    return u * phi, phi + u * e * (1.0 / math.sqrt(2 * math.pi))


def whole_weights(shards):
    wq, wp, wu, wd = shards
    wq = lax.all_gather(lax.all_gather(wq, "fsdp", axis=2, tiled=True), "tp", axis=1, tiled=True)
    wp = lax.all_gather(lax.all_gather(wp, "fsdp", axis=1, tiled=True), "tp", axis=0, tiled=True)
    wu = lax.all_gather(lax.all_gather(wu, "fsdp", axis=0, tiled=True), "tp", axis=1, tiled=True)
    wd = lax.all_gather(lax.all_gather(wd, "fsdp", axis=1, tiled=True), "tp", axis=0, tiled=True)
    return wq, wp, wu, wd


def summed_weights(grads):
    out = []
    for w, grad in enumerate(grads):
        part = lax.psum_scatter(grad, "tp", scatter_dimension=0, tiled=True)
        part = lax.psum_scatter(part, "fsdp", scatter_dimension=0 if w == 0 else 1, tiled=True)
        out.append(lax.psum(part, "ctx").astype(F32))
    return out


def local(direct, block_input, ln1_gain, ln1_bias, w_qkv, qkv_bias, rel_h, rel_w, w_proj, proj_bias,
          ln2_gain, ln2_bias, w_up, up_bias, w_down, down_bias, cotangent):
    images = block_input.shape[1]
    x3 = jnp.transpose(block_input, (1, 0, 2))
    c3 = jnp.transpose(cotangent, (1, 0, 2))
    shards = (jnp.transpose(w_qkv, (0, 2, 1)), w_proj, w_up, w_down)
    front = (ln1_gain, ln1_bias, qkv_bias, ln2_gain, ln2_bias, proj_bias, down_bias, rel_h, rel_w)
    if direct:
        kept = forward(x3, c3, shards, None, front)
    else:
        wq, wp, wu, wd = whole_weights(shards)
        wu = jnp.swapaxes(wu.reshape(D, 4, D), 0, 1).reshape(4 * D, D)
        kept = forward(x3, c3, None, (wq, wp), front)
        kept = [*kept[:10], wq, wp, wu, wd, *kept[10:]]
    staged, few, *grads = backward(kept, (ln1_gain, ln2_gain, qkv_bias, up_bias), images, direct)
    if direct:
        small = results(staged, few, grads)
        ou, od, op, oq = small[12:]
        oq = oq.reshape(3, 192, 384)
    else:
        few = lax.psum(few, ("fsdp", "ctx", "tp"))
        small = results(staged, few, ())
        ou, od, op, oq, ok, ov = summed_weights(grads[:3] + [grads[3][k] for k in range(3)])
        oq = jnp.stack([oq, ok, ov])
    out3, dx3, s_g1, s_b1, s_proj, s_g2, s_b2, s_down, s_qv, s_up, s_relh, s_relw = small[:12]
    return (
        jnp.transpose(out3, (1, 0, 2)), jnp.transpose(dx3, (1, 0, 2)), s_g1.reshape(D), s_b1.reshape(D),
        jnp.transpose(oq, (0, 2, 1)), s_qv, s_relh, s_relw,
        op, s_proj.reshape(D), s_g2.reshape(D), s_b2.reshape(D), ou, s_up.reshape(4 * D), od, s_down.reshape(D),
    )


def solution(mesh):
    direct = mesh.shape["fsdp"] == 2
    rows = P(("ctx", "tp"), "fsdp", None)
    w_specs = (P(None, "fsdp", "tp"), P("tp", "fsdp"), P("fsdp", "tp"), P("tp", "fsdp"))
    return jax.shard_map(
        functools.partial(local, direct),
        mesh=mesh,
        in_specs=(rows, P(), P(), w_specs[0], P(), P(), P(), w_specs[1], P(), P(), P(), w_specs[2], P(), w_specs[3], P(), rows),
        out_specs=(rows, rows, P(), P(), w_specs[0], P(), P(), P(), w_specs[1], P(), P(), P(), w_specs[2], P(), w_specs[3], P()),
        check_vma=False,
    )
```

time: 317 us -> 270 us (0.85)
  the two profiles are of different devices: /device:TPU:0 before, /device:TPU:9 now
where the time goes in v4:
time: 270 us; the launch traced here: 267 us
  Pallas kernels  266 us (99%)
    pallas_call x1, Pallas kernels, backward(): pl.pallas_call(functools.partial(backward_kernel, images, direct), out_sh...  174 us
    pallas_call x1, Pallas kernels, forward(): pl.pallas_call(functools.partial(forward_kernel, images, direct), out_sha...  85.7 us
    pallas_call x1, Pallas kernels, results(): pl.pallas_call(functools.partial(results_kernel, images, len(grads)), out...  6.05 us

profile of v4, /device:TPU:9, one launch (start us, length us, event | category | flops | bytes accessed | tf_op | source)
XLA Modules:
  0.0 266.9 jit_solution(18356534468486924558)
XLA Ops:
  0.7 85.7 %forward.1 = (bf16[928,768]{1,0:T(8,128)(2,1)}, bf16[928,768]{1,0:T(8,128)(2,1)}, bf16[928,768]{1,0:T(8,128)(2,1)}, bf16[928,2304]{1,0:T(8,128)(2,1)}, bf16[928,...) custom-call(bf16[3,256,768]{2,1,0:T(8,128)(2,1)} %bitcast.15, ...), custom_call_target="tpu_custom_call" | custom-call | tf_op jit(solution)/shard_map/forward/pallas_call | solution.py:589
  86.4 174.3 %backward.1 = (bf16[2,3,2,144,768]{4,3,2,1,0:T(8,128)(2,1)}, f32[136,128]{1,0:T(8,128)}, bf16[384,768]{1,0:T(8,128)(2,1)}, bf16[768,384]{1,0:T(8,128)(2,1)}, bf1...) custom-call(bf16[928,768]{1,0:T(8,128)(2,1)} %get-tuple-element.54.refs_0_, bf16[928,768]{1,0:T(8,128)(2,1)} %get-tuple-element.55.refs_1_, ...), custom_call_target="tpu_custom_call" | custom-call | tf_op jit(solution)/shard_map/backward/pallas_call | solution.py:1264
  260.7 6.0 %results.1 = (bf16[3,256,768]{2,1,0:T(8,128)(2,1)}, bf16[3,256,768]{2,1,0:T(8,128)(2,1)}, f32[6,128]{1,0:T(8,128)}, f32[6,128]{1,0:T(8,128)}, f32[6,128]{1,0:T(8...) custom-call(bf16[2,3,2,144,768]{4,3,2,1,0:T(8,128)(2,1)} %get-tuple-, ...), custom_call_target="tpu_custom_call" | custom-call | tf_op jit(solution)/shard_map/results/pallas_call | solution.py:1315

commit v5 on v4

--- a/solution.py
+++ b/solution.py
@@ -441,6 +441,8 @@
     if direct:
         for w in range(3):
             gather.on(w, 0, (4,))
+        for w in (4, 5, 3):
+            gather.start_own(w, (0, 2))
     wait_pieces(xw, 0, me, rs)
     if direct:
         for w in range(3):
@@ -457,7 +459,6 @@
     if direct:
         for w in range(3):
             gather.arrived(w, (2, 4))
-        gather.start_own(4)
     else:
         for cp in load:
             cp.wait()
@@ -481,30 +482,23 @@
                 def _():
                     for w in range(3):
                         gather.on(w, 1, (3, 5))
-                    gather.start_own(3)
-                    gather.start_own(5)
-
-                @pl.when(n == 1)
-                def _():
-                    gather.forward_x(4)
-                    start_pieces(stage, cw, 1, images, me, ss, rs)
+                    for w in (3, 4, 5):
+                        gather.start_own(w, (1,))
+                    for w in (4, 5, 3):
+                        gather.forward_x(w)
 
                 @pl.when(n == 2)
                 def _():
-                    gather.forward_y(4)
-                    for w in range(3):
-                        gather.on(w, 3, (6,))
+                    pass
             else:
                 @pl.when(n == 0)
                 def _():
-                    gather.forward_x(3)
                     gather.forward_y(3)
-                    gather.forward_x(5)
+                    start_pieces(stage, cw, 1, images, me, ss, rs)
 
                 @pl.when(n == 1)
                 def _():
                     gather.forward_y(5)
-                    gather.forward_second(4)
 
                 @pl.when(n == 2)
                 def _():
@@ -518,11 +512,13 @@
         if direct:
             if turn == 0:
                 for w in range(3):
+                    gather.on(w, 3, (6,))
+                gather.forward_y(4)
+                for w in range(3):
                     gather.arrived(w, (5, 6))
                 write(wq, wq_o)
             else:
-                gather.forward_second(5)
-                gather.forward_z(4)
+                gather.forward_second(4)
 
     write(qkv, qkv_o)
     write(att, att_o)
@@ -544,6 +540,8 @@
     for src, dst in ((n2, n2_o), (mid, mid_o), (xhat2, xhat_o), (r2, r2_o)):
         write(src, dst)
     if direct:
+        gather.forward_second(5)
+        gather.forward_z(4)
         gather.forward_z(5)
     wait_pieces(cw, 1, me, rs)
     for slot, base, rows in slots():
@@ -781,15 +779,26 @@
         self.core_copy(w, j).start()
 
     def x_copy(self, w, j):
+        if w == 0:
+            src = self.half(0, self.c + 2 * self.own, self.g)
+            return remote(src, self.rx[0].at[0], self.to_x, self.s2.at[0, 0], self.v2.at[0, 0])
         src = self.half(w, self.c + 2 * j, self.g)
         return remote(src, self.rx[w].at[j], self.to_x, self.s2.at[w, j], self.v2.at[w, j])
 
     def core_add(self, w, j):
         self.core_copy(w, j).wait_recv()
         add_rows(self.tile(w, self.c + 2 * j), self.landing(w, j))
-        self.x_copy(w, j).start()
+        if w == 0:
+            @pl.when(self.own != j)
+            def _():
+                self.y_copy(0).start()
+        else:
+            self.x_copy(w, j).start()
 
     def y_copy(self, w):
+        if w == 0:
+            src = self.tile(0, self.c + 2 * (1 - self.own))
+            return remote(src, self.ry[0], self.to_y, self.s3.at[0], self.v3.at[0])
         src = self.half(w, self.c + 2 * (1 - self.own), self.f)
         return remote(src, self.ry[w], self.to_y, self.s3.at[w], self.v3.at[w])
 
@@ -800,6 +809,17 @@
         @pl.when(self.own != j)
         def _():
             self.y_copy(w).start()
+
+    def up_y_add(self):
+        self.y_copy(0).wait_recv()
+        add_rows(self.tile(0, self.c + 2 * self.own), self.ry[0])
+        self.x_copy(0, 0).start()
+
+    def up_x_add(self):
+        self.x_copy(0, 0).wait_recv()
+        add_rows(self.mine(0), self.rx[0].at[0])
+        for h in range(Z_PIECES[0]):
+            self.z_in(0, h)
 
     def mine(self, w):
         return self.half(w, self.c + 2 * self.own, self.f)
@@ -863,7 +883,8 @@
     def sent(self, w):
         for j in range(2):
             self.core_copy(w, j).wait_send()
-            self.x_copy(w, j).wait_send()
+            if w or j == 0:
+                self.x_copy(w, j).wait_send()
         self.y_copy(w).wait_send()
         for h in range(Z_PIECES[w]):
             self.z_wait(w, h, self.sz.at[w, h, 0])
@@ -967,16 +988,18 @@
         t = tile_at[n]
         base = pl.multiple_of(t * D, 16)
 
-        @pl.loop(0, 3)
-        def _(j, base=base, t=t):
-            units = pl.ds(pl.multiple_of(j * 256, 128), 256)
-            gate = jnp.dot(n2[...], wu[pl.ds(base, D), units], preferred_element_type=F32)
-            hidden, slope = gelu_both(gate + vec[pl.ds(9 + t, 1), units])
-            hid[:, units] = hidden.astype(BF)
+        for j in range(3):
+            units = pl.ds(j * 256, 256)
             there = pl.ds(pl.multiple_of(base + j * 256, 16), 256)
-            d_gate = (nt(cot[...], wd[there, :]) * slope).astype(BF)
-            dg[:, units] = d_gate
-            sums[pl.ds(8 + t, 1), units] = jnp.sum(d_gate.astype(F32), axis=0, keepdims=True)
+            for r in range(ROWS // CHUNK):
+                here = pl.ds(r * CHUNK, CHUNK)
+                d_hidden = nt(cot[here, :], wd[there, :])
+                gate = jnp.dot(n2[here, :], wu[pl.ds(base, D), units], preferred_element_type=F32)
+                hidden, slope = gelu_both(gate + vec[pl.ds(9 + t, 1), units])
+                hid[here, units] = hidden.astype(BF)
+                d_gate = (d_hidden * slope).astype(BF)
+                dg[here, units] = d_gate
+                sums[pl.ds(8 + t, 1), units] += jnp.sum(d_gate.astype(F32), axis=0, keepdims=True)
 
         if direct and n:
             @pl.when(c == (n - 1) % 2)
@@ -989,16 +1012,13 @@
         if n == 0:
             loads["acc"].wait()
 
-        def through(here, tile=tile, n=n):
+        for r in range(ROWS // CHUNK):
+            here = pl.ds(r * CHUNK, CHUNK)
             acc[here] += jnp.dot(hid[here], wd[tile, :], preferred_element_type=F32)
             more = nt(dg[here], wu[tile, :])
             dn2[here] = dn2[here] + more if n else more
-
-        row_chunks(through)
-
-        @pl.loop(0, 3)
-        def _(j, base=base):
-            part = pl.ds(pl.multiple_of(j * 256, 128), 256)
+        for j in range(3):
+            part = pl.ds(j * 256, 256)
             there = pl.ds(pl.multiple_of(base + j * 256, 16), 256)
             wd[there, :] = tn(hid[:, part], cot[...]).astype(BF)
             wu[there, :] = tn(n2[:, part], dg[...]).astype(BF)
@@ -1008,10 +1028,6 @@
             def _(pair=pair):
                 red.core_send(1, pair)
                 red.core_send(0, pair)
-
-    if direct:
-        red.x_add(1, pair_at[0])
-        red.x_add(0, pair_at[0])
 
     for name in ("xhat", "r2", "wp", "att"):
         loads[name].wait()
@@ -1043,10 +1059,16 @@
             def _():
                 red.core_add(1, own)
                 red.core_add(0, own)
+
+            red.x_add(1, pair_at[0])
+            red.up_y_add()
     places = window_places(ctx, tp)
 
-    def tokens_out(a, src_ref):
+    def tokens_out(a, src_ref, which=range(NFULL + NPART)):
         for n, (slot, p, rows, exists, image, u, col, d_ctx, d_tp, row) in enumerate(places):
+            if slot not in which:
+                continue
+
             def go(n=n, rows=rows, image=image, u=u, col=col, d_ctx=d_ctx, d_tp=d_tp, row=row):
                 src = src_ref.at[pl.ds(row, rows)]
                 dst = staged.at[a, image, u, pl.ds(pl.multiple_of(col * 32, 16), rows)]
@@ -1101,28 +1123,32 @@
                 dwq[w, half_cols(0, pair), :] = tn(qkv[:, d_cols], n2[...]).astype(BF)
                 if direct:
                     red.core_send(3 + w, pair)
-        if n == 2:
+        if n == 4:
             tokens_out(0, dg)
         if not direct:
             continue
         if n == 0:
             red.core_add(2, 0)
             red.core_add(2, 1)
+        elif n == 2:
+            red.x_add(1, own)
+        elif n == 3:
+            red.y_add(1)
+        elif n == 4:
+            red.up_x_add()
         elif n == 5:
             for w in (3, 4, 5):
                 red.core_add(w, pair_at[0])
-        elif n == 6:
-            red.x_add(1, own)
-            red.y_add(1)
         elif n == 7:
-            red.x_add(0, own)
-            red.y_add(0)
+            red.z_mid(1, 0)
         elif n == 8:
-            red.z_mid(1, 0)
+            red.z_mid(1, 1)
+            red.x_add(2, 0)
+            red.x_add(2, 1)
         elif n == 9:
-            red.z_mid(1, 1)
             for w in (3, 4, 5):
                 red.core_add(w, own)
+            red.z_out(1, 0)
 
     load_x.wait()
     loads["wq"].wait()
@@ -1147,19 +1173,17 @@
         cot[here] = (dn2[here] + r * (m - mean - xhat * mean_x)).astype(BF)
 
     if direct:
-        red.x_add(2, 0)
-        red.x_add(2, 1)
         red.z_mid(0, 0)
-        red.z_out(1, 0)
-    back_one(pl.ds(0, CHUNK))
-    if direct:
-        red.z_mid(0, 1)
-        red.z_out(1, 1)
         for w in (3, 4, 5):
             red.x_add(w, pair_at[0])
         red.y_add(2)
+    back_one(pl.ds(0, CHUNK))
+    tokens_out(1, cot, (0, 1))
+    if direct:
+        red.z_out(1, 1)
+        red.z_mid(0, 1)
     back_one(pl.ds(CHUNK, CHUNK))
-    tokens_out(1, cot)
+    tokens_out(1, cot, (2, 3, 4))
 
     sums[3:4, :] += pad_acc[...]
     order = (0, 1, 2, 3, 4, 5, 6, 7, 8, 9, 10, 11)
@@ -1194,21 +1218,21 @@
         red.z_mid(2, 0)
         for w in (3, 4, 5):
             red.x_add(w, own)
+        red.z_end(1, 1)
+        red.z_out(0, 1)
         few_add(0)
         few_start(1)
         red.y_add(3)
-        red.z_end(1, 1)
-        red.z_out(0, 1)
+        red.z_out(2, 0)
         red.z_end(0, 0)
         red.y_add(4)
         red.z_mid(3, 0)
-        red.z_out(2, 0)
+        red.y_add(5)
         few_add(1)
         few_start(2)
-        red.y_add(5)
+        red.z_end(0, 1)
         red.z_mid(4, 0)
         red.z_out(3, 0)
-        red.z_end(0, 1)
         red.z_end(2, 0)
         few_add(2)
         few_start(3)
@@ -1255,8 +1279,8 @@
     ]
     if direct:
         scratch += [v((2, D, D), BF), v((2, D, D), BF), v((2, 192, D), BF)]
-        scratch += [v((2,) + s, BF) for s in HALVES]
-        scratch += [v(s, BF) for s in HALVES]
+        scratch += [v((2 if w else 1,) + s, BF) for w, s in enumerate(HALVES)]
+        scratch += [v(s if w else (D, D), BF) for w, s in enumerate(HALVES)]
         scratch += [v((2,) + s, BF) for s in HALVES]
         scratch += [v((10, FEW, 128), F32)]
         scratch += [dma((6, 2)), dma((6, 2)), dma((6, 2)), dma((6, 2)), dma((6,)), dma((6,)), dma((6, 2, 2)), dma((6, 2, 3)), dma((6, 2))]

time: 270 us -> 253 us (0.937)
  the two profiles are of different devices: /device:TPU:9 before, /device:TPU:25 now
where the time goes in v5:
time: 253 us; the launch traced here: 250 us
  Pallas kernels  249 us (98%)
    pallas_call x1, Pallas kernels, backward(): pl.pallas_call(functools.partial(backward_kernel, images, direct), out_sh...  160 us
    pallas_call x1, Pallas kernels, forward(): pl.pallas_call(functools.partial(forward_kernel, images, direct), out_sha...  83.2 us
    pallas_call x1, Pallas kernels, results(): pl.pallas_call(functools.partial(results_kernel, images, len(grads)), out...  6.05 us

profile of v5, /device:TPU:25, one launch (start us, length us, event | category | flops | bytes accessed | tf_op | source)
XLA Modules:
  0.0 249.8 jit_solution(2071886617327361112)
XLA Ops:
  0.7 83.2 %forward.1 = (bf16[928,768]{1,0:T(8,128)(2,1)}, bf16[928,768]{1,0:T(8,128)(2,1)}, bf16[928,768]{1,0:T(8,128)(2,1)}, bf16[928,2304]{1,0:T(8,128)(2,1)}, bf16[928,...) custom-call(bf16[3,256,768]{2,1,0:T(8,128)(2,1)} %bitcast.15, ...), custom_call_target="tpu_custom_call" | custom-call | tf_op jit(solution)/shard_map/forward/pallas_call | solution.py:587
  83.9 159.7 %backward.1 = (bf16[2,3,2,144,768]{4,3,2,1,0:T(8,128)(2,1)}, f32[136,128]{1,0:T(8,128)}, bf16[384,768]{1,0:T(8,128)(2,1)}, bf16[768,384]{1,0:T(8,128)(2,1)}, bf1...) custom-call(bf16[928,768]{1,0:T(8,128)(2,1)} %get-tuple-element.54.refs_0_, bf16[928,768]{1,0:T(8,128)(2,1)} %get-tuple-element.55.refs_1_, ...), custom_call_target="tpu_custom_call" | custom-call | tf_op jit(solution)/shard_map/backward/pallas_call | solution.py:1288
  243.5 6.1 %results.1 = (bf16[3,256,768]{2,1,0:T(8,128)(2,1)}, bf16[3,256,768]{2,1,0:T(8,128)(2,1)}, f32[6,128]{1,0:T(8,128)}, f32[6,128]{1,0:T(8,128)}, f32[6,128]{1,0:T(8...) custom-call(bf16[2,3,2,144,768]{4,3,2,1,0:T(8,128)(2,1)} %get-tuple-, ...), custom_call_target="tpu_custom_call" | custom-call | tf_op jit(solution)/shard_map/results/pallas_call | solution.py:1339
